TPU v7x, 128 devices: a whole 4x4x4 slice. The times are simulated.
128 devices in a mesh: scen: 8 (over x, core), var: 16 (over z, y).
Axes of the slice: x: 4, y: 4, z: 4, core: 2. Of those that a mesh axis runs over, the one named last changes fastest.
Arguments:
- start_point: float32 [1024, 65536], P('scen', 'var'), may hold values from -1 to 1
- multipliers: float32 [1024, 65536], P('scen', 'var'), may hold values from -3 to 3
- cost: bfloat16 [1024, 65536], P('scen', 'var'), may hold values from -6 to 6
- curvature: bfloat16 [1024, 65536], P('scen', 'var'), may hold values from 0.5 to 2
- recourse_rhs: float32 [1024, 512], P('scen'), may hold values from -12 to 12
- technology: bfloat16 [512, 65536], P(None, 'var'), may hold values from -0.0234375 to 0.0234375
- scenario_weight: float32 [1024], P('scen'), may hold values from 1 to 30
- previous_mean: float32 [4, 65536], P(None, 'var'), may hold values from -1 to 1
- active: int32 [1024, 512], P('scen', 'var'), may hold values 0 or 1
Outputs:
- iterate: float32 [1024, 65536], P('scen', 'var')
- new_multipliers: float32 [1024, 65536], P('scen', 'var')
- bundle_mean: float32 [4, 65536], P(None, 'var')
- primal_norm: float32 [], replicated
- dual_norm: float32 [], replicated
All inputs are finite; a program needn't handle non-finite values. No bound on the sum of `active` on one device may be relied on, other than what follows from the above.
Results may differ from a plain program's by a relative error of at most 0.0007.
Values sent between devices are 32-bit elements; how exact they have to be, the bound alone decides.
No kernel may reach another device: no remote copies, remote signals or barrier semaphores. Data moves between devices by JAX's collectives and lax.ppermute only.
A program may use at most 64 MiB of HBM per device.

v0:
```python
import jax
import jax.numpy as jnp
from jax import lax
from jax.sharding import Mesh
from jax.sharding import PartitionSpec as P

V = 65536
BLK = 128
STEPS = 8
SCEN = ("scen_0", "scen_1")
VAR = ("var_0", "var_1")
SCEN_VAR = ("scen_0", "scen_1", "var_0", "var_1")


highest = lax.Precision.HIGHEST
penalty = 1.0
recourse_scale = 4.0
stride = 0.2
epsilon = 1e-06


def copy_for_each(x, axis):
    devices = lax.axis_size(axis)
    return lax.all_to_all(jnp.broadcast_to(x[None], (devices, *x.shape)), axis, 0, 0, tiled=True)


def of_everyone(x, axis):
    everything = copy_for_each(x, axis)
    return jnp.sum(everything, axis=0)


def padded_to(lines, devices):
    spare = -lines.shape[0] % devices
    if not spare:
        return lines
    return jnp.concatenate([lines, jnp.zeros((spare, *lines.shape[1:]), lines.dtype)])


def laid_out(pieces, dim):
    pieces = jnp.moveaxis(pieces, 0, dim)
    dims = pieces.shape
    return pieces.reshape(*dims[:dim], dims[dim] * dims[dim + 1], *dims[dim + 2 :])


def collect(x, axis, dim):
    pieces = copy_for_each(x, axis)
    return laid_out(pieces, dim)


def cut_along(x, dim, devices):
    before, after = (x.shape[:dim], x.shape[dim + 1 :])
    return jnp.moveaxis(x.reshape(*before, devices, -1, *after), dim, 0)


def sum_at_owner(x, axis, dim):
    pieces = cut_along(x, dim, lax.axis_size(axis))
    arrived = lax.all_to_all(pieces, axis, split_axis=0, concat_axis=0, tiled=True)
    return arrived.sum(axis=0)


def total_of(x, axes):
    lines = x.reshape(-1, x.shape[-1])
    padded = padded_to(lines, lax.axis_size(axes))
    whole = collect(sum_at_owner(padded, axes, 0), axes, 0)
    return lax.slice_in_dim(whole, 0, len(lines)).reshape(x.shape)


def from_partner(block, axis, bit):
    count = lax.axis_size(axis)
    route = []
    for low in range(count):
        high = low | 1 << bit
        if high != low and high < count:
            route += [(low, high), (high, low)]
    return lax.ppermute(block, axis, route)


def by_axis(x, axes):
    for axis in axes:
        x = lax.psum(x, axis)
    return x


def shards(
    start_point,
    multipliers,
    cost,
    curvature,
    recourse_rhs,
    technology,
    scenario_weight,
    previous_mean,
    active,
):
    scen_rows, var_cols = start_point.shape
    groups = previous_mean.shape[0]
    group_size = lax.axis_size(SCEN) // groups
    position = lax.axis_index(SCEN)
    my_node = position // group_size
    node_of = jnp.full((scen_rows,), my_node, jnp.int32)
    member = (node_of[:, None] == jnp.arange(groups, dtype=jnp.int32)[None, :]).astype(jnp.float32)
    bundle_mass = of_everyone(jnp.sum(member * scenario_weight[:, None], axis=0), SCEN)
    anchor = jnp.dot(member, previous_mean, precision=highest, preferred_element_type=jnp.float32)
    linear = cost.astype(jnp.float32) + multipliers - penalty * anchor
    diagonal = curvature.astype(jnp.float32) + penalty
    active_mask = (active > 0)[:, :, None]
    iterate = start_point
    for sweep in range(STEPS):
        rounded = iterate.astype(jnp.bfloat16)
        partial_image = lax.dot_general(
            rounded, technology, (((1,), (1,)), ((), ())), preferred_element_type=jnp.float32
        )
        image = total_of(partial_image, VAR)
        shortfall = (image - recourse_rhs).astype(jnp.bfloat16)
        pullback = jnp.dot(shortfall, technology, preferred_element_type=jnp.float32)
        stepped = jnp.clip(
            iterate - stride * (diagonal * iterate + linear + recourse_scale * pullback), -1.0, 1.0
        )
        blocked = jnp.where(
            active_mask, stepped.reshape(scen_rows, -1, BLK), iterate.reshape(scen_rows, -1, BLK)
        )
        iterate = blocked.reshape(scen_rows, var_cols)
    weighted = scenario_weight[:, None] * iterate
    normaliser = jnp.sum(bundle_mass) * V
    own_total = jnp.sum(weighted, axis=0, keepdims=True)
    own_total = own_total + from_partner(own_total, SCEN, 0)
    own_mass = jnp.sum(
        bundle_mass * (jnp.arange(groups, dtype=jnp.int32) == my_node).astype(jnp.float32)
    )
    mean_row = own_total / own_mass
    old_row = lax.dynamic_slice_in_dim(previous_mean, my_node, 1, 0)
    leader = (position % group_size == 0).astype(jnp.float32)
    centred = iterate - mean_row
    drift_part = leader * own_mass * jnp.sum((mean_row - old_row) ** 2)
    spread_part = jnp.sum(scenario_weight[:, None] * centred * centred)
    drift_sum, spread = (by_axis(drift_part, SCEN_VAR), by_axis(spread_part, SCEN_VAR))
    collected = collect(mean_row, SCEN, 0)
    bundle_mean = collected.reshape(groups, group_size, var_cols)[:, 0, :]
    primal_norm = jnp.sqrt(spread / normaliser + epsilon)
    dual_norm = penalty * jnp.sqrt(drift_sum / normaliser + epsilon)
    factor = penalty * jnp.sqrt(primal_norm / dual_norm)
    new_multipliers = multipliers + factor * centred
    return (iterate, new_multipliers, bundle_mean, primal_norm, dual_norm)


def solution(mesh):
    torus = Mesh(mesh.devices.reshape(4, 2, 4, 4), ("scen_0", "scen_1", "var_0", "var_1"))
    return jax.shard_map(
        shards,
        mesh=torus,
        in_specs=(
            P(SCEN, VAR),
            P(SCEN, VAR),
            P(SCEN, VAR),
            P(SCEN, VAR),
            P(SCEN, None),
            P(None, VAR),
            P(SCEN),
            P(None, VAR),
            P(SCEN, VAR),
        ),
        out_specs=(P(SCEN, VAR), P(SCEN, VAR), P(None, VAR), P(), P()),
        check_vma=False,
    )
```

profile of v0, /device:TPU:0, one launch (start us, length us, event | category | flops | bytes accessed | tf_op | source)
XLA Modules:
  0.0 346.7 jit_solution(13121193242066260157)
XLA Ops:
  0.7 5.1 %convolution_bitcast_fusion = f32[16,8,512]{2,1,0:T(8,128)} fusion(bf16[512,4096]{1,0:T(8,128)(2,1)} %param.14, f32[128,4096]{1,0:T(8,128)} %param.9), kind=kOutput, calls=%fused_computation.68 | convolution fusion | flops 537395200 | bytes 6553600 | tf_op jit(solution)/shard_map/dot_general | solution.py:110
  5.7 8.1 %all-to-all-start = ((f32[16,8,512]{2,1,0:T(8,128)}), f32[16,8,512]{2,1,0:T(8,128)S(1)}, u32[]{:S(2)}, u32[]{:S(2)}) async-start(f32[16,8,512]{2,1,0:T(8,128)} %convolution_bitcast_fusion), calls=%async_computation | async-start | bytes 524288 | tf_op jit(solution)/shard_map/all_to_all | solution.py:57
  14.1 8.5 %all-to-all-done = f32[16,8,512]{2,1,0:T(8,128)S(1)} async-done(((f32[16,8,512]{2,1,0:T(8,128)}), f32[16,8,512]{2,1,0:T(8,128)S(1)}, u32[]{:S(2)}, u32[]{:S(2)}) %all-to-all-start) | async-done | bytes 262176 | tf_op jit(solution)/shard_map/all_to_all | solution.py:57
  22.6 0.7 broadcast_in_dim.101
  23.3 4.2 %all-to-all-start.1 = ((f32[16,8,512]{2,1,0:T(8,128)}), f32[16,8,512]{2,1,0:T(8,128)}, u32[]{:S(2)}, u32[]{:S(2)}) async-start(f32[16,8,512]{2,1,0:T(8,128)} %broadcast_in_dim.101), calls=%async_computation.1 | async-start | bytes 524288 | tf_op jit(solution)/shard_map/all_to_all | solution.py:24
  27.6 3.0 convolution_subtract_fusion
  30.6 5.7 %all-to-all-done.1 = f32[16,8,512]{2,1,0:T(8,128)} async-done(((f32[16,8,512]{2,1,0:T(8,128)}), f32[16,8,512]{2,1,0:T(8,128)}, u32[]{:S(2)}, u32[]{:S(2)}) %all-to-all-start.1) | async-done | bytes 262176 | tf_op jit(solution)/shard_map/all_to_all | solution.py:24
  36.2 1.0 broadcast_in_dim.99
  37.3 0.8 copy-done.1
  38.0 4.5 %fusion.39 = f32[128,4096]{1,0:T(8,128)S(1)} fusion(f32[128,4096]{1,0:T(8,128)} %param.9, bf16[512,4096]{1,0:T(8,128)(2,1)} %param.14, f32[128,4096]{1,0:T(8,128)S(1)} %convolution_subtract_fusion, bf16[128,4096]{1,0:T(8,128)(2,1)S(1)} %copy-done, f32[128,512]{1,0:T(8,128)S(1)} %copy-done.10, f32[16,8,512]{2,1,0:T(8,128)} %all-to-all-done.1, ...), kind=kOutput, calls=%fused_computation.47 | convolution fusion | flops 542244864 | bytes 12582912 | tf_op jit(solution)/shard_map/dot_general | solution.py:115
  42.6 4.4 %fusion.52 = f32[16,8,512]{2,1,0:T(8,128)S(1)} fusion(bf16[512,4096]{1,0:T(8,128)(2,1)} %param.14, f32[128,4096]{1,0:T(8,128)S(1)} %fusion.39), kind=kOutput, calls=%fused_computation.61 | convolution fusion | flops 537395200 | bytes 6553600 | tf_op jit(solution)/shard_map/dot_general | solution.py:110
  47.0 12.0 %all_to_all.91 = f32[16,8,512]{2,1,0:T(8,128)} all-to-all(f32[16,8,512]{2,1,0:T(8,128)S(1)} %fusion.52), channel_id=1, replica_groups=mesh['scen_0'=4,'scen_1'=2,'var_0'=4,'var_1'=4] {'var_0','var_1'}, dimensions={0} | all-to-all | bytes 524288 | tf_op jit(solution)/shard_map/all_to_all | solution.py:57
  59.0 1.0 reduce_sum.136
  60.0 11.6 %all_to_all.92 = f32[16,8,512]{2,1,0:T(8,128)S(1)} all-to-all(f32[16,8,512]{2,1,0:T(8,128)S(1)} %broadcast_in_dim.102), channel_id=1, replica_groups=mesh['scen_0'=4,'scen_1'=2,'var_0'=4,'var_1'=4] {'var_0','var_1'}, dimensions={0} | all-to-all | bytes 524288 | tf_op jit(solution)/shard_map/all_to_all | solution.py:24
  71.6 4.5 %fusion.34 = f32[128,4096]{1,0:T(8,128)S(1)} fusion(f32[128,4096]{1,0:T(8,128)} %copy-done.9, bf16[512,4096]{1,0:T(8,128)(2,1)} %param.14, f32[128,4096]{1,0:T(8,128)S(1)} %convolution_subtract_fusion, bf16[128,4096]{1,0:T(8,128)(2,1)S(1)} %copy-done, f32[128,512]{1,0:T(8,128)} %param.13, f32[16,8,512]{2,1,0:T(8,128)S(1)} %all_to_all.92, ...), kind=kOutput, calls=%fused_computation.41 | convolution fusion | flops 542244864 | bytes 12582912 | tf_op jit(solution)/shard_map/dot_general | solution.py:115
  76.1 4.4 %fusion.50 = f32[16,8,512]{2,1,0:T(8,128)S(1)} fusion(bf16[512,4096]{1,0:T(8,128)(2,1)} %param.14, f32[128,4096]{1,0:T(8,128)S(1)} %fusion.34), kind=kOutput, calls=%fused_computation.59 | convolution fusion | flops 537395200 | bytes 6553600 | tf_op jit(solution)/shard_map/dot_general | solution.py:110
  80.6 12.0 %all_to_all.93 = f32[16,8,512]{2,1,0:T(8,128)} all-to-all(f32[16,8,512]{2,1,0:T(8,128)S(1)} %fusion.50), channel_id=1, replica_groups=mesh['scen_0'=4,'scen_1'=2,'var_0'=4,'var_1'=4] {'var_0','var_1'}, dimensions={0} | all-to-all | bytes 524288 | tf_op jit(solution)/shard_map/all_to_all | solution.py:57
  92.5 1.0 reduce_sum.137
  93.5 11.6 %all_to_all.94 = f32[16,8,512]{2,1,0:T(8,128)S(1)} all-to-all(f32[16,8,512]{2,1,0:T(8,128)S(1)} %broadcast_in_dim.103), channel_id=1, replica_groups=mesh['scen_0'=4,'scen_1'=2,'var_0'=4,'var_1'=4] {'var_0','var_1'}, dimensions={0} | all-to-all | bytes 524288 | tf_op jit(solution)/shard_map/all_to_all | solution.py:24
  105.1 4.5 %fusion.29 = f32[128,4096]{1,0:T(8,128)S(1)} fusion(f32[128,4096]{1,0:T(8,128)} %copy-done.4, bf16[512,4096]{1,0:T(8,128)(2,1)} %param.14, f32[128,4096]{1,0:T(8,128)S(1)} %convolution_subtract_fusion, bf16[128,4096]{1,0:T(8,128)(2,1)S(1)} %copy-done, f32[128,512]{1,0:T(8,128)} %param.13, f32[16,8,512]{2,1,0:T(8,128)S(1)} %all_to_all.94, ...), kind=kOutput, calls=%fused_computation.35 | convolution fusion | flops 542244864 | bytes 12582912 | tf_op jit(solution)/shard_map/dot_general | solution.py:115
  109.7 4.4 %fusion.48 = f32[16,8,512]{2,1,0:T(8,128)S(1)} fusion(bf16[512,4096]{1,0:T(8,128)(2,1)} %param.14, f32[128,4096]{1,0:T(8,128)S(1)} %fusion.29), kind=kOutput, calls=%fused_computation.57 | convolution fusion | flops 537395200 | bytes 6553600 | tf_op jit(solution)/shard_map/dot_general | solution.py:110
  114.1 12.0 %all_to_all.95 = f32[16,8,512]{2,1,0:T(8,128)} all-to-all(f32[16,8,512]{2,1,0:T(8,128)S(1)} %fusion.48), channel_id=1, replica_groups=mesh['scen_0'=4,'scen_1'=2,'var_0'=4,'var_1'=4] {'var_0','var_1'}, dimensions={0} | all-to-all | bytes 524288 | tf_op jit(solution)/shard_map/all_to_all | solution.py:57
  126.1 1.0 reduce_sum.138
  127.1 11.6 %all_to_all.96 = f32[16,8,512]{2,1,0:T(8,128)S(1)} all-to-all(f32[16,8,512]{2,1,0:T(8,128)S(1)} %broadcast_in_dim.104), channel_id=1, replica_groups=mesh['scen_0'=4,'scen_1'=2,'var_0'=4,'var_1'=4] {'var_0','var_1'}, dimensions={0} | all-to-all | bytes 524288 | tf_op jit(solution)/shard_map/all_to_all | solution.py:24
  138.7 4.5 %fusion.24 = f32[128,4096]{1,0:T(8,128)S(1)} fusion(f32[128,4096]{1,0:T(8,128)} %copy-done.5, bf16[512,4096]{1,0:T(8,128)(2,1)} %param.14, f32[128,4096]{1,0:T(8,128)S(1)} %convolution_subtract_fusion, bf16[128,4096]{1,0:T(8,128)(2,1)S(1)} %copy-done, f32[128,512]{1,0:T(8,128)} %param.13, f32[16,8,512]{2,1,0:T(8,128)S(1)} %all_to_all.96, ...), kind=kOutput, calls=%fused_computation.29 | convolution fusion | flops 542244864 | bytes 12582912 | tf_op jit(solution)/shard_map/dot_general | solution.py:115
  143.2 4.4 %fusion.46 = f32[16,8,512]{2,1,0:T(8,128)S(1)} fusion(bf16[512,4096]{1,0:T(8,128)(2,1)} %param.14, f32[128,4096]{1,0:T(8,128)S(1)} %fusion.24), kind=kOutput, calls=%fused_computation.55 | convolution fusion | flops 537395200 | bytes 6553600 | tf_op jit(solution)/shard_map/dot_general | solution.py:110
  147.7 13.4 %all_to_all.97 = f32[16,8,512]{2,1,0:T(8,128)} all-to-all(f32[16,8,512]{2,1,0:T(8,128)S(1)} %fusion.46), channel_id=1, replica_groups=mesh['scen_0'=4,'scen_1'=2,'var_0'=4,'var_1'=4] {'var_0','var_1'}, dimensions={0} | all-to-all | bytes 524288 | tf_op jit(solution)/shard_map/all_to_all | solution.py:57
  161.1 1.0 reduce_sum.139
  162.1 11.6 %all_to_all.98 = f32[16,8,512]{2,1,0:T(8,128)S(1)} all-to-all(f32[16,8,512]{2,1,0:T(8,128)S(1)} %broadcast_in_dim.105), channel_id=1, replica_groups=mesh['scen_0'=4,'scen_1'=2,'var_0'=4,'var_1'=4] {'var_0','var_1'}, dimensions={0} | all-to-all | bytes 524288 | tf_op jit(solution)/shard_map/all_to_all | solution.py:24
  173.7 4.5 %fusion.19 = f32[128,4096]{1,0:T(8,128)S(1)} fusion(f32[128,4096]{1,0:T(8,128)} %copy-done.6, bf16[512,4096]{1,0:T(8,128)(2,1)} %param.14, f32[128,4096]{1,0:T(8,128)S(1)} %convolution_subtract_fusion, bf16[128,4096]{1,0:T(8,128)(2,1)S(1)} %copy-done, f32[128,512]{1,0:T(8,128)} %param.13, f32[16,8,512]{2,1,0:T(8,128)S(1)} %all_to_all.98, ...), kind=kOutput, calls=%fused_computation.23 | convolution fusion | flops 542244864 | bytes 12582912 | tf_op jit(solution)/shard_map/dot_general | solution.py:115
  178.2 4.4 %fusion.44 = f32[16,8,512]{2,1,0:T(8,128)S(1)} fusion(bf16[512,4096]{1,0:T(8,128)(2,1)} %param.14, f32[128,4096]{1,0:T(8,128)S(1)} %fusion.19), kind=kOutput, calls=%fused_computation.53 | convolution fusion | flops 537395200 | bytes 6553600 | tf_op jit(solution)/shard_map/dot_general | solution.py:110
  182.7 12.0 %all_to_all.99 = f32[16,8,512]{2,1,0:T(8,128)} all-to-all(f32[16,8,512]{2,1,0:T(8,128)S(1)} %fusion.44), channel_id=1, replica_groups=mesh['scen_0'=4,'scen_1'=2,'var_0'=4,'var_1'=4] {'var_0','var_1'}, dimensions={0} | all-to-all | bytes 524288 | tf_op jit(solution)/shard_map/all_to_all | solution.py:57
  194.7 1.0 reduce_sum.140
  195.7 11.6 %all_to_all.100 = f32[16,8,512]{2,1,0:T(8,128)S(1)} all-to-all(f32[16,8,512]{2,1,0:T(8,128)S(1)} %broadcast_in_dim.106), channel_id=1, replica_groups=mesh['scen_0'=4,'scen_1'=2,'var_0'=4,'var_1'=4] {'var_0','var_1'}, dimensions={0} | all-to-all | bytes 524288 | tf_op jit(solution)/shard_map/all_to_all | solution.py:24
  207.3 4.5 %fusion.14 = f32[128,4096]{1,0:T(8,128)S(1)} fusion(f32[128,4096]{1,0:T(8,128)} %copy-done.7, bf16[512,4096]{1,0:T(8,128)(2,1)} %param.14, f32[128,4096]{1,0:T(8,128)S(1)} %convolution_subtract_fusion, bf16[128,4096]{1,0:T(8,128)(2,1)S(1)} %copy-done, f32[128,512]{1,0:T(8,128)} %param.13, f32[16,8,512]{2,1,0:T(8,128)S(1)} %all_to_all.100, ...), kind=kOutput, calls=%fused_computation.17 | convolution fusion | flops 542244864 | bytes 12582912 | tf_op jit(solution)/shard_map/dot_general | solution.py:115
  211.8 4.4 %fusion.42 = f32[16,8,512]{2,1,0:T(8,128)S(1)} fusion(bf16[512,4096]{1,0:T(8,128)(2,1)} %param.14, f32[128,4096]{1,0:T(8,128)S(1)} %fusion.14), kind=kOutput, calls=%fused_computation.51 | convolution fusion | flops 537395200 | bytes 6553600 | tf_op jit(solution)/shard_map/dot_general | solution.py:110
  216.3 12.0 %all_to_all.101 = f32[16,8,512]{2,1,0:T(8,128)} all-to-all(f32[16,8,512]{2,1,0:T(8,128)S(1)} %fusion.42), channel_id=1, replica_groups=mesh['scen_0'=4,'scen_1'=2,'var_0'=4,'var_1'=4] {'var_0','var_1'}, dimensions={0} | all-to-all | bytes 524288 | tf_op jit(solution)/shard_map/all_to_all | solution.py:57
  228.2 1.0 reduce_sum.141
  229.2 11.6 %all_to_all.102 = f32[16,8,512]{2,1,0:T(8,128)S(1)} all-to-all(f32[16,8,512]{2,1,0:T(8,128)S(1)} %broadcast_in_dim.107), channel_id=1, replica_groups=mesh['scen_0'=4,'scen_1'=2,'var_0'=4,'var_1'=4] {'var_0','var_1'}, dimensions={0} | all-to-all | bytes 524288 | tf_op jit(solution)/shard_map/all_to_all | solution.py:24
  240.8 4.5 %fusion.9 = f32[128,4096]{1,0:T(8,128)S(1)} fusion(f32[128,4096]{1,0:T(8,128)} %copy-done.8, bf16[512,4096]{1,0:T(8,128)(2,1)} %param.14, f32[128,4096]{1,0:T(8,128)S(1)} %convolution_subtract_fusion, bf16[128,4096]{1,0:T(8,128)(2,1)S(1)} %copy-done, f32[128,512]{1,0:T(8,128)} %param.13, f32[16,8,512]{2,1,0:T(8,128)S(1)} %all_to_all.102, ...), kind=kOutput, calls=%fused_computation.11 | convolution fusion | flops 542244864 | bytes 12582912 | tf_op jit(solution)/shard_map/dot_general | solution.py:115
  245.4 1.3 copy-done.3
  246.7 4.4 %fusion.40 = f32[16,8,512]{2,1,0:T(8,128)} fusion(bf16[512,4096]{1,0:T(8,128)(2,1)} %param.14, f32[128,4096]{1,0:T(8,128)S(1)} %fusion.9), kind=kOutput, calls=%fused_computation.49 | convolution fusion | flops 537395200 | bytes 6553600 | tf_op jit(solution)/shard_map/dot_general | solution.py:110
  251.1 4.4 %all-to-all-start.14 = ((f32[16,8,512]{2,1,0:T(8,128)}), f32[16,8,512]{2,1,0:T(8,128)}, u32[]{:S(2)}, u32[]{:S(2)}) async-start(f32[16,8,512]{2,1,0:T(8,128)} %fusion.40), calls=%async_computation.14 | async-start | bytes 524288 | tf_op jit(solution)/shard_map/all_to_all | solution.py:57
  255.7 8.3 %all-to-all-done.14 = f32[16,8,512]{2,1,0:T(8,128)} async-done(((f32[16,8,512]{2,1,0:T(8,128)}), f32[16,8,512]{2,1,0:T(8,128)}, u32[]{:S(2)}, u32[]{:S(2)}) %all-to-all-start.14) | async-done | bytes 262176 | tf_op jit(solution)/shard_map/all_to_all | solution.py:57
  264.6 4.3 %all-to-all-start.16 = ((f32[8,1,4]{2,1,0:T(1,128)}), f32[8,1,4]{2,1,0:T(1,128)S(1)}, u32[]{:S(2)}, u32[]{:S(2)}) async-start(f32[8,1,4]{2,1,0:T(1,128)} %broadcast_in_dim.110), calls=%async_computation.16 | async-start | bytes 8192 | tf_op jit(solution)/shard_map/all_to_all | solution.py:24
  268.9 1.0 reduce_sum.142
  269.8 4.2 %all-to-all-done.16 = f32[8,1,4]{2,1,0:T(1,128)S(1)} async-done(((f32[8,1,4]{2,1,0:T(1,128)}), f32[8,1,4]{2,1,0:T(1,128)S(1)}, u32[]{:S(2)}, u32[]{:S(2)}) %all-to-all-start.16) | async-done | bytes 160 | tf_op jit(solution)/shard_map/all_to_all | solution.py:24
  274.1 0.7 broadcast_in_dim.108
  274.8 4.2 %all-to-all-start.15 = ((f32[16,8,512]{2,1,0:T(8,128)}), f32[16,8,512]{2,1,0:T(8,128)}, u32[]{:S(2)}, u32[]{:S(2)}) async-start(f32[16,8,512]{2,1,0:T(8,128)} %broadcast_in_dim.108), calls=%async_computation.15 | async-start | bytes 524288 | tf_op jit(solution)/shard_map/all_to_all | solution.py:24
  279.0 0.6 fusion.89
  279.6 8.3 %all-to-all-done.15 = f32[16,8,512]{2,1,0:T(8,128)} async-done(((f32[16,8,512]{2,1,0:T(8,128)}), f32[16,8,512]{2,1,0:T(8,128)}, u32[]{:S(2)}, u32[]{:S(2)}) %all-to-all-start.15) | async-done | bytes 262176 | tf_op jit(solution)/shard_map/all_to_all | solution.py:24
  287.9 5.9 %multiply_reduce_fusion = (f32[4096]{0:T(1024)S(1)}, f32[128,4096]{1,0:T(8,128)}) fusion(f32[128]{0:T(128)S(1)} %copy-done.13, f32[128,4096]{1,0:T(8,128)} %copy-done.3, bf16[512,4096]{1,0:T(8,128)(2,1)} %param.14, f32[128,512]{1,0:T(8,128)S(1)} %copy-done.10, f32[16,8,512]{2,1,0:T(8,128)} %all-to-all-done.15, ...), kind=kOutput, calls=%fused_computation.66 | convolution fusion | flops 543289344 | bytes 12599808 | tf_op jit(solution)/shard_map/dot_general | solution.py:115
  293.9 0.6 fusion.87
  295.2 1.3 multiply_reduce_fusion.1
  297.1 2.8 fusion.54
  300.6 9.5 %all-reduce.2 = (f32[]{:T(128)}, f32[]{:T(128)}) all-reduce(f32[]{:T(128)} %fusion.54, f32[]{:T(128)S(6)} %mul.152), channel_id=1, replica_groups=mesh['scen_0'=4,'scen_1'=2,'var_0'=4,'var_1'=4] {'scen_0'}, use_global_device_ids=true, to_apply=%region_13.14 | all-reduce | flops 2 | bytes 16 | tf_op jit(solution)/shard_map/psum | solution.py:80
  310.1 3.1 all-reduce.3
  313.2 9.2 %all-reduce.1 = (f32[]{:T(128)}, f32[]{:T(128)}) all-reduce(f32[]{:T(128)} %get-tuple-element.13, f32[]{:T(128)} %get-tuple-element.14), channel_id=1, replica_groups=mesh['scen_0'=4,'scen_1'=2,'var_0'=4,'var_1'=4] {'var_0'}, use_global_device_ids=true, to_apply=%region_15.16 | all-reduce | flops 2 | bytes 16 | tf_op jit(solution)/shard_map/psum | solution.py:80
  322.4 9.3 %all-reduce = (f32[]{:T(128)}, f32[]{:T(128)}) all-reduce(f32[]{:T(128)} %get-tuple-element.9, f32[]{:T(128)} %get-tuple-element.10), channel_id=1, replica_groups=mesh['scen_0'=4,'scen_1'=2,'var_0'=4,'var_1'=4] {'var_1'}, use_global_device_ids=true, to_apply=%region_16.17 | all-reduce | flops 2 | bytes 16 | tf_op jit(solution)/shard_map/psum | solution.py:80
  333.1 0.7 broadcast_in_dim.111
  333.8 3.4 all-to-all-start.17
  337.2 3.2 multiply_add_fusion
  340.4 2.9 all-to-all-done.17
  343.7 0.7 copy.35
  (44 shorter events, 1.6 us)
Async XLA Ops:
  0.6 13.3 %copy-start.12 = (s32[128,32]{0,1:T(8,128)S(1)}, s32[128,32]{0,1:T(8,128)}, u32[]{:S(2)}) copy-start(s32[128,32]{0,1:T(8,128)} %param.17) | copy-start | bytes 49156
  0.6 26.9 %copy-start.11 = (f32[4,4096]{1,0:T(4,128)S(1)}, f32[4,4096]{1,0:T(4,128)}, u32[]{:S(2)}) copy-start(f32[4,4096]{1,0:T(4,128)} %param.16) | copy-start | bytes 196612
  5.7 16.8 %all-to-all-start = ((f32[16,8,512]{2,1,0:T(8,128)}), f32[16,8,512]{2,1,0:T(8,128)S(1)}, u32[]{:S(2)}, u32[]{:S(2)}) async-start(f32[16,8,512]{2,1,0:T(8,128)} %convolution_bitcast_fusion), calls=%async_computation | async-start | bytes 524288 | tf_op jit(solution)/shard_map/all_to_all | solution.py:57
  23.3 12.9 %all-to-all-start.1 = ((f32[16,8,512]{2,1,0:T(8,128)}), f32[16,8,512]{2,1,0:T(8,128)}, u32[]{:S(2)}, u32[]{:S(2)}) async-start(f32[16,8,512]{2,1,0:T(8,128)} %broadcast_in_dim.101), calls=%async_computation.1 | async-start | bytes 524288 | tf_op jit(solution)/shard_map/all_to_all | solution.py:24
  27.5 10.5 %copy-start = (bf16[128,4096]{1,0:T(8,128)(2,1)S(1)}, bf16[128,4096]{1,0:T(8,128)(2,1)}, u32[]{:S(2)}) copy-start(bf16[128,4096]{1,0:T(8,128)(2,1)} %param.12) | copy-start | bytes 3145732
  27.5 10.5 %copy-start.10 = (f32[128,512]{1,0:T(8,128)S(1)}, f32[128,512]{1,0:T(8,128)}, u32[]{:S(2)}) copy-start(f32[128,512]{1,0:T(8,128)} %param.13) | copy-start | bytes 786436
  37.3 0.8 copy-start.1
  42.5 4.5 %copy-start.9 = (f32[128,4096]{1,0:T(8,128)}, f32[128,4096]{1,0:T(8,128)S(1)}, u32[]{:S(2)}) copy-start(f32[128,4096]{1,0:T(8,128)S(1)} %fusion.39) | copy-start | bytes 6291460
  76.1 4.5 %copy-start.4 = (f32[128,4096]{1,0:T(8,128)}, f32[128,4096]{1,0:T(8,128)S(1)}, u32[]{:S(2)}) copy-start(f32[128,4096]{1,0:T(8,128)S(1)} %fusion.34) | copy-start | bytes 6291460
  109.7 4.5 %copy-start.5 = (f32[128,4096]{1,0:T(8,128)}, f32[128,4096]{1,0:T(8,128)S(1)}, u32[]{:S(2)}) copy-start(f32[128,4096]{1,0:T(8,128)S(1)} %fusion.29) | copy-start | bytes 6291460
  143.2 4.5 %copy-start.6 = (f32[128,4096]{1,0:T(8,128)}, f32[128,4096]{1,0:T(8,128)S(1)}, u32[]{:S(2)}) copy-start(f32[128,4096]{1,0:T(8,128)S(1)} %fusion.24) | copy-start | bytes 6291460
  178.2 4.5 %copy-start.7 = (f32[128,4096]{1,0:T(8,128)}, f32[128,4096]{1,0:T(8,128)S(1)}, u32[]{:S(2)}) copy-start(f32[128,4096]{1,0:T(8,128)S(1)} %fusion.19) | copy-start | bytes 6291460
  211.8 4.5 %copy-start.8 = (f32[128,4096]{1,0:T(8,128)}, f32[128,4096]{1,0:T(8,128)S(1)}, u32[]{:S(2)}) copy-start(f32[128,4096]{1,0:T(8,128)S(1)} %fusion.14) | copy-start | bytes 6291460
  245.3 1.3 copy-start.3
  246.7 8.8 %copy-start.13 = (f32[128]{0:T(128)S(1)}, f32[128]{0:T(128)}, u32[]{:S(2)}) copy-start(f32[128]{0:T(128)} %param.15) | copy-start | bytes 1540
  251.1 12.9 %all-to-all-start.14 = ((f32[16,8,512]{2,1,0:T(8,128)}), f32[16,8,512]{2,1,0:T(8,128)}, u32[]{:S(2)}, u32[]{:S(2)}) async-start(f32[16,8,512]{2,1,0:T(8,128)} %fusion.40), calls=%async_computation.14 | async-start | bytes 524288 | tf_op jit(solution)/shard_map/all_to_all | solution.py:57
  264.6 9.5 %all-to-all-start.16 = ((f32[8,1,4]{2,1,0:T(1,128)}), f32[8,1,4]{2,1,0:T(1,128)S(1)}, u32[]{:S(2)}, u32[]{:S(2)}) async-start(f32[8,1,4]{2,1,0:T(1,128)} %broadcast_in_dim.110), calls=%async_computation.16 | async-start | bytes 8192 | tf_op jit(solution)/shard_map/all_to_all | solution.py:24
  274.8 13.1 %all-to-all-start.15 = ((f32[16,8,512]{2,1,0:T(8,128)}), f32[16,8,512]{2,1,0:T(8,128)}, u32[]{:S(2)}, u32[]{:S(2)}) async-start(f32[16,8,512]{2,1,0:T(8,128)} %broadcast_in_dim.108), calls=%async_computation.15 | async-start | bytes 524288 | tf_op jit(solution)/shard_map/all_to_all | solution.py:24
  293.9 43.4 %copy-start.2 = (f32[128,4096]{1,0:T(8,128)S(1)}, f32[128,4096]{1,0:T(8,128)}, u32[]{:S(2)}) copy-start(f32[128,4096]{1,0:T(8,128)} %get-tuple-element.18) | copy-start | bytes 6291460
  293.9 1.3 collective-permute-start
  333.8 9.4 %all-to-all-start.17 = ((f32[8,1,4096]{2,1,0:T(1,128)}), f32[8,1,4096]{2,1,0:T(1,128)S(1)}, u32[]{:S(2)}, u32[]{:S(2)}) async-start(f32[8,1,4096]{2,1,0:T(1,128)} %broadcast_in_dim.111), calls=%async_computation.17 | async-start | bytes 262144 | tf_op jit(solution)/shard_map/all_to_all | solution.py:24
where the time goes:
time: 349 us; the launch traced here: 347 us
  blocking collectives  174 us (50%)
  matrix products  76.6 us (22%)
  waiting for transfers between devices  37.8 us (11%)
  starting transfers between devices  28.6 us (8%)
  other arithmetic  15.8 us (5%)
  local copies, waits for them, and re-layouts  6.98 us (2%)
  between operations  6.86 us (2%)
    all_to_all x6, blocking collectives, sum_at_owner(): lax.all_to_all(pieces, axis, split_axis=0, concat_axis=0, tiled=True)  73.2 us
    all_to_all x6, blocking collectives, copy_for_each(): lax.all_to_all(jnp.broadcast_to(x[None], (devices, *x.shape)), axis, 0, 0...  69.6 us
    dot_general x8, matrix products, shards(): jnp.dot(shortfall, technology, preferred_element_type=jnp.float32)  37.5 us
    dot_general x8, matrix products, shards(): lax.dot_general(rounded, technology, (((1,), (1,)), ((), ())), preferred_...  36.2 us
    psum x4, blocking collectives, by_axis(): x = lax.psum(x, axis)  31.1 us
    all_to_all x4, waiting for transfers between devices, copy_for_each(): lax.all_to_all(jnp.broadcast_to(x[None], (devices, *x.shape)), axis, 0, 0...  21.1 us
    all_to_all x2, waiting for transfers between devices, sum_at_owner(): lax.all_to_all(pieces, axis, split_axis=0, concat_axis=0, tiled=True)  16.8 us
    all_to_all x4, starting transfers between devices, copy_for_each(): lax.all_to_all(jnp.broadcast_to(x[None], (devices, *x.shape)), axis, 0, 0...  16 us
  transfers between devices with their start and end apart: 7, of which 6 were waited for; matrix products, arithmetic and copies ran while one was open for 3% of the time, Pallas kernels for 0%

commit v1 on v0

v1 whole, which is shorter than its diff:
```python
import jax
import jax.numpy as jnp
from jax import lax
from jax.experimental import pallas as pl
from jax.experimental.pallas import tpu as pltpu
from jax.sharding import Mesh
from jax.sharding import PartitionSpec as P

V = 65536
BLK = 128
STEPS = 8
SCEN = ("x", "core")
VAR = ("z", "y")
CHUNK = 512
LANES = 128

penalty = 1.0
recourse_scale = 4.0
stride = 0.2
epsilon = 1e-06

WHOLE = pl.BlockSpec(memory_space=pltpu.VMEM)


def local_call(body, outs, args, flops=0, limit=48 << 20, aliases=None):
    outs = [jax.ShapeDtypeStruct(s, jnp.float32) for s in outs]
    moved = sum(a.size * a.dtype.itemsize for a in args) + sum(4 * o.size for o in outs)
    return pl.pallas_call(
        body,
        out_shape=outs,
        in_specs=[WHOLE] * len(args),
        out_specs=[WHOLE] * len(outs),
        input_output_aliases=aliases or {},
        compiler_params=pltpu.CompilerParams(vmem_limit_bytes=limit),
        cost_estimate=pl.CostEstimate(flops=flops, bytes_accessed=moved, transcendentals=0),
    )(*args)


def image_of(x, tech):
    return lax.dot_general(
        x.astype(jnp.bfloat16), tech, (((1,), (1,)), ((), ())), preferred_element_type=jnp.float32
    )


def first_image(x_ref, tech_ref, image_ref):
    total = None
    for start in range(0, x_ref.shape[1], CHUNK):
        cols = slice(start, start + CHUNK)
        part = image_of(x_ref[:, cols], tech_ref[:, cols])
        total = part if total is None else total + part
    image_ref[...] = total


def coefficients(mult_ref, cost_ref, curv_ref, old_ref, active_ref, scale_ref, shift_ref):
    for block in range(mult_ref.shape[1] // BLK):
        cols = slice(block * BLK, (block + 1) * BLK)
        linear = cost_ref[:, cols].astype(jnp.float32) + mult_ref[:, cols] - penalty * old_ref[:, cols]
        diagonal = curv_ref[:, cols].astype(jnp.float32) + penalty
        on = jnp.broadcast_to(active_ref[:, block : block + 1], linear.shape) > 0
        scale_ref[:, cols] = jnp.where(on, 1.0 - stride * diagonal, 1.0)
        shift_ref[:, cols] = jnp.where(on, -stride * linear, 0.0)


def stepped(start, shortfall, tech, x_ref, scale_ref, shift_ref, gain_ref):
    pullback = jnp.dot(shortfall, tech, preferred_element_type=jnp.float32)
    pieces = []
    for k in range(CHUNK // BLK):
        cols = slice(start + k * BLK, start + (k + 1) * BLK)
        block = (start + k * BLK) // BLK
        gain = jnp.broadcast_to(gain_ref[:, block : block + 1], (x_ref.shape[0], BLK))
        moved = x_ref[:, cols] * scale_ref[:, cols] + shift_ref[:, cols]
        moved = moved - gain * pullback[:, k * BLK : (k + 1) * BLK]
        pieces.append(jnp.clip(moved, -1.0, 1.0))
    return jnp.concatenate(pieces, axis=1)


def step(image_ref, rhs_ref, tech_ref, x_ref, scale_ref, shift_ref, gain_ref, new_ref, out_ref):
    shortfall = (image_ref[...] - rhs_ref[...]).astype(jnp.bfloat16)
    total = None
    for start in range(0, x_ref.shape[1], CHUNK):
        cols = slice(start, start + CHUNK)
        tech = tech_ref[:, cols]
        new = stepped(start, shortfall, tech, x_ref, scale_ref, shift_ref, gain_ref)
        new_ref[:, cols] = new
        part = image_of(new, tech)
        total = part if total is None else total + part
    out_ref[...] = total


def last_step(image_ref, rhs_ref, tech_ref, x_ref, scale_ref, shift_ref, gain_ref, weight_ref, new_ref, row_ref):
    shortfall = (image_ref[...] - rhs_ref[...]).astype(jnp.bfloat16)
    for start in range(0, x_ref.shape[1], CHUNK):
        cols = slice(start, start + CHUNK)
        new = stepped(start, shortfall, tech_ref[:, cols], x_ref, scale_ref, shift_ref, gain_ref)
        new_ref[:, cols] = new
        weight = jnp.broadcast_to(weight_ref[...], (x_ref.shape[0], BLK))
        for k in range(CHUNK // BLK):
            here = slice(start + k * BLK, start + (k + 1) * BLK)
            row_ref[:, here] = jnp.sum(weight * new[:, k * BLK : (k + 1) * BLK], axis=0, keepdims=True)
    mass = jnp.sum(jnp.broadcast_to(weight_ref[...], (x_ref.shape[0], LANES)), axis=0, keepdims=True)
    row_ref[:, x_ref.shape[1] :] = mass


def own_spread(x_ref, row_ref, weight_ref, out_ref):
    width = x_ref.shape[1]
    weight = jnp.broadcast_to(weight_ref[...], (x_ref.shape[0], BLK))
    mass = row_ref[:, width:]
    total = jnp.zeros((x_ref.shape[0], BLK), jnp.float32)
    for start in range(0, width, BLK):
        away = x_ref[:, start : start + BLK] - row_ref[:, start : start + BLK] / mass
        total = total + weight * away * away
    out_ref[...] = jnp.sum(total, axis=0, keepdims=True)


def node_row(own_ref, other_ref, old_ref, spread_ref, leads_ref, out_ref):
    width = old_ref.shape[1]
    own_mass, other_mass = own_ref[:, width:], other_ref[:, width:]
    mass = own_mass + other_mass
    apart = jnp.zeros((1, BLK), jnp.float32)
    drift = jnp.zeros((1, BLK), jnp.float32)
    for start in range(0, width, BLK):
        cols = slice(start, start + BLK)
        own, other = own_ref[:, cols], other_ref[:, cols]
        mean = (own + other) / mass
        out_ref[:, cols] = mean
        gap = own / own_mass - other / other_mass
        apart = apart + gap * gap
        drift = drift + (mean - old_ref[:, cols]) ** 2
    leads = leads_ref[...]
    spread = spread_ref[...] + leads * (own_mass * other_mass / mass) * apart
    drift = leads * mass * drift
    lane = lax.broadcasted_iota(jnp.int32, (1, LANES), 1)
    spread = jnp.sum(spread, axis=1, keepdims=True)
    drift = jnp.sum(drift, axis=1, keepdims=True)
    parts = jnp.where(lane == 0, spread, jnp.where(lane == 1, drift, own_mass))
    out_ref[:, width:] = parts


def new_duals(mult_ref, x_ref, mean_ref, factor_ref, out_ref):
    for start in range(0, x_ref.shape[1], CHUNK):
        cols = slice(start, start + CHUNK)
        factor = factor_ref[:, 0:1]
        out_ref[:, cols] = mult_ref[:, cols] + factor * (x_ref[:, cols] - mean_ref[:, cols])


def to_all(x, axes):
    devices = lax.axis_size(axes)
    return lax.all_to_all(jnp.broadcast_to(x[None], (devices, *x.shape)), axes, 0, 0, tiled=True)


def total_of(partial, axes):
    devices = lax.axis_size(axes)
    rows, width = partial.shape
    pieces = partial.reshape(devices, rows // devices, width)
    arrived = lax.all_to_all(pieces, axes, 0, 0, tiled=True)
    return to_all(jnp.sum(arrived, axis=0), axes).reshape(rows, width)


def shards(
    start_point,
    multipliers,
    cost,
    curvature,
    recourse_rhs,
    technology,
    scenario_weight,
    previous_mean,
    active,
):
    rows, width = start_point.shape
    images = recourse_rhs.shape[1]
    groups = previous_mean.shape[0]
    group_size = lax.axis_size(SCEN) // groups
    position = lax.axis_index(SCEN)
    old_row = lax.dynamic_slice_in_dim(previous_mean, position // group_size, 1, 0)
    weight = scenario_weight[:, None]
    leads = jnp.full((1, LANES), (position % group_size == 0).astype(jnp.float32))
    gain = (stride * recourse_scale) * active.astype(jnp.float32)
    product = 2 * rows * width * images

    (partial,) = local_call(first_image, [(rows, images)], [start_point, technology], product)
    scale, shift = local_call(
        coefficients, [(rows, width)] * 2, [multipliers, cost, curvature, old_row, active], 8 * rows * width
    )
    iterate = start_point
    for sweep in range(STEPS):
        image = total_of(partial, VAR)
        operands = [image, recourse_rhs, technology, iterate, scale, shift, gain]
        if sweep < STEPS - 1:
            iterate, partial = local_call(step, [(rows, width), (rows, images)], operands, 2 * product)
        else:
            iterate, own_row = local_call(
                last_step, [(rows, width), (1, width + LANES)], [*operands, weight], product
            )
    other_row = lax.ppermute(own_row, "core", [(0, 1), (1, 0)])
    (spread,) = local_call(own_spread, [(1, LANES)], [iterate, own_row, weight], 4 * rows * width)
    (row,) = local_call(node_row, [(1, width + LANES)], [own_row, other_row, old_row, spread, leads])
    everyone = to_all(row, SCEN)
    bundle_mean = everyone[::group_size, 0, :width]
    parts = jnp.sum(everyone[:, :, width:], axis=0)
    sums = jnp.sum(to_all(parts, VAR), axis=0)
    normaliser = sums[0, 2] / lax.axis_size(VAR) * V
    primal_norm = jnp.sqrt(sums[0, 0] / normaliser + epsilon)
    dual_norm = penalty * jnp.sqrt(sums[0, 1] / normaliser + epsilon)
    factor = penalty * jnp.sqrt(primal_norm / dual_norm)
    (new_multipliers,) = local_call(
        new_duals,
        [(rows, width)],
        [multipliers, iterate, row[:, :width], jnp.full((1, LANES), factor)],
        3 * rows * width,
    )
    return (iterate, new_multipliers, bundle_mean, primal_norm, dual_norm)


def solution(mesh):
    torus = Mesh(mesh.devices.reshape(4, 2, 4, 4), ("x", "core", "z", "y"))
    return jax.shard_map(
        shards,
        mesh=torus,
        in_specs=(
            P(SCEN, VAR),
            P(SCEN, VAR),
            P(SCEN, VAR),
            P(SCEN, VAR),
            P(SCEN, None),
            P(None, VAR),
            P(SCEN),
            P(None, VAR),
            P(SCEN, VAR),
        ),
        out_specs=(P(SCEN, VAR), P(SCEN, VAR), P(None, VAR), P(), P()),
        check_vma=False,
    )
```

time: 349 us -> 303 us (0.87)
  matrix products: 76.6 us -> 0 us
  Pallas kernels: 0 us -> 57.8 us
  local copies, waits for them, and re-layouts: 6.98 us -> 30 us
  other arithmetic: 15.8 us -> 0.27 us
  waiting for transfers between devices: 37.8 us -> 24.8 us
  starting transfers between devices: 28.6 us -> 18.7 us
  blocking collectives: 174 us -> 165 us
    dot_general x17 -> x0, matrix products: 76.6 us -> none  [the longest x8 37.5 us: shards(): jnp.dot(shortfall, technology, preferred_element_type=jnp.float32)]
    pallas_call x0 -> x13, Pallas kernels: none -> 57.8 us  [local_call(): pl.pallas_call(body, out_shape=outs, in_specs=[WHOLE] * len(args), out_sp...]
    psum x4 -> x0, blocking collectives: 31.1 us -> none  [by_axis(): x = lax.psum(x, axis)]
    unnamed x29 -> x52, local copies, waits for them, and re-layouts: 2.84 us -> 27 us
    all_to_all x12 -> x14, blocking collectives: 143 us -> 165 us  [the longest x7 84.8 us: total_of(): arrived = lax.all_to_all(pieces, axes, 0, 0, tiled=True)]
    all_to_all x6 -> x4, waiting for transfers between devices: 37.8 us -> 24.8 us  [the longest x3 16.1 us: to_all(): lax.all_to_all(jnp.broadcast_to(x[None], (devices, *x.shape)), axes, 0, 0...]
    reduce_sum x13 -> x10, other arithmetic: 12.3 us -> 0.21 us  [the longest x8 0.17 us: total_of(): return to_all(jnp.sum(arrived, axis=0), axes).reshape(rows, width)]
    all_to_all x6 -> x4, starting transfers between devices: 28.6 us -> 18.7 us  [the longest x3 10.5 us: to_all(): lax.all_to_all(jnp.broadcast_to(x[None], (devices, *x.shape)), axes, 0, 0...]
  transfers between devices with their start and end apart: 7 -> 5, of which waited for: 6 -> 4; matrix products, arithmetic and copies ran while one was open for 3% -> 0% of each run, Pallas kernels for 0% -> 1%
where the time goes in v1:
time: 303 us; the launch traced here: 302 us
  blocking collectives  165 us (54%)
  Pallas kernels  57.8 us (19%)
  local copies, waits for them, and re-layouts  30 us (10%)
  waiting for transfers between devices  24.8 us (8%)
  starting transfers between devices  18.7 us (6%)
  between operations  5.4 us (2%)
    all_to_all x7, blocking collectives, total_of(): arrived = lax.all_to_all(pieces, axes, 0, 0, tiled=True)  84.8 us
    all_to_all x7, blocking collectives, to_all(): lax.all_to_all(jnp.broadcast_to(x[None], (devices, *x.shape)), axes, 0, 0...  80.3 us
    pallas_call x13, Pallas kernels, local_call(): pl.pallas_call(body, out_shape=outs, in_specs=[WHOLE] * len(args), out_sp...  57.8 us
    unnamed x52, local copies, waits for them, and re-layouts  27 us
    all_to_all x3, waiting for transfers between devices, to_all(): lax.all_to_all(jnp.broadcast_to(x[None], (devices, *x.shape)), axes, 0, 0...  16.1 us
    all_to_all x3, starting transfers between devices, to_all(): lax.all_to_all(jnp.broadcast_to(x[None], (devices, *x.shape)), axes, 0, 0...  10.5 us
    all_to_all x1, waiting for transfers between devices, total_of(): arrived = lax.all_to_all(pieces, axes, 0, 0, tiled=True)  8.67 us
    all_to_all x1, starting transfers between devices, total_of(): arrived = lax.all_to_all(pieces, axes, 0, 0, tiled=True)  8.13 us
  transfers between devices with their start and end apart: 5, of which 4 were waited for; matrix products, arithmetic and copies ran while one was open for 0% of the time, Pallas kernels for 1%

profile of v1, /device:TPU:0, one launch (start us, length us, event | category | flops | bytes accessed | tf_op | source)
XLA Modules:
  0.0 302.1 jit_solution(14872137174361094660)
XLA Ops:
  0.6 0.0 copy-start
  0.6 0.0 copy-start.7
  0.7 1.6 copy-done.7
  2.3 4.4 %shard_map.128 = f32[128,512]{1,0:T(8,128)} custom-call(f32[128,4096]{1,0:T(8,128)S(1)} %copy-done.7, bf16[512,4096]{1,0:T(8,128)(2,1)} %tech_ref.17), custom_call_target="tpu_custom_call" | custom-call | flops 536870912 | bytes 6553600 | tf_op jit(solution)/shard_map/pallas_call | solution.py:28
  6.7 8.1 %all-to-all-start = ((f32[16,8,512]{2,1,0:T(8,128)}), f32[16,8,512]{2,1,0:T(8,128)S(1)}, u32[]{:S(2)}, u32[]{:S(2)}) async-start(f32[16,8,512]{2,1,0:T(8,128)} %bitcast), calls=%async_computation | async-start | bytes 524288 | tf_op jit(solution)/shard_map/all_to_all | solution.py:155
  14.8 8.7 %all-to-all-done = f32[16,8,512]{2,1,0:T(8,128)S(1)} async-done(((f32[16,8,512]{2,1,0:T(8,128)}), f32[16,8,512]{2,1,0:T(8,128)S(1)}, u32[]{:S(2)}, u32[]{:S(2)}) %all-to-all-start) | async-done | bytes 262176 | tf_op jit(solution)/shard_map/all_to_all | solution.py:155
  23.5 0.7 broadcast_in_dim.28
  24.3 3.5 %all-to-all-start.1 = ((f32[16,8,512]{2,1,0:T(8,128)}), f32[16,8,512]{2,1,0:T(8,128)S(1)}, u32[]{:S(2)}, u32[]{:S(2)}) async-start(f32[16,8,512]{2,1,0:T(8,128)} %broadcast_in_dim.28), calls=%async_computation.1 | async-start | bytes 524288 | tf_op jit(solution)/shard_map/all_to_all | solution.py:148
  27.8 0.1 copy.26.active_ref
  27.9 1.2 copy-done.21
  29.2 1.2 copy-done.22
  30.4 3.9 %shard_map.129 = (f32[128,4096]{1,0:T(8,128)S(1)}, f32[128,4096]{1,0:T(8,128)}) custom-call(f32[128,4096]{1,0:T(8,128)} %mult_ref.3, bf16[128,4096]{1,0:T(8,128)(2,1)S(1)} %copy-done.21, bf16[128,4096]{1,0:T(8,128)(2,1)S(1)} %copy-done.22, f32[1,4096]{1,0:T(1,128)S(1)} %constant_dynamic-slice_fusion.old_ref, s32[128,32]{1,0:T(8,128)S(1)} %copy.26.active_ref), custom_call_target="tpu_custom_call" | custom-call | flops 4194304 | bytes 8421376 | tf_op jit(solution)/shard_map/pallas_call | solution.py:28
  34.3 1.3 copy-done.1
  35.6 0.9 all-to-all-done.1
  36.5 6.0 %shard_map.130 = (f32[128,4096]{1,0:T(8,128)S(1)}, f32[128,512]{1,0:T(8,128)S(1)}) custom-call(f32[128,512]{1,0:T(8,128)S(1)} %bitcast.24, f32[128,512]{1,0:T(8,128)S(1)} %copy-done.3, bf16[512,4096]{1,0:T(8,128)(2,1)} %tech_ref.17, f32[128,4096]{1,0:T(8,128)S(1)} %copy-done.8, f32[128,4096]{1,0:T(8,128)} %copy-done.1, ...), custom_call_target="tpu_custom_call" | custom-call | flops 1073741824 | bytes 13385728 | tf_op jit(solution)/shard_map/pallas_call | solution.py:28
  42.5 1.3 copy-done.19
  43.8 14.8 %all_to_all.90 = f32[16,8,512]{2,1,0:T(8,128)S(1)} all-to-all(f32[16,8,512]{2,1,0:T(8,128)S(1)} %bitcast.38), channel_id=1, replica_groups=mesh['x'=4,'core'=2,'z'=4,'y'=4] {'z','y'}, dimensions={0} | all-to-all | bytes 524288 | tf_op jit(solution)/shard_map/all_to_all | solution.py:155
  58.6 11.6 %all_to_all.91 = f32[16,8,512]{2,1,0:T(8,128)S(1)} all-to-all(f32[16,8,512]{2,1,0:T(8,128)S(1)} %broadcast_in_dim.29), channel_id=1, replica_groups=mesh['x'=4,'core'=2,'z'=4,'y'=4] {'z','y'}, dimensions={0} | all-to-all | bytes 524288 | tf_op jit(solution)/shard_map/all_to_all | solution.py:148
  70.2 1.6 copy-done.20
  71.8 6.0 %shard_map.131 = (f32[128,4096]{1,0:T(8,128)S(1)}, f32[128,512]{1,0:T(8,128)S(1)}) custom-call(f32[128,512]{1,0:T(8,128)S(1)} %bitcast.26, f32[128,512]{1,0:T(8,128)S(1)} %copy-done.3, bf16[512,4096]{1,0:T(8,128)(2,1)} %tech_ref.17, f32[128,4096]{1,0:T(8,128)S(1)} %copy-done.20, f32[128,4096]{1,0:T(8,128)} %copy-done.1, ...), custom_call_target="tpu_custom_call" | custom-call | flops 1073741824 | bytes 13385728 | tf_op jit(solution)/shard_map/pallas_call | solution.py:28
  77.8 11.6 %all_to_all.92 = f32[16,8,512]{2,1,0:T(8,128)S(1)} all-to-all(f32[16,8,512]{2,1,0:T(8,128)S(1)} %bitcast.32), channel_id=1, replica_groups=mesh['x'=4,'core'=2,'z'=4,'y'=4] {'z','y'}, dimensions={0} | all-to-all | bytes 524288 | tf_op jit(solution)/shard_map/all_to_all | solution.py:155
  89.4 11.6 %all_to_all.93 = f32[16,8,512]{2,1,0:T(8,128)S(1)} all-to-all(f32[16,8,512]{2,1,0:T(8,128)S(1)} %broadcast_in_dim.30), channel_id=1, replica_groups=mesh['x'=4,'core'=2,'z'=4,'y'=4] {'z','y'}, dimensions={0} | all-to-all | bytes 524288 | tf_op jit(solution)/shard_map/all_to_all | solution.py:148
  101.0 6.0 %shard_map.132 = (f32[128,4096]{1,0:T(8,128)S(1)}, f32[128,512]{1,0:T(8,128)S(1)}) custom-call(f32[128,512]{1,0:T(8,128)S(1)} %bitcast.27, f32[128,512]{1,0:T(8,128)S(1)} %copy-done.3, bf16[512,4096]{1,0:T(8,128)(2,1)} %tech_ref.17, f32[128,4096]{1,0:T(8,128)S(1)} %get-tuple-element.28.x_ref, f32[128,4096]{1,0:T(8,128)} %copy-done.1, ...), custom_call_target="tpu_custom_call" | custom-call | flops 1073741824 | bytes 13385728 | tf_op jit(solution)/shard_map/pallas_call | solution.py:28
  107.0 1.3 copy-done.11
  108.3 11.7 %all_to_all.94 = f32[16,8,512]{2,1,0:T(8,128)S(1)} all-to-all(f32[16,8,512]{2,1,0:T(8,128)S(1)} %bitcast.33), channel_id=1, replica_groups=mesh['x'=4,'core'=2,'z'=4,'y'=4] {'z','y'}, dimensions={0} | all-to-all | bytes 524288 | tf_op jit(solution)/shard_map/all_to_all | solution.py:155
  120.1 11.5 %all_to_all.95 = f32[16,8,512]{2,1,0:T(8,128)S(1)} all-to-all(f32[16,8,512]{2,1,0:T(8,128)S(1)} %broadcast_in_dim.31), channel_id=1, replica_groups=mesh['x'=4,'core'=2,'z'=4,'y'=4] {'z','y'}, dimensions={0} | all-to-all | bytes 524288 | tf_op jit(solution)/shard_map/all_to_all | solution.py:148
  131.6 1.6 copy-done.12
  133.1 6.0 %shard_map.133 = (f32[128,4096]{1,0:T(8,128)S(1)}, f32[128,512]{1,0:T(8,128)S(1)}) custom-call(f32[128,512]{1,0:T(8,128)S(1)} %bitcast.28, f32[128,512]{1,0:T(8,128)S(1)} %copy-done.3, bf16[512,4096]{1,0:T(8,128)(2,1)} %tech_ref.17, f32[128,4096]{1,0:T(8,128)S(1)} %copy-done.12, f32[128,4096]{1,0:T(8,128)} %copy-done.1, ...), custom_call_target="tpu_custom_call" | custom-call | flops 1073741824 | bytes 13385728 | tf_op jit(solution)/shard_map/pallas_call | solution.py:28
  139.1 1.3 copy-done.13
  140.5 12.0 %all_to_all.96 = f32[16,8,512]{2,1,0:T(8,128)S(1)} all-to-all(f32[16,8,512]{2,1,0:T(8,128)S(1)} %bitcast.34), channel_id=1, replica_groups=mesh['x'=4,'core'=2,'z'=4,'y'=4] {'z','y'}, dimensions={0} | all-to-all | bytes 524288 | tf_op jit(solution)/shard_map/all_to_all | solution.py:155
  152.5 11.8 %all_to_all.97 = f32[16,8,512]{2,1,0:T(8,128)S(1)} all-to-all(f32[16,8,512]{2,1,0:T(8,128)S(1)} %broadcast_in_dim.32), channel_id=1, replica_groups=mesh['x'=4,'core'=2,'z'=4,'y'=4] {'z','y'}, dimensions={0} | all-to-all | bytes 524288 | tf_op jit(solution)/shard_map/all_to_all | solution.py:148
  164.3 1.6 copy-done.14
  165.9 6.0 %shard_map.134 = (f32[128,4096]{1,0:T(8,128)S(1)}, f32[128,512]{1,0:T(8,128)S(1)}) custom-call(f32[128,512]{1,0:T(8,128)S(1)} %bitcast.29, f32[128,512]{1,0:T(8,128)S(1)} %copy-done.3, bf16[512,4096]{1,0:T(8,128)(2,1)} %tech_ref.17, f32[128,4096]{1,0:T(8,128)S(1)} %copy-done.14, f32[128,4096]{1,0:T(8,128)} %copy-done.1, ...), custom_call_target="tpu_custom_call" | custom-call | flops 1073741824 | bytes 13385728 | tf_op jit(solution)/shard_map/pallas_call | solution.py:28
  171.9 1.3 copy-done.15
  173.2 11.6 %all_to_all.98 = f32[16,8,512]{2,1,0:T(8,128)S(1)} all-to-all(f32[16,8,512]{2,1,0:T(8,128)S(1)} %bitcast.35), channel_id=1, replica_groups=mesh['x'=4,'core'=2,'z'=4,'y'=4] {'z','y'}, dimensions={0} | all-to-all | bytes 524288 | tf_op jit(solution)/shard_map/all_to_all | solution.py:155
  184.8 11.6 %all_to_all.99 = f32[16,8,512]{2,1,0:T(8,128)S(1)} all-to-all(f32[16,8,512]{2,1,0:T(8,128)S(1)} %broadcast_in_dim.33), channel_id=1, replica_groups=mesh['x'=4,'core'=2,'z'=4,'y'=4] {'z','y'}, dimensions={0} | all-to-all | bytes 524288 | tf_op jit(solution)/shard_map/all_to_all | solution.py:148
  196.4 1.6 copy-done.16
  198.0 6.0 %shard_map.135 = (f32[128,4096]{1,0:T(8,128)S(1)}, f32[128,512]{1,0:T(8,128)S(1)}) custom-call(f32[128,512]{1,0:T(8,128)S(1)} %bitcast.30, f32[128,512]{1,0:T(8,128)S(1)} %copy-done.3, bf16[512,4096]{1,0:T(8,128)(2,1)} %tech_ref.17, f32[128,4096]{1,0:T(8,128)S(1)} %copy-done.16, f32[128,4096]{1,0:T(8,128)} %copy-done.1, ...), custom_call_target="tpu_custom_call" | custom-call | flops 1073741824 | bytes 13385728 | tf_op jit(solution)/shard_map/pallas_call | solution.py:28
  204.0 1.3 copy-done.17
  205.3 11.6 %all_to_all.100 = f32[16,8,512]{2,1,0:T(8,128)S(1)} all-to-all(f32[16,8,512]{2,1,0:T(8,128)S(1)} %bitcast.36), channel_id=1, replica_groups=mesh['x'=4,'core'=2,'z'=4,'y'=4] {'z','y'}, dimensions={0} | all-to-all | bytes 524288 | tf_op jit(solution)/shard_map/all_to_all | solution.py:155
  216.9 12.0 %all_to_all.101 = f32[16,8,512]{2,1,0:T(8,128)S(1)} all-to-all(f32[16,8,512]{2,1,0:T(8,128)S(1)} %broadcast_in_dim.34), channel_id=1, replica_groups=mesh['x'=4,'core'=2,'z'=4,'y'=4] {'z','y'}, dimensions={0} | all-to-all | bytes 524288 | tf_op jit(solution)/shard_map/all_to_all | solution.py:148
  229.0 1.6 copy-done.18
  230.6 6.1 %shard_map.136 = (f32[128,4096]{1,0:T(8,128)S(1)}, f32[128,512]{1,0:T(8,128)S(1)}) custom-call(f32[128,512]{1,0:T(8,128)S(1)} %bitcast.31, f32[128,512]{1,0:T(8,128)S(1)} %copy-done.3, bf16[512,4096]{1,0:T(8,128)(2,1)} %tech_ref.17, f32[128,4096]{1,0:T(8,128)S(1)} %copy-done.18, f32[128,4096]{1,0:T(8,128)} %copy-done.1, ...), custom_call_target="tpu_custom_call" | custom-call | flops 1073741824 | bytes 13385728 | tf_op jit(solution)/shard_map/pallas_call | solution.py:28
  236.7 1.3 copy-done.9
  238.0 11.6 %all_to_all.102 = f32[16,8,512]{2,1,0:T(8,128)S(1)} all-to-all(f32[16,8,512]{2,1,0:T(8,128)S(1)} %bitcast.37), channel_id=1, replica_groups=mesh['x'=4,'core'=2,'z'=4,'y'=4] {'z','y'}, dimensions={0} | all-to-all | bytes 524288 | tf_op jit(solution)/shard_map/all_to_all | solution.py:155
  249.7 0.7 broadcast_in_dim.35
  250.4 3.5 %all-to-all-start.15 = ((f32[16,8,512]{2,1,0:T(8,128)}), f32[16,8,512]{2,1,0:T(8,128)S(1)}, u32[]{:S(2)}, u32[]{:S(2)}) async-start(f32[16,8,512]{2,1,0:T(8,128)} %broadcast_in_dim.35), calls=%async_computation.15 | async-start | bytes 524288 | tf_op jit(solution)/shard_map/all_to_all | solution.py:148
  253.9 0.1 copy.28.weight_ref
  254.1 8.5 %all-to-all-done.15 = f32[16,8,512]{2,1,0:T(8,128)S(1)} async-done(((f32[16,8,512]{2,1,0:T(8,128)}), f32[16,8,512]{2,1,0:T(8,128)S(1)}, u32[]{:S(2)}, u32[]{:S(2)}) %all-to-all-start.15) | async-done | bytes 262176 | tf_op jit(solution)/shard_map/all_to_all | solution.py:148
  262.6 1.6 copy-done.10
  264.2 5.3 %shard_map.137 = (f32[128,4096]{1,0:T(8,128)}, f32[1,4224]{1,0:T(1,128)S(1)}) custom-call(f32[128,512]{1,0:T(8,128)S(1)} %bitcast.25, f32[128,512]{1,0:T(8,128)S(1)} %copy-done.3, bf16[512,4096]{1,0:T(8,128)(2,1)} %tech_ref.17, f32[128,4096]{1,0:T(8,128)S(1)} %copy-done.10, f32[128,4096]{1,0:T(8,128)S(1)} %copy-done.2, ...), custom_call_target="tpu_custom_call" | custom-call | flops 536870912 | bytes 13140992 | tf_op jit(solution)/shard_map/pallas_call | solution.py:28
  269.5 1.7 copy-done.5
  271.2 0.4 shard_map.138.spread_ref
  271.6 0.1 shard_map.139
  271.8 0.1 broadcast_in_dim.39
  271.9 10.3 %all_to_all.103 = f32[8,1,4224]{2,1,0:T(1,128)S(1)} all-to-all(f32[8,1,4224]{2,1,0:T(1,128)S(1)} %broadcast_in_dim.39), channel_id=1, replica_groups=mesh['x'=4,'core'=2,'z'=4,'y'=4] {'x','core'}, dimensions={0} | all-to-all | bytes 270336 | tf_op jit(solution)/shard_map/all_to_all | solution.py:148
  282.2 0.6 broadcast_in_dim.40
  282.8 3.5 %all-to-all-start.17 = ((f32[16,1,128]{2,1,0:T(1,128)}), f32[16,1,128]{2,1,0:T(1,128)S(1)}, u32[]{:S(2)}, u32[]{:S(2)}) async-start(f32[16,1,128]{2,1,0:T(1,128)} %broadcast_in_dim.40), calls=%async_computation.17 | async-start | bytes 16384 | tf_op jit(solution)/shard_map/all_to_all | solution.py:148
  286.3 0.7 copy.33
  287.0 6.7 %all-to-all-done.17 = f32[16,1,128]{2,1,0:T(1,128)S(1)} async-done(((f32[16,1,128]{2,1,0:T(1,128)}), f32[16,1,128]{2,1,0:T(1,128)S(1)}, u32[]{:S(2)}, u32[]{:S(2)}) %all-to-all-start.17) | async-done | bytes 8224 | tf_op jit(solution)/shard_map/all_to_all | solution.py:148
  293.7 0.6 fusion
  296.5 0.0 copy-start.6
  296.5 1.6 copy-done.6
  298.1 1.8 shard_map.140
  (54 shorter events, 0.5 us)
Async XLA Ops:
  0.6 27.2 %copy-start = (f32[4,4096]{1,0:T(4,128)S(1)}, f32[4,4096]{1,0:T(4,128)}, u32[]{:S(2)}) copy-start(f32[4,4096]{1,0:T(4,128)} %param.16) | copy-start | bytes 196612
  0.6 1.6 copy-start.7
  2.3 25.6 %copy-start.23 = (s32[128,32]{0,1:T(8,128)S(1)}, s32[128,32]{0,1:T(8,128)}, u32[]{:S(2)}) copy-start(s32[128,32]{0,1:T(8,128)} %param.17) | copy-start | bytes 49156
  6.7 16.8 %all-to-all-start = ((f32[16,8,512]{2,1,0:T(8,128)}), f32[16,8,512]{2,1,0:T(8,128)S(1)}, u32[]{:S(2)}, u32[]{:S(2)}) async-start(f32[16,8,512]{2,1,0:T(8,128)} %bitcast), calls=%async_computation | async-start | bytes 524288 | tf_op jit(solution)/shard_map/all_to_all | solution.py:155
  24.3 12.2 %all-to-all-start.1 = ((f32[16,8,512]{2,1,0:T(8,128)}), f32[16,8,512]{2,1,0:T(8,128)S(1)}, u32[]{:S(2)}, u32[]{:S(2)}) async-start(f32[16,8,512]{2,1,0:T(8,128)} %broadcast_in_dim.28), calls=%async_computation.1 | async-start | bytes 524288 | tf_op jit(solution)/shard_map/all_to_all | solution.py:148
  27.9 1.2 copy-start.21
  29.2 1.2 copy-start.22
  30.4 6.1 %copy-start.3 = (f32[128,512]{1,0:T(8,128)S(1)}, f32[128,512]{1,0:T(8,128)}, u32[]{:S(2)}) copy-start(f32[128,512]{1,0:T(8,128)} %rhs_ref.15) | copy-start | bytes 786436
  30.4 6.1 %copy-start.8 = (f32[128,4096]{1,0:T(8,128)S(1)}, f32[128,4096]{1,0:T(8,128)}, u32[]{:S(2)}) copy-start(f32[128,4096]{1,0:T(8,128)} %x_ref.3) | copy-start | bytes 6291460
  34.2 1.3 copy-start.1
  42.4 1.3 copy-start.19
  70.2 1.6 copy-start.20
  107.0 1.3 copy-start.11
  131.6 1.6 copy-start.12
  139.1 1.3 copy-start.13
  164.3 1.6 copy-start.14
  171.8 1.3 copy-start.15
  196.4 1.6 copy-start.16
  204.0 1.3 copy-start.17
  229.0 1.6 copy-start.18
  230.6 23.4 %copy-start.24 = (f32[128]{0:T(128)S(1)}, f32[128]{0:T(128)}, u32[]{:S(2)}) copy-start(f32[128]{0:T(128)} %param.15) | copy-start | bytes 1540
  230.6 32.0 %copy-start.2 = (f32[128,4096]{1,0:T(8,128)S(1)}, f32[128,4096]{1,0:T(8,128)}, u32[]{:S(2)}) copy-start(f32[128,4096]{1,0:T(8,128)} %copy-done.1) | copy-start | bytes 6291460
  236.7 1.3 copy-start.9
  250.4 12.2 %all-to-all-start.15 = ((f32[16,8,512]{2,1,0:T(8,128)}), f32[16,8,512]{2,1,0:T(8,128)S(1)}, u32[]{:S(2)}, u32[]{:S(2)}) async-start(f32[16,8,512]{2,1,0:T(8,128)} %broadcast_in_dim.35), calls=%async_computation.15 | async-start | bytes 524288 | tf_op jit(solution)/shard_map/all_to_all | solution.py:148
  262.6 1.6 copy-start.10
  269.5 27.0 %copy-start.4 = (f32[128,4096]{1,0:T(8,128)S(1)}, f32[128,4096]{1,0:T(8,128)}, u32[]{:S(2)}) copy-start(f32[128,4096]{1,0:T(8,128)} %mult_ref.3) | copy-start | bytes 6291460
  269.5 2.1 collective-permute-start
  269.5 1.7 copy-start.5
  282.8 10.9 %all-to-all-start.17 = ((f32[16,1,128]{2,1,0:T(1,128)}), f32[16,1,128]{2,1,0:T(1,128)S(1)}, u32[]{:S(2)}, u32[]{:S(2)}) async-start(f32[16,1,128]{2,1,0:T(1,128)} %broadcast_in_dim.40), calls=%async_computation.17 | async-start | bytes 16384 | tf_op jit(solution)/shard_map/all_to_all | solution.py:148
  296.5 1.6 copy-start.6

commit v2 on v1

v2 whole, which is shorter than its diff:
```python
import jax
import jax.numpy as jnp
from jax import lax
from jax.experimental import pallas as pl
from jax.experimental.pallas import tpu as pltpu
from jax.sharding import Mesh
from jax.sharding import PartitionSpec as P

V = 65536
BLK = 128
STEPS = 8
SCEN = ("x", "core")
VAR = ("z", "y")
CHUNK = 512
LANES = 128

penalty = 1.0
recourse_scale = 4.0
stride = 0.2
epsilon = 1e-06

WHOLE = pl.BlockSpec(memory_space=pltpu.VMEM)
FAR = pl.BlockSpec(memory_space=pltpu.HBM)
ROOM = 51 << 20


def local_call(body, outs, args, flops=0, far_in=(), far_out=(), scratch=(), aliases=None):
    outs = [s if isinstance(s, jax.ShapeDtypeStruct) else jax.ShapeDtypeStruct(s, jnp.float32) for s in outs]
    moved = sum(a.size * a.dtype.itemsize for a in args) + sum(o.size * o.dtype.itemsize for o in outs)
    return pl.pallas_call(
        body,
        out_shape=outs,
        in_specs=[FAR if k in far_in else WHOLE for k in range(len(args))],
        out_specs=[FAR if k in far_out else WHOLE for k in range(len(outs))],
        scratch_shapes=list(scratch),
        input_output_aliases=aliases or {},
        compiler_params=pltpu.CompilerParams(vmem_limit_bytes=ROOM),
        cost_estimate=pl.CostEstimate(flops=flops, bytes_accessed=moved, transcendentals=0),
    )(*args)


def landing(array):
    rows, width = array.shape
    chunks = width // CHUNK
    return [pltpu.VMEM((chunks, rows, CHUNK), array.dtype), pltpu.SemaphoreType.DMA((chunks,))]


def cols_of(k):
    return slice(k * CHUNK, (k + 1) * CHUNK)


def fetch(*triples):
    chunks = triples[0][1].shape[0]
    copies = []
    for k in range(chunks):
        row = [
            pltpu.make_async_copy(far.at[pl.ds(0, near.shape[1]), cols_of(k)], near.at[k], sems.at[k])
            for far, near, sems in triples
        ]
        for copy in row:
            copy.start()
        copies.append(row)
    return copies


def image_of(x, tech):
    return lax.dot_general(
        x.astype(jnp.bfloat16), tech, (((1,), (1,)), ((), ())), preferred_element_type=jnp.float32
    )


def first_image(start_far, tech_far, x_ref, image_ref, start_near, start_sem, tech_near, tech_sem):
    copies = fetch((tech_far, tech_near, tech_sem), (start_far, start_near, start_sem))
    total = None
    for k, row in enumerate(copies):
        for copy in row:
            copy.wait()
        x = start_near[k]
        x_ref[:, cols_of(k)] = x
        part = image_of(x, tech_near[k])
        total = part if total is None else total + part
    image_ref[...] = total


def linear_terms(
    mult_far, cost_far, curv_far, old_ref, linear_far, curv_out,
    mult_near, mult_sem, cost_near, cost_sem, curv_near, curv_sem, out_near, out_sem, curv_out_sem,
):
    rows = curv_far.shape[0]
    copies = fetch((mult_far, mult_near, mult_sem), (cost_far, cost_near, cost_sem), (curv_far, curv_near, curv_sem))
    outs = []
    for k, row in enumerate(copies):
        for copy in row:
            copy.wait()
        out_near[k] = cost_near[k].astype(jnp.float32) + mult_near[k] - penalty * old_ref[:, cols_of(k)]
        for near, far, sems in ((out_near, linear_far, out_sem), (curv_near, curv_out, curv_out_sem)):
            out = pltpu.make_async_copy(near.at[k], far.at[pl.ds(0, rows), cols_of(k)], sems.at[k])
            out.start()
            outs.append(out)
    for out in outs:
        out.wait()


def moved(k, shortfall, tech, x_ref, linear, curv, gain_ref):
    pullback = jnp.dot(shortfall, tech, preferred_element_type=jnp.float32)
    x = x_ref[:, cols_of(k)]
    slope = curv.astype(jnp.float32) * x + x + linear + pullback
    pieces = []
    for b in range(CHUNK // BLK):
        block = k * (CHUNK // BLK) + b
        cols = slice(b * BLK, (b + 1) * BLK)
        gain = jnp.broadcast_to(gain_ref[:, block : block + 1], (x_ref.shape[0], BLK))
        pieces.append(jnp.clip(x[:, cols] - gain * slope[:, cols], -1.0, 1.0))
    return jnp.concatenate(pieces, axis=1)


def scaled_shortfall(image_ref, rhs_ref):
    return (image_ref[...] - rhs_ref[...]).astype(jnp.bfloat16) * jnp.bfloat16(recourse_scale)


def step(
    image_ref, rhs_ref, x_ref, gain_ref, tech_far, linear_far, curv_far, new_ref, out_ref,
    tech_near, tech_sem, linear_near, linear_sem, curv_near, curv_sem,
):
    copies = fetch(
        (tech_far, tech_near, tech_sem), (curv_far, curv_near, curv_sem), (linear_far, linear_near, linear_sem)
    )
    shortfall = scaled_shortfall(image_ref, rhs_ref)
    total = None
    for k, row in enumerate(copies):
        for copy in row:
            copy.wait()
        tech = tech_near[k]
        new = moved(k, shortfall, tech, x_ref, linear_near[k], curv_near[k], gain_ref)
        new_ref[:, cols_of(k)] = new
        part = image_of(new, tech)
        total = part if total is None else total + part
    out_ref[...] = total


def last_step(
    image_ref, rhs_ref, x_ref, gain_ref, weight_ref, tech_far, linear_far, curv_far, new_ref, row_ref,
    tech_near, tech_sem, linear_near, linear_sem, curv_near, curv_sem,
):
    copies = fetch(
        (tech_far, tech_near, tech_sem), (curv_far, curv_near, curv_sem), (linear_far, linear_near, linear_sem)
    )
    shortfall = scaled_shortfall(image_ref, rhs_ref)
    rows, width = x_ref.shape
    weight = jnp.broadcast_to(weight_ref[...], (rows, LANES))
    row_ref[:, width:] = jnp.sum(weight, axis=0, keepdims=True)
    for k, row in enumerate(copies):
        for copy in row:
            copy.wait()
        new = moved(k, shortfall, tech_near[k], x_ref, linear_near[k], curv_near[k], gain_ref)
        new_ref[:, cols_of(k)] = new
        for b in range(CHUNK // LANES):
            part = weight * new[:, b * LANES : (b + 1) * LANES]
            start = k * CHUNK + b * LANES
            row_ref[:, start : start + LANES] = jnp.sum(part, axis=0, keepdims=True)


def own_spread(x_ref, row_ref, weight_ref, out_far, out_ref, sem):
    copy = pltpu.make_async_copy(x_ref, out_far, sem)
    copy.start()
    rows, width = x_ref.shape
    weight = jnp.broadcast_to(weight_ref[...], (rows, LANES))
    mass = row_ref[:, width:]
    total = jnp.zeros((rows, LANES), jnp.float32)
    for start in range(0, width, LANES):
        away = x_ref[:, start : start + LANES] - row_ref[:, start : start + LANES] / mass
        total = total + weight * away * away
    out_ref[...] = jnp.sum(total, axis=0, keepdims=True)
    copy.wait()


def node_row(own_ref, other_ref, old_ref, spread_ref, leads_ref, out_ref):
    width = old_ref.shape[1]
    own_mass, other_mass = own_ref[:, width:], other_ref[:, width:]
    mass = own_mass + other_mass
    apart = jnp.zeros((1, LANES), jnp.float32)
    drift = jnp.zeros((1, LANES), jnp.float32)
    for start in range(0, width, LANES):
        cols = slice(start, start + LANES)
        own, other = own_ref[:, cols], other_ref[:, cols]
        mean = (own + other) / mass
        out_ref[:, cols] = mean
        gap = own / own_mass - other / other_mass
        apart = apart + gap * gap
        drift = drift + (mean - old_ref[:, cols]) ** 2
    leads = leads_ref[...]
    spread = spread_ref[...] + leads * (own_mass * other_mass / mass) * apart
    drift = leads * mass * drift
    lane = lax.broadcasted_iota(jnp.int32, (1, LANES), 1)
    spread = jnp.sum(spread, axis=1, keepdims=True)
    drift = jnp.sum(drift, axis=1, keepdims=True)
    out_ref[:, width:] = jnp.where(lane == 0, spread, jnp.where(lane == 1, drift, own_mass))


def new_duals(x_ref, mean_ref, factor_ref, mult_far, out_far, mult_near, mult_sem, out_near, out_sem):
    copies = fetch((mult_far, mult_near, mult_sem))
    factor = factor_ref[:, 0:1]
    outs = []
    for k, row in enumerate(copies):
        for copy in row:
            copy.wait()
        out_near[k] = mult_near[k] + factor * (x_ref[:, cols_of(k)] - mean_ref[:, cols_of(k)])
        out = pltpu.make_async_copy(out_near.at[k], out_far.at[:, cols_of(k)], out_sem.at[k])
        out.start()
        outs.append(out)
    for out in outs:
        out.wait()


def to_all(x, axes):
    devices = lax.axis_size(axes)
    return lax.all_to_all(jnp.broadcast_to(x[None], (devices, *x.shape)), axes, 0, 0, tiled=True)


def total_of(partial, axes):
    devices = lax.axis_size(axes)
    rows, width = partial.shape
    pieces = partial.reshape(devices, rows // devices, width)
    arrived = lax.all_to_all(pieces, axes, 0, 0, tiled=True)
    return to_all(jnp.sum(arrived, axis=0), axes).reshape(rows, width)


def shards(
    start_point,
    multipliers,
    cost,
    curvature,
    recourse_rhs,
    technology,
    scenario_weight,
    previous_mean,
    active,
):
    rows, width = start_point.shape
    images = recourse_rhs.shape[1]
    groups = previous_mean.shape[0]
    group_size = lax.axis_size(SCEN) // groups
    position = lax.axis_index(SCEN)
    old_row = lax.dynamic_slice_in_dim(previous_mean, position // group_size, 1, 0)
    weight = scenario_weight[:, None]
    leads = jnp.full((1, LANES), (position % group_size == 0).astype(jnp.float32))
    gain = stride * active.astype(jnp.float32)
    product = 2 * rows * width * images

    iterate, partial = local_call(
        first_image,
        [(rows, width), (rows, images)],
        [start_point, technology],
        product,
        far_in=(0, 1),
        scratch=landing(start_point) + landing(technology),
    )
    linear, curvature_far = local_call(
        linear_terms,
        [(2 * rows, width), jax.ShapeDtypeStruct((4 * rows, width), curvature.dtype)],
        [multipliers, cost, curvature, old_row],
        2 * rows * width,
        far_in=(0, 1, 2),
        far_out=(0, 1),
        scratch=landing(multipliers) + 2 * landing(cost) + landing(multipliers) + landing(cost)[1:],
    )
    far = [technology, linear, curvature_far]
    near = landing(technology) + landing(multipliers) + landing(curvature)
    for sweep in range(STEPS):
        image = total_of(partial, VAR)
        operands = [image, recourse_rhs, iterate, gain]
        if sweep < STEPS - 1:
            iterate, partial = local_call(
                step,
                [(rows, width), (rows, images)],
                operands + far,
                2 * product,
                far_in=(4, 5, 6),
                scratch=near,
                aliases={2: 0},
            )
        else:
            iterate, own_row = local_call(
                last_step,
                [(rows, width), (1, width + LANES)],
                operands + [weight] + far,
                product,
                far_in=(5, 6, 7),
                scratch=near,
                aliases={2: 0},
            )
    other_row = lax.ppermute(own_row, "core", [(0, 1), (1, 0)])
    final, spread = local_call(
        own_spread,
        [(rows, width), (1, LANES)],
        [iterate, own_row, weight],
        4 * rows * width,
        far_out=(0,),
        scratch=[pltpu.SemaphoreType.DMA],
    )
    (row,) = local_call(node_row, [(1, width + LANES)], [own_row, other_row, old_row, spread, leads])
    everyone = to_all(row, SCEN)
    bundle_mean = everyone[::group_size, 0, :width]
    parts = jnp.sum(everyone[:, :, width:], axis=0)
    sums = jnp.sum(to_all(parts, VAR), axis=0)
    normaliser = sums[0, 2] / lax.axis_size(VAR) * V
    primal_norm = jnp.sqrt(sums[0, 0] / normaliser + epsilon)
    dual_norm = penalty * jnp.sqrt(sums[0, 1] / normaliser + epsilon)
    factor = penalty * jnp.sqrt(primal_norm / dual_norm)
    (new_multipliers,) = local_call(
        new_duals,
        [(rows, width)],
        [iterate, row[:, :width], jnp.full((1, LANES), factor), multipliers],
        3 * rows * width,
        far_in=(3,),
        far_out=(0,),
        scratch=landing(multipliers) + landing(multipliers),
    )
    return (final, new_multipliers, bundle_mean, primal_norm, dual_norm)


def solution(mesh):
    torus = Mesh(mesh.devices.reshape(4, 2, 4, 4), ("x", "core", "z", "y"))
    return jax.shard_map(
        shards,
        mesh=torus,
        in_specs=(
            P(SCEN, VAR),
            P(SCEN, VAR),
            P(SCEN, VAR),
            P(SCEN, VAR),
            P(SCEN, None),
            P(None, VAR),
            P(SCEN),
            P(None, VAR),
            P(SCEN, VAR),
        ),
        out_specs=(P(SCEN, VAR), P(SCEN, VAR), P(None, VAR), P(), P()),
        check_vma=False,
    )
```

time: 303 us -> 270 us (0.89)
  local copies, waits for them, and re-layouts: 30 us -> 5.72 us
  Pallas kernels: 57.8 us -> 47.6 us
    unnamed x52 -> x12, local copies, waits for them, and re-layouts: 27 us -> 2.73 us
    pallas_call x13, Pallas kernels: 57.8 us -> 47.6 us  [local_call(): pl.pallas_call(body, out_shape=outs, in_specs=[FAR if k in far_in else WH...]
  transfers between devices with their start and end apart: 5 -> 5, of which waited for: 4 -> 4; matrix products, arithmetic and copies ran while one was open for 0% -> 1% of each run, Pallas kernels for 1% -> 2%
where the time goes in v2:
time: 270 us; the launch traced here: 268 us
  blocking collectives  162 us (60%)
  Pallas kernels  47.6 us (18%)
  waiting for transfers between devices  27.3 us (10%)
  starting transfers between devices  19.8 us (7%)
  local copies, waits for them, and re-layouts  5.72 us (2%)
  between operations  5.38 us (2%)
    all_to_all x7, blocking collectives, total_of(): arrived = lax.all_to_all(pieces, axes, 0, 0, tiled=True)  81.8 us
    all_to_all x7, blocking collectives, to_all(): lax.all_to_all(jnp.broadcast_to(x[None], (devices, *x.shape)), axes, 0, 0...  80.6 us
    pallas_call x13, Pallas kernels, local_call(): pl.pallas_call(body, out_shape=outs, in_specs=[FAR if k in far_in else WH...  47.6 us
    all_to_all x3, waiting for transfers between devices, to_all(): lax.all_to_all(jnp.broadcast_to(x[None], (devices, *x.shape)), axes, 0, 0...  18.6 us
    all_to_all x3, starting transfers between devices, to_all(): lax.all_to_all(jnp.broadcast_to(x[None], (devices, *x.shape)), axes, 0, 0...  11.4 us
    all_to_all x1, waiting for transfers between devices, total_of(): arrived = lax.all_to_all(pieces, axes, 0, 0, tiled=True)  8.67 us
    all_to_all x1, starting transfers between devices, total_of(): arrived = lax.all_to_all(pieces, axes, 0, 0, tiled=True)  8.28 us
  transfers between devices with their start and end apart: 5, of which 4 were waited for; matrix products, arithmetic and copies ran while one was open for 1% of the time, Pallas kernels for 2%

profile of v2, /device:TPU:0, one launch (start us, length us, event | category | flops | bytes accessed | tf_op | source)
XLA Modules:
  0.0 268.4 jit_solution(5664604325839128063)
XLA Ops:
  0.6 0.0 copy-start
  0.6 4.0 %shard_map.128 = (f32[128,4096]{1,0:T(8,128)S(1)}, f32[128,512]{1,0:T(8,128)}) custom-call(f32[128,4096]{1,0:T(8,128)} %start_far.1, bf16[512,4096]{1,0:T(8,128)(2,1)} %tech_far.17), custom_call_target="tpu_custom_call" | custom-call | flops 536870912 | bytes 8650752 | tf_op jit(solution)/shard_map/pallas_call | solution.py:30
  4.6 0.0 copy-start.2
  4.6 8.3 %all-to-all-start = ((f32[16,8,512]{2,1,0:T(8,128)}), f32[16,8,512]{2,1,0:T(8,128)S(1)}, u32[]{:S(2)}, u32[]{:S(2)}) async-start(f32[16,8,512]{2,1,0:T(8,128)} %bitcast), calls=%async_computation | async-start | bytes 524288 | tf_op jit(solution)/shard_map/all_to_all | solution.py:224
  12.9 8.7 %all-to-all-done = f32[16,8,512]{2,1,0:T(8,128)S(1)} async-done(((f32[16,8,512]{2,1,0:T(8,128)}), f32[16,8,512]{2,1,0:T(8,128)S(1)}, u32[]{:S(2)}, u32[]{:S(2)}) %all-to-all-start) | async-done | bytes 262176 | tf_op jit(solution)/shard_map/all_to_all | solution.py:224
  21.6 0.7 broadcast_in_dim.28
  22.4 4.2 %all-to-all-start.1 = ((f32[16,8,512]{2,1,0:T(8,128)}), f32[16,8,512]{2,1,0:T(8,128)}, u32[]{:S(2)}, u32[]{:S(2)}) async-start(f32[16,8,512]{2,1,0:T(8,128)} %broadcast_in_dim.28), calls=%async_computation.1 | async-start | bytes 524288 | tf_op jit(solution)/shard_map/all_to_all | solution.py:217
  26.6 0.0 copy-done
  26.6 0.8 copy.31
  27.4 0.0 copy-done.2
  27.4 0.0 copy-start.3
  27.4 1.2 copy-done.3
  28.7 0.0 copy-start.1
  28.7 3.0 %shard_map.129 = (f32[256,4096]{1,0:T(8,128)}, bf16[512,4096]{1,0:T(8,128)(2,1)}) custom-call(f32[128,4096]{1,0:T(8,128)} %mult_far.3, bf16[128,4096]{1,0:T(8,128)(2,1)S(1)} %copy-done.2, bf16[128,4096]{1,0:T(8,128)(2,1)S(1)} %copy-done.3, f32[1,4096]{1,0:T(1,128)S(1)} %constant_dynamic-slice_fusion.old_ref), custom_call_target="tpu_custom_call" | custom-call | flops 1048576 | bytes 12599296 | tf_op jit(solution)/shard_map/pallas_call | solution.py:30
  31.7 3.6 %all-to-all-done.1 = f32[16,8,512]{2,1,0:T(8,128)} async-done(((f32[16,8,512]{2,1,0:T(8,128)}), f32[16,8,512]{2,1,0:T(8,128)}, u32[]{:S(2)}, u32[]{:S(2)}) %all-to-all-start.1) | async-done | bytes 262176 | tf_op jit(solution)/shard_map/all_to_all | solution.py:217
  35.3 0.0 copy-done.1
  35.3 5.5 %shard_map.130 = (f32[128,4096]{1,0:T(8,128)S(1)}, f32[128,512]{1,0:T(8,128)S(1)}) custom-call(f32[128,512]{1,0:T(8,128)} %bitcast.1.image_ref, f32[128,512]{1,0:T(8,128)S(1)} %copy-done.1, f32[128,4096]{1,0:T(8,128)S(1)} %get-tuple-element.28.x_ref, f32[128,32]{1,0:T(8,128)S(1)} %convert_multiply_fusion.gain_ref, ...), custom_call_target="tpu_custom_call", output_to_operand_aliasing={{0}: (2, {})} | custom-call | flops 1073741824 | bytes 17580032 | tf_op jit(solution)/shard_map/pallas_call | solution.py:30
  40.8 12.0 %all_to_all.90 = f32[16,8,512]{2,1,0:T(8,128)S(1)} all-to-all(f32[16,8,512]{2,1,0:T(8,128)S(1)} %bitcast.31), channel_id=1, replica_groups=mesh['x'=4,'core'=2,'z'=4,'y'=4] {'z','y'}, dimensions={0} | all-to-all | bytes 524288 | tf_op jit(solution)/shard_map/all_to_all | solution.py:224
  52.9 11.6 %all_to_all.91 = f32[16,8,512]{2,1,0:T(8,128)S(1)} all-to-all(f32[16,8,512]{2,1,0:T(8,128)S(1)} %broadcast_in_dim.29), channel_id=1, replica_groups=mesh['x'=4,'core'=2,'z'=4,'y'=4] {'z','y'}, dimensions={0} | all-to-all | bytes 524288 | tf_op jit(solution)/shard_map/all_to_all | solution.py:217
  64.5 4.5 %shard_map.131 = (f32[128,4096]{1,0:T(8,128)S(1)}, f32[128,512]{1,0:T(8,128)S(1)}) custom-call(f32[128,512]{1,0:T(8,128)S(1)} %bitcast.25, f32[128,512]{1,0:T(8,128)S(1)} %copy-done.1, f32[128,4096]{1,0:T(8,128)S(1)} %get-tuple-element.32.x_ref, f32[128,32]{1,0:T(8,128)S(1)} %convert_multiply_fusion.gain_ref, ...), custom_call_target="tpu_custom_call", output_to_operand_aliasing={{0}: (2, {})} | custom-call | flops 1073741824 | bytes 17580032 | tf_op jit(solution)/shard_map/pallas_call | solution.py:30
  69.0 11.6 %all_to_all.92 = f32[16,8,512]{2,1,0:T(8,128)S(1)} all-to-all(f32[16,8,512]{2,1,0:T(8,128)S(1)} %bitcast.32), channel_id=1, replica_groups=mesh['x'=4,'core'=2,'z'=4,'y'=4] {'z','y'}, dimensions={0} | all-to-all | bytes 524288 | tf_op jit(solution)/shard_map/all_to_all | solution.py:224
  80.6 11.6 %all_to_all.93 = f32[16,8,512]{2,1,0:T(8,128)S(1)} all-to-all(f32[16,8,512]{2,1,0:T(8,128)S(1)} %broadcast_in_dim.30), channel_id=1, replica_groups=mesh['x'=4,'core'=2,'z'=4,'y'=4] {'z','y'}, dimensions={0} | all-to-all | bytes 524288 | tf_op jit(solution)/shard_map/all_to_all | solution.py:217
  92.2 4.5 %shard_map.132 = (f32[128,4096]{1,0:T(8,128)S(1)}, f32[128,512]{1,0:T(8,128)S(1)}) custom-call(f32[128,512]{1,0:T(8,128)S(1)} %bitcast.26, f32[128,512]{1,0:T(8,128)S(1)} %copy-done.1, f32[128,4096]{1,0:T(8,128)S(1)} %get-tuple-element.34.x_ref, f32[128,32]{1,0:T(8,128)S(1)} %convert_multiply_fusion.gain_ref, ...), custom_call_target="tpu_custom_call", output_to_operand_aliasing={{0}: (2, {})} | custom-call | flops 1073741824 | bytes 17580032 | tf_op jit(solution)/shard_map/pallas_call | solution.py:30
  96.8 11.7 %all_to_all.94 = f32[16,8,512]{2,1,0:T(8,128)S(1)} all-to-all(f32[16,8,512]{2,1,0:T(8,128)S(1)} %bitcast.33), channel_id=1, replica_groups=mesh['x'=4,'core'=2,'z'=4,'y'=4] {'z','y'}, dimensions={0} | all-to-all | bytes 524288 | tf_op jit(solution)/shard_map/all_to_all | solution.py:224
  108.5 11.5 %all_to_all.95 = f32[16,8,512]{2,1,0:T(8,128)S(1)} all-to-all(f32[16,8,512]{2,1,0:T(8,128)S(1)} %broadcast_in_dim.31), channel_id=1, replica_groups=mesh['x'=4,'core'=2,'z'=4,'y'=4] {'z','y'}, dimensions={0} | all-to-all | bytes 524288 | tf_op jit(solution)/shard_map/all_to_all | solution.py:217
  120.0 4.6 %shard_map.133 = (f32[128,4096]{1,0:T(8,128)S(1)}, f32[128,512]{1,0:T(8,128)S(1)}) custom-call(f32[128,512]{1,0:T(8,128)S(1)} %bitcast.27, f32[128,512]{1,0:T(8,128)S(1)} %copy-done.1, f32[128,4096]{1,0:T(8,128)S(1)} %get-tuple-element.36.x_ref, f32[128,32]{1,0:T(8,128)S(1)} %convert_multiply_fusion.gain_ref, ...), custom_call_target="tpu_custom_call", output_to_operand_aliasing={{0}: (2, {})} | custom-call | flops 1073741824 | bytes 17580032 | tf_op jit(solution)/shard_map/pallas_call | solution.py:30
  124.6 11.8 %all_to_all.96 = f32[16,8,512]{2,1,0:T(8,128)S(1)} all-to-all(f32[16,8,512]{2,1,0:T(8,128)S(1)} %bitcast.34), channel_id=1, replica_groups=mesh['x'=4,'core'=2,'z'=4,'y'=4] {'z','y'}, dimensions={0} | all-to-all | bytes 524288 | tf_op jit(solution)/shard_map/all_to_all | solution.py:224
  136.4 11.7 %all_to_all.97 = f32[16,8,512]{2,1,0:T(8,128)S(1)} all-to-all(f32[16,8,512]{2,1,0:T(8,128)S(1)} %broadcast_in_dim.32), channel_id=1, replica_groups=mesh['x'=4,'core'=2,'z'=4,'y'=4] {'z','y'}, dimensions={0} | all-to-all | bytes 524288 | tf_op jit(solution)/shard_map/all_to_all | solution.py:217
  148.1 4.5 %shard_map.134 = (f32[128,4096]{1,0:T(8,128)S(1)}, f32[128,512]{1,0:T(8,128)S(1)}) custom-call(f32[128,512]{1,0:T(8,128)S(1)} %bitcast.28, f32[128,512]{1,0:T(8,128)S(1)} %copy-done.1, f32[128,4096]{1,0:T(8,128)S(1)} %get-tuple-element.38.x_ref, f32[128,32]{1,0:T(8,128)S(1)} %convert_multiply_fusion.gain_ref, ...), custom_call_target="tpu_custom_call", output_to_operand_aliasing={{0}: (2, {})} | custom-call | flops 1073741824 | bytes 17580032 | tf_op jit(solution)/shard_map/pallas_call | solution.py:30
  152.7 11.5 %all_to_all.98 = f32[16,8,512]{2,1,0:T(8,128)S(1)} all-to-all(f32[16,8,512]{2,1,0:T(8,128)S(1)} %bitcast.35), channel_id=1, replica_groups=mesh['x'=4,'core'=2,'z'=4,'y'=4] {'z','y'}, dimensions={0} | all-to-all | bytes 524288 | tf_op jit(solution)/shard_map/all_to_all | solution.py:224
  164.2 12.3 %all_to_all.99 = f32[16,8,512]{2,1,0:T(8,128)S(1)} all-to-all(f32[16,8,512]{2,1,0:T(8,128)S(1)} %broadcast_in_dim.33), channel_id=1, replica_groups=mesh['x'=4,'core'=2,'z'=4,'y'=4] {'z','y'}, dimensions={0} | all-to-all | bytes 524288 | tf_op jit(solution)/shard_map/all_to_all | solution.py:217
  176.5 4.5 %shard_map.135 = (f32[128,4096]{1,0:T(8,128)S(1)}, f32[128,512]{1,0:T(8,128)S(1)}) custom-call(f32[128,512]{1,0:T(8,128)S(1)} %bitcast.29, f32[128,512]{1,0:T(8,128)S(1)} %copy-done.1, f32[128,4096]{1,0:T(8,128)S(1)} %get-tuple-element.40.x_ref, f32[128,32]{1,0:T(8,128)S(1)} %convert_multiply_fusion.gain_ref, ...), custom_call_target="tpu_custom_call", output_to_operand_aliasing={{0}: (2, {})} | custom-call | flops 1073741824 | bytes 17580032 | tf_op jit(solution)/shard_map/pallas_call | solution.py:30
  181.0 11.6 %all_to_all.100 = f32[16,8,512]{2,1,0:T(8,128)S(1)} all-to-all(f32[16,8,512]{2,1,0:T(8,128)S(1)} %bitcast.36), channel_id=1, replica_groups=mesh['x'=4,'core'=2,'z'=4,'y'=4] {'z','y'}, dimensions={0} | all-to-all | bytes 524288 | tf_op jit(solution)/shard_map/all_to_all | solution.py:224
  192.7 11.6 %all_to_all.101 = f32[16,8,512]{2,1,0:T(8,128)S(1)} all-to-all(f32[16,8,512]{2,1,0:T(8,128)S(1)} %broadcast_in_dim.34), channel_id=1, replica_groups=mesh['x'=4,'core'=2,'z'=4,'y'=4] {'z','y'}, dimensions={0} | all-to-all | bytes 524288 | tf_op jit(solution)/shard_map/all_to_all | solution.py:217
  204.3 0.0 copy-start.4
  204.3 4.6 %shard_map.136 = (f32[128,4096]{1,0:T(8,128)S(1)}, f32[128,512]{1,0:T(8,128)S(1)}) custom-call(f32[128,512]{1,0:T(8,128)S(1)} %bitcast.30, f32[128,512]{1,0:T(8,128)S(1)} %copy-done.1, f32[128,4096]{1,0:T(8,128)S(1)} %get-tuple-element.42.x_ref, f32[128,32]{1,0:T(8,128)S(1)} %convert_multiply_fusion.gain_ref, ...), custom_call_target="tpu_custom_call", output_to_operand_aliasing={{0}: (2, {})} | custom-call | flops 1073741824 | bytes 17580032 | tf_op jit(solution)/shard_map/pallas_call | solution.py:30
  208.8 11.6 %all_to_all.102 = f32[16,8,512]{2,1,0:T(8,128)S(1)} all-to-all(f32[16,8,512]{2,1,0:T(8,128)S(1)} %bitcast.37), channel_id=1, replica_groups=mesh['x'=4,'core'=2,'z'=4,'y'=4] {'z','y'}, dimensions={0} | all-to-all | bytes 524288 | tf_op jit(solution)/shard_map/all_to_all | solution.py:224
  220.5 0.7 broadcast_in_dim.35
  221.2 3.8 %all-to-all-start.15 = ((f32[16,8,512]{2,1,0:T(8,128)}), f32[16,8,512]{2,1,0:T(8,128)S(1)}, u32[]{:S(2)}, u32[]{:S(2)}) async-start(f32[16,8,512]{2,1,0:T(8,128)} %broadcast_in_dim.35), calls=%async_computation.15 | async-start | bytes 524288 | tf_op jit(solution)/shard_map/all_to_all | solution.py:217
  225.0 0.0 copy-done.4
  225.0 0.1 copy.32.weight_ref
  225.1 8.3 %all-to-all-done.15 = f32[16,8,512]{2,1,0:T(8,128)S(1)} async-done(((f32[16,8,512]{2,1,0:T(8,128)}), f32[16,8,512]{2,1,0:T(8,128)S(1)}, u32[]{:S(2)}, u32[]{:S(2)}) %all-to-all-start.15) | async-done | bytes 262176 | tf_op jit(solution)/shard_map/all_to_all | solution.py:217
  233.4 3.8 %shard_map.137 = (f32[128,4096]{1,0:T(8,128)S(1)}, f32[1,4224]{1,0:T(1,128)S(1)}) custom-call(f32[128,512]{1,0:T(8,128)S(1)} %bitcast.24, f32[128,512]{1,0:T(8,128)S(1)} %copy-done.1, f32[128,4096]{1,0:T(8,128)S(1)} %get-tuple-element.44.x_ref, f32[128,32]{1,0:T(8,128)S(1)} %convert_multiply_fusion.gain_ref, ...), custom_call_target="tpu_custom_call", output_to_operand_aliasing={{0}: (2, {})} | custom-call | flops 536870912 | bytes 17335296 | tf_op jit(solution)/shard_map/pallas_call | solution.py:30
  237.2 0.1 collective-permute-start
  237.3 1.3 shard_map.138
  238.7 0.0 collective-permute-done.other_ref
  238.7 0.1 shard_map.139
  238.9 0.1 broadcast_in_dim.39
  239.0 10.4 %all_to_all.103 = f32[8,1,4224]{2,1,0:T(1,128)S(1)} all-to-all(f32[8,1,4224]{2,1,0:T(1,128)S(1)} %broadcast_in_dim.39), channel_id=1, replica_groups=mesh['x'=4,'core'=2,'z'=4,'y'=4] {'x','core'}, dimensions={0} | all-to-all | bytes 270336 | tf_op jit(solution)/shard_map/all_to_all | solution.py:217
  249.4 0.6 broadcast_in_dim.40
  250.0 3.5 %all-to-all-start.17 = ((f32[16,1,128]{2,1,0:T(1,128)}), f32[16,1,128]{2,1,0:T(1,128)S(1)}, u32[]{:S(2)}, u32[]{:S(2)}) async-start(f32[16,1,128]{2,1,0:T(1,128)} %broadcast_in_dim.40), calls=%async_computation.17 | async-start | bytes 16384 | tf_op jit(solution)/shard_map/all_to_all | solution.py:217
  253.5 0.7 copy.37
  254.2 6.7 %all-to-all-done.17 = f32[16,1,128]{2,1,0:T(1,128)S(1)} async-done(((f32[16,1,128]{2,1,0:T(1,128)}), f32[16,1,128]{2,1,0:T(1,128)S(1)}, u32[]{:S(2)}, u32[]{:S(2)}) %all-to-all-start.17) | async-done | bytes 8224 | tf_op jit(solution)/shard_map/all_to_all | solution.py:217
  260.9 0.6 fusion
  263.7 2.5 shard_map.140
  (23 shorter events, 0.4 us)
Async XLA Ops:
  0.6 25.9 %copy-start = (f32[4,4096]{1,0:T(4,128)S(1)}, f32[4,4096]{1,0:T(4,128)}, u32[]{:S(2)}) copy-start(f32[4,4096]{1,0:T(4,128)} %param.16) | copy-start | bytes 196612
  4.6 22.8 %copy-start.2 = (bf16[128,4096]{1,0:T(8,128)(2,1)S(1)}, bf16[128,4096]{1,0:T(8,128)(2,1)}, u32[]{:S(2)}) copy-start(bf16[128,4096]{1,0:T(8,128)(2,1)} %cost_far.1) | copy-start | bytes 3145732
  4.6 17.0 %all-to-all-start = ((f32[16,8,512]{2,1,0:T(8,128)}), f32[16,8,512]{2,1,0:T(8,128)S(1)}, u32[]{:S(2)}, u32[]{:S(2)}) async-start(f32[16,8,512]{2,1,0:T(8,128)} %bitcast), calls=%async_computation | async-start | bytes 524288 | tf_op jit(solution)/shard_map/all_to_all | solution.py:224
  22.4 12.9 %all-to-all-start.1 = ((f32[16,8,512]{2,1,0:T(8,128)}), f32[16,8,512]{2,1,0:T(8,128)}, u32[]{:S(2)}, u32[]{:S(2)}) async-start(f32[16,8,512]{2,1,0:T(8,128)} %broadcast_in_dim.28), calls=%async_computation.1 | async-start | bytes 524288 | tf_op jit(solution)/shard_map/all_to_all | solution.py:217
  27.4 1.2 copy-start.3
  28.7 6.6 %copy-start.1 = (f32[128,512]{1,0:T(8,128)S(1)}, f32[128,512]{1,0:T(8,128)}, u32[]{:S(2)}) copy-start(f32[128,512]{1,0:T(8,128)} %rhs_ref.15) | copy-start | bytes 786436
  204.3 20.7 %copy-start.4 = (f32[128]{0:T(128)S(1)}, f32[128]{0:T(128)}, u32[]{:S(2)}) copy-start(f32[128]{0:T(128)} %param.15) | copy-start | bytes 1540
  221.2 12.2 %all-to-all-start.15 = ((f32[16,8,512]{2,1,0:T(8,128)}), f32[16,8,512]{2,1,0:T(8,128)S(1)}, u32[]{:S(2)}, u32[]{:S(2)}) async-start(f32[16,8,512]{2,1,0:T(8,128)} %broadcast_in_dim.35), calls=%async_computation.15 | async-start | bytes 524288 | tf_op jit(solution)/shard_map/all_to_all | solution.py:217
  237.2 1.4 collective-permute-start
  250.0 10.9 %all-to-all-start.17 = ((f32[16,1,128]{2,1,0:T(1,128)}), f32[16,1,128]{2,1,0:T(1,128)S(1)}, u32[]{:S(2)}, u32[]{:S(2)}) async-start(f32[16,1,128]{2,1,0:T(1,128)} %broadcast_in_dim.40), calls=%async_computation.17 | async-start | bytes 16384 | tf_op jit(solution)/shard_map/all_to_all | solution.py:217

commit v3 on v2

v3 whole, which is shorter than its diff:
```python
import jax
import jax.numpy as jnp
from jax import lax
from jax.experimental import pallas as pl
from jax.experimental.pallas import tpu as pltpu
from jax.sharding import Mesh
from jax.sharding import PartitionSpec as P

V = 65536
STEPS = 8
SCEN = ("x", "core")
VAR = ("z", "y")
LANES = 128
SPANS = ((0, 512), (512, 1024), (1536, 1024), (2560, 1024), (3584, 512))

penalty = 1.0
recourse_scale = 4.0
stride = 0.2
epsilon = 1e-06

WHOLE = pl.BlockSpec(memory_space=pltpu.VMEM)
FAR = pl.BlockSpec(memory_space=pltpu.HBM)
SMALL = pl.BlockSpec(memory_space=pltpu.SMEM)
ROOM = 51 << 20


def local_call(body, outs, args, flops=0, scalar_in=(), far_in=(), far_out=(), scratch=(), aliases=None):
    outs = [s if isinstance(s, jax.ShapeDtypeStruct) else jax.ShapeDtypeStruct(s, jnp.float32) for s in outs]
    moved = sum(a.size * a.dtype.itemsize for a in args) + sum(o.size * o.dtype.itemsize for o in outs)
    return pl.pallas_call(
        body,
        out_shape=outs,
        in_specs=[SMALL if k in scalar_in else FAR if k in far_in else WHOLE for k in range(len(args))],
        out_specs=[FAR if k in far_out else WHOLE for k in range(len(outs))],
        scratch_shapes=list(scratch),
        input_output_aliases=aliases or {},
        compiler_params=pltpu.CompilerParams(vmem_limit_bytes=ROOM),
        cost_estimate=pl.CostEstimate(flops=flops, bytes_accessed=moved, transcendentals=0),
    )(*args)


def landing(array):
    return [pltpu.VMEM(array.shape, array.dtype), pltpu.SemaphoreType.DMA((len(SPANS),))]


def cols_of(k):
    start, size = SPANS[k]
    return slice(start, start + size)


def spans(*triples):
    copies = []
    for k, span in enumerate(SPANS):
        cols = pl.ds(*span)
        row = [
            pltpu.make_async_copy(far.at[pl.ds(0, near.shape[0]), cols], near.at[:, cols], sems.at[k])
            for far, near, sems in triples
        ]
        for copy in row:
            copy.start()
        copies.append(row)
    for k, row in enumerate(copies):
        for copy in row:
            copy.wait()
        yield k, cols_of(k)


def image_of(x, tech):
    return lax.dot_general(
        x.astype(jnp.bfloat16), tech, (((1,), (1,)), ((), ())), preferred_element_type=jnp.float32
    )


def first_image(start_far, tech_far, x_ref, image_ref, start_near, start_sem, tech_near, tech_sem):
    total = None
    for _, cols in spans((tech_far, tech_near, tech_sem), (start_far, start_near, start_sem)):
        x = start_near[:, cols]
        x_ref[:, cols] = x
        part = image_of(x, tech_near[:, cols])
        total = part if total is None else total + part
    image_ref[...] = total


def per_lane_block(cols):
    return [(b, slice(b * LANES, (b + 1) * LANES)) for b in range(cols.start // LANES, cols.stop // LANES)]


def linear_terms(
    mult_far, cost_far, curv_far, old_ref, linear_far, curv_out,
    mult_near, mult_sem, cost_near, cost_sem, curv_near, curv_sem, out_near, out_sem, curv_out_sem,
):
    rows = curv_far.shape[0]
    outs = []
    for k, cols in spans((mult_far, mult_near, mult_sem), (cost_far, cost_near, cost_sem), (curv_far, curv_near, curv_sem)):
        for b, block in per_lane_block(cols):
            anchor = old_ref[b : b + 1, :]
            out_near[:, block] = cost_near[:, block].astype(jnp.float32) + mult_near[:, block] - penalty * anchor
        for near, far, sems in ((out_near, linear_far, out_sem), (curv_near, curv_out, curv_out_sem)):
            out = pltpu.make_async_copy(near.at[:, cols], far.at[pl.ds(0, rows), cols], sems.at[k])
            out.start()
            outs.append(out)
    for out in outs:
        out.wait()


def moved(cols, pullback, x_ref, linear, curv, gain_ref):
    pieces = []
    for b, block in per_lane_block(cols):
        here = slice(block.start - cols.start, block.stop - cols.start)
        x = x_ref[:, block]
        slope = curv[:, block].astype(jnp.float32) * x + x + linear[:, block] + pullback[:, here]
        gain = jnp.broadcast_to(gain_ref[:, b : b + 1], x.shape)
        pieces.append(jnp.clip(x - gain * slope, -1.0, 1.0))
    return jnp.concatenate(pieces, axis=1)


def each_span(arrivals, shortfall, tech_near, finish):
    for k, cols in arrivals:
        finish(k, cols, jnp.dot(shortfall, tech_near[:, cols], preferred_element_type=jnp.float32))


def scaled_shortfall(excess_ref):
    return excess_ref[...].astype(jnp.bfloat16) * jnp.bfloat16(recourse_scale)


def step(
    excess_ref, x_ref, gain_ref, tech_far, linear_far, curv_far, new_ref, out_ref,
    tech_near, tech_sem, linear_near, linear_sem, curv_near, curv_sem,
):
    parts = []

    def finish(k, cols, pullback):
        new = moved(cols, pullback, x_ref, linear_near, curv_near, gain_ref)
        new_ref[:, cols] = new
        part = image_of(new, tech_near[:, cols])
        parts[:] = [parts[0] + part if parts else part]

    each_span(
        spans((tech_far, tech_near, tech_sem), (curv_far, curv_near, curv_sem), (linear_far, linear_near, linear_sem)),
        scaled_shortfall(excess_ref),
        tech_near,
        finish,
    )
    out_ref[...] = parts[0]


def last_step(
    excess_ref, x_ref, gain_ref, weight_ref, tech_far, linear_far, curv_far, new_ref, final_far, row_ref,
    tech_near, tech_sem, linear_near, linear_sem, curv_near, curv_sem, out_sem,
):
    rows, width = x_ref.shape
    blocks = width // LANES
    weight = jnp.broadcast_to(weight_ref[...], (rows, LANES))
    mass = jnp.sum(weight, axis=0, keepdims=True)
    spreads = [jnp.zeros((rows, LANES), jnp.float32)]
    outs = []

    def finish(k, cols, pullback):
        new = moved(cols, pullback, x_ref, linear_near, curv_near, gain_ref)
        new_ref[:, cols] = new
        out = pltpu.make_async_copy(new_ref.at[:, cols], final_far.at[:, cols], out_sem.at[k])
        out.start()
        outs.append(out)
        for b, block in per_lane_block(cols):
            part = new[:, block.start - cols.start : block.stop - cols.start]
            row = jnp.sum(weight * part, axis=0, keepdims=True)
            row_ref[b : b + 1, :] = row
            away = part - row / mass
            spreads[0] = spreads[0] + weight * away * away

    each_span(
        spans((tech_far, tech_near, tech_sem), (curv_far, curv_near, curv_sem), (linear_far, linear_near, linear_sem)),
        scaled_shortfall(excess_ref),
        tech_near,
        finish,
    )
    row_ref[blocks : blocks + 1, :] = mass
    row_ref[blocks + 1 : blocks + 2, :] = jnp.sum(spreads[0], axis=0, keepdims=True)
    for out in outs:
        out.wait()


def node_means(all_ref, old_ref, means_ref, parts_ref):
    groups, blocks, _ = old_ref.shape
    spread, drift, mass = 0.0, 0.0, 0.0
    for g in range(groups):
        first, second = 2 * g, 2 * g + 1
        a, b = all_ref[first, 0:blocks], all_ref[second, 0:blocks]
        mass_a, mass_b = all_ref[first, blocks : blocks + 1], all_ref[second, blocks : blocks + 1]
        both = mass_a + mass_b
        mean = (a + b) / both
        means_ref[g] = mean
        gap = a / mass_a - b / mass_b
        spread = spread + all_ref[first, blocks + 1 : blocks + 2] + all_ref[second, blocks + 1 : blocks + 2]
        spread = spread + (mass_a * mass_b / both) * jnp.sum(gap * gap, axis=0, keepdims=True)
        change = mean - old_ref[g]
        drift = drift + both * jnp.sum(change * change, axis=0, keepdims=True)
        mass = mass + both
    lane = lax.broadcasted_iota(jnp.int32, (1, LANES), 1)
    spread = jnp.sum(spread, axis=1, keepdims=True)
    drift = jnp.sum(drift, axis=1, keepdims=True)
    parts = jnp.where(lane == 0, spread, jnp.where(lane == 1, drift, mass))
    parts_ref[...] = jnp.broadcast_to(parts[None], parts_ref.shape)


def new_duals(
    node_ref, x_ref, means_ref, parts_ref, mult_far, out_far, primal_ref, dual_ref,
    mult_near, mult_sem, out_near, out_sem,
):
    factor = None
    outs = []
    for k, cols in spans((mult_far, mult_near, mult_sem)):
        if factor is None:
            sums = jnp.sum(parts_ref[...], axis=0)[0:1, :]
            normaliser = parts_ref[0, 0:1, 2:3] * V
            primal = jnp.sqrt(sums[:, 0:1] / normaliser + epsilon)
            dual = penalty * jnp.sqrt(sums[:, 1:2] / normaliser + epsilon)
            factor = penalty * jnp.sqrt(primal / dual)
            primal_ref[...] = primal
            dual_ref[...] = dual
            mean = means_ref[node_ref[0]]
        for b, block in per_lane_block(cols):
            out_near[:, block] = mult_near[:, block] + factor * (x_ref[:, block] - mean[b : b + 1, :])
        out = pltpu.make_async_copy(out_near.at[:, cols], out_far.at[:, cols], out_sem.at[k])
        out.start()
        outs.append(out)
    for out in outs:
        out.wait()


def to_all(x, axes):
    devices = lax.axis_size(axes)
    return lax.all_to_all(jnp.broadcast_to(x[None], (devices, *x.shape)), axes, 0, 0, tiled=True)


def excess_of(partial, rhs_rows, axes):
    devices = lax.axis_size(axes)
    rows, width = partial.shape
    pieces = partial.reshape(devices, rows // devices, width)
    arrived = lax.all_to_all(pieces, axes, 0, 0, tiled=True)
    return to_all(jnp.sum(arrived, axis=0) - rhs_rows, axes).reshape(rows, width)


def shards(
    start_point,
    multipliers,
    cost,
    curvature,
    recourse_rhs,
    technology,
    scenario_weight,
    previous_mean,
    active,
):
    rows, width = start_point.shape
    images = recourse_rhs.shape[1]
    groups = previous_mean.shape[0]
    group_size = lax.axis_size(SCEN) // groups
    my_node = lax.axis_index(SCEN) // group_size
    blocks = width // LANES
    old_means = previous_mean.reshape(groups, blocks, LANES)
    old_row = lax.dynamic_index_in_dim(old_means, my_node, 0, keepdims=False)
    owned = rows // lax.axis_size(VAR)
    rhs_rows = lax.dynamic_slice_in_dim(recourse_rhs, lax.axis_index(VAR) * owned, owned, 0)
    rhs_rows = lax.optimization_barrier(rhs_rows)
    weight = scenario_weight[:, None]
    gain = stride * active.astype(jnp.float32)
    product = 2 * rows * width * images
    spread_over = pltpu.SemaphoreType.DMA((len(SPANS),))

    iterate, partial = local_call(
        first_image,
        [(rows, width), (rows, images)],
        [start_point, technology],
        product,
        far_in=(0, 1),
        scratch=landing(start_point) + landing(technology),
    )
    linear, curvature_far = local_call(
        linear_terms,
        [(2 * rows, width), jax.ShapeDtypeStruct((4 * rows, width), curvature.dtype)],
        [multipliers, cost, curvature, old_row],
        2 * rows * width,
        far_in=(0, 1, 2),
        far_out=(0, 1),
        scratch=landing(multipliers) + 2 * landing(cost) + landing(multipliers) + [spread_over],
    )
    far = [technology, linear, curvature_far]
    near = landing(technology) + landing(multipliers) + landing(curvature)
    for sweep in range(STEPS):
        excess = excess_of(partial, rhs_rows, VAR)
        operands = [excess, iterate, gain]
        if sweep < STEPS - 1:
            iterate, partial = local_call(
                step,
                [(rows, width), (rows, images)],
                operands + far,
                2 * product,
                far_in=(3, 4, 5),
                scratch=near,
                aliases={1: 0},
            )
        else:
            iterate, final, own_row = local_call(
                last_step,
                [(rows, width), (rows, width), (blocks + 2, LANES)],
                operands + [weight] + far,
                product,
                far_in=(4, 5, 6),
                far_out=(1,),
                scratch=near + [spread_over],
                aliases={1: 0},
            )
    everyone = to_all(own_row, SCEN)
    means, parts = local_call(
        node_means, [(groups, blocks, LANES), (lax.axis_size(VAR), 8, LANES)], [everyone, old_means]
    )
    bundle_mean = means.reshape(groups, width)
    parts = lax.all_to_all(parts, VAR, 0, 0, tiled=True)
    new_multipliers, primal_norm, dual_norm = local_call(
        new_duals,
        [(rows, width), (1, 1), (1, 1)],
        [jnp.full((1,), my_node, jnp.int32), iterate, means, parts, multipliers],
        3 * rows * width,
        scalar_in=(0,),
        far_in=(4,),
        far_out=(0,),
        scratch=landing(multipliers) + landing(multipliers)[:1] + [spread_over],
    )
    return (final, new_multipliers, bundle_mean, primal_norm[0, 0], dual_norm[0, 0])


def solution(mesh):
    torus = Mesh(mesh.devices.reshape(4, 2, 4, 4), ("x", "core", "z", "y"))
    return jax.shard_map(
        shards,
        mesh=torus,
        in_specs=(
            P(SCEN, VAR),
            P(SCEN, VAR),
            P(SCEN, VAR),
            P(SCEN, VAR),
            P(SCEN, None),
            P(None, VAR),
            P(SCEN),
            P(None, VAR),
            P(SCEN, VAR),
        ),
        out_specs=(P(SCEN, VAR), P(SCEN, VAR), P(None, VAR), P(), P()),
        check_vma=False,
    )
```

time: 270 us -> 263 us (0.974)
  between operations: 5.38 us -> 1.2 us
    all_to_all x3 -> x2, waiting for transfers between devices: 18.6 us -> 11.5 us  [to_all(): lax.all_to_all(jnp.broadcast_to(x[None], (devices, *x.shape)), axes, 0, 0...]
    all_to_all x1 -> x2, waiting for transfers between devices: 8.67 us -> 15.5 us  [the longest x1 8.61 us: excess_of(): arrived = lax.all_to_all(pieces, axes, 0, 0, tiled=True)]
    all_to_all x3 -> x2, starting transfers between devices: 11.4 us -> 7.29 us  [to_all(): lax.all_to_all(jnp.broadcast_to(x[None], (devices, *x.shape)), axes, 0, 0...]
    all_to_all x1 -> x2, starting transfers between devices: 8.28 us -> 11.6 us  [the longest x1 8.14 us: excess_of(): arrived = lax.all_to_all(pieces, axes, 0, 0, tiled=True)]
    pallas_call x13 -> x12, Pallas kernels: 47.6 us -> 47 us  [local_call(): pl.pallas_call(body, out_shape=outs, in_specs=[SMALL if k in scalar_in el...]
  transfers between devices with their start and end apart: 5 -> 4, of which waited for: 4 -> 4; matrix products, arithmetic and copies ran while one was open for 1% -> 0% of each run, Pallas kernels for 2% -> 1%
where the time goes in v3:
time: 263 us; the launch traced here: 262 us
  blocking collectives  163 us (62%)
  Pallas kernels  47 us (18%)
  waiting for transfers between devices  27 us (10%)
  starting transfers between devices  18.9 us (7%)
  local copies, waits for them, and re-layouts  4.96 us (2%)
    all_to_all x7, blocking collectives, excess_of(): arrived = lax.all_to_all(pieces, axes, 0, 0, tiled=True)  82.4 us
    all_to_all x7, blocking collectives, to_all(): lax.all_to_all(jnp.broadcast_to(x[None], (devices, *x.shape)), axes, 0, 0...  80.6 us
    pallas_call x12, Pallas kernels, local_call(): pl.pallas_call(body, out_shape=outs, in_specs=[SMALL if k in scalar_in el...  47 us
    all_to_all x2, waiting for transfers between devices, to_all(): lax.all_to_all(jnp.broadcast_to(x[None], (devices, *x.shape)), axes, 0, 0...  11.5 us
    all_to_all x1, waiting for transfers between devices, excess_of(): arrived = lax.all_to_all(pieces, axes, 0, 0, tiled=True)  8.61 us
    all_to_all x1, starting transfers between devices, excess_of(): arrived = lax.all_to_all(pieces, axes, 0, 0, tiled=True)  8.14 us
    all_to_all x2, starting transfers between devices, to_all(): lax.all_to_all(jnp.broadcast_to(x[None], (devices, *x.shape)), axes, 0, 0...  7.29 us
    all_to_all x1, waiting for transfers between devices, shards(): parts = lax.all_to_all(parts, VAR, 0, 0, tiled=True)  6.93 us
  transfers between devices with their start and end apart: 4, of which 4 were waited for; matrix products, arithmetic and copies ran while one was open for 0% of the time, Pallas kernels for 1%

profile of v3, /device:TPU:0, one launch (start us, length us, event | category | flops | bytes accessed | tf_op | source)
XLA Modules:
  0.0 262.3 jit_solution(7870249586349015301)
XLA Ops:
  0.6 0.0 copy-start
  0.6 0.0 copy-start.3
  0.7 0.0 copy-start.4
  0.7 4.1 %shard_map.128 = (f32[128,4096]{1,0:T(8,128)S(1)}, f32[128,512]{1,0:T(8,128)}) custom-call(f32[128,4096]{1,0:T(8,128)} %start_far.1, bf16[512,4096]{1,0:T(8,128)(2,1)} %tech_far.17), custom_call_target="tpu_custom_call" | custom-call | flops 536870912 | bytes 8650752 | tf_op jit(solution)/shard_map/pallas_call | solution.py:30
  4.7 8.1 %all-to-all-start = ((f32[16,8,512]{2,1,0:T(8,128)}), f32[16,8,512]{2,1,0:T(8,128)S(1)}, u32[]{:S(2)}, u32[]{:S(2)}) async-start(f32[16,8,512]{2,1,0:T(8,128)} %bitcast), calls=%async_computation | async-start | bytes 524288 | tf_op jit(solution)/shard_map/all_to_all | solution.py:240
  12.9 0.0 copy-done
  12.9 0.0 copy-done.3
  13.0 8.6 %all-to-all-done = f32[16,8,512]{2,1,0:T(8,128)S(1)} async-done(((f32[16,8,512]{2,1,0:T(8,128)}), f32[16,8,512]{2,1,0:T(8,128)S(1)}, u32[]{:S(2)}, u32[]{:S(2)}) %all-to-all-start) | async-done | bytes 262176 | tf_op jit(solution)/shard_map/all_to_all | solution.py:240
  21.6 0.7 broadcast_in_dim.22
  22.4 3.5 %all-to-all-start.1 = ((f32[16,8,512]{2,1,0:T(8,128)}), f32[16,8,512]{2,1,0:T(8,128)S(1)}, u32[]{:S(2)}, u32[]{:S(2)}) async-start(f32[16,8,512]{2,1,0:T(8,128)} %broadcast_in_dim.22), calls=%async_computation.1 | async-start | bytes 524288 | tf_op jit(solution)/shard_map/all_to_all | solution.py:233
  25.9 0.0 copy-done.4
  25.9 0.1 copy.22
  26.0 0.0 copy-start.1
  26.0 1.2 copy-done.1
  27.3 0.0 copy-start.2
  27.3 1.2 copy-done.2
  28.5 2.9 %shard_map.129 = (f32[256,4096]{1,0:T(8,128)}, bf16[512,4096]{1,0:T(8,128)(2,1)}) custom-call(f32[128,4096]{1,0:T(8,128)} %mult_far.3, bf16[128,4096]{1,0:T(8,128)(2,1)S(1)} %copy-done.1, bf16[128,4096]{1,0:T(8,128)(2,1)S(1)} %copy-done.2, f32[32,128]{1,0:T(8,128)S(1)} %dynamic-slice_bitcast_fusion.old_ref), custom_call_target="tpu_custom_call" | custom-call | flops 1048576 | bytes 12599296 | tf_op jit(solution)/shard_map/pallas_call | solution.py:30
  31.4 3.1 %all-to-all-done.1 = f32[16,8,512]{2,1,0:T(8,128)S(1)} async-done(((f32[16,8,512]{2,1,0:T(8,128)}), f32[16,8,512]{2,1,0:T(8,128)S(1)}, u32[]{:S(2)}, u32[]{:S(2)}) %all-to-all-start.1) | async-done | bytes 262176 | tf_op jit(solution)/shard_map/all_to_all | solution.py:233
  34.6 4.5 %shard_map.130 = (f32[128,4096]{1,0:T(8,128)S(1)}, f32[128,512]{1,0:T(8,128)S(1)}) custom-call(f32[128,512]{1,0:T(8,128)S(1)} %bitcast.30, f32[128,4096]{1,0:T(8,128)S(1)} %get-tuple-element.32.x_ref, f32[128,32]{1,0:T(8,128)S(1)} %convert_multiply_fusion.gain_ref, bf16[512,4096]{1,0:T(8,128)(2,1)} %tech_far.17, ...), custom_call_target="tpu_custom_call", output_to_operand_aliasing={{0}: (1, {})} | custom-call | flops 1073741824 | bytes 17317888 | tf_op jit(solution)/shard_map/pallas_call | solution.py:30
  39.0 12.5 %all_to_all.90 = f32[16,8,512]{2,1,0:T(8,128)S(1)} all-to-all(f32[16,8,512]{2,1,0:T(8,128)S(1)} %bitcast.41), channel_id=1, replica_groups=mesh['x'=4,'core'=2,'z'=4,'y'=4] {'z','y'}, dimensions={0} | all-to-all | bytes 524288 | tf_op jit(solution)/shard_map/all_to_all | solution.py:240
  51.6 11.6 %all_to_all.91 = f32[16,8,512]{2,1,0:T(8,128)S(1)} all-to-all(f32[16,8,512]{2,1,0:T(8,128)S(1)} %broadcast_in_dim.23), channel_id=1, replica_groups=mesh['x'=4,'core'=2,'z'=4,'y'=4] {'z','y'}, dimensions={0} | all-to-all | bytes 524288 | tf_op jit(solution)/shard_map/all_to_all | solution.py:233
  63.2 4.5 %shard_map.131 = (f32[128,4096]{1,0:T(8,128)S(1)}, f32[128,512]{1,0:T(8,128)S(1)}) custom-call(f32[128,512]{1,0:T(8,128)S(1)} %bitcast.32, f32[128,4096]{1,0:T(8,128)S(1)} %get-tuple-element.36.x_ref, f32[128,32]{1,0:T(8,128)S(1)} %convert_multiply_fusion.gain_ref, bf16[512,4096]{1,0:T(8,128)(2,1)} %tech_far.17, ...), custom_call_target="tpu_custom_call", output_to_operand_aliasing={{0}: (1, {})} | custom-call | flops 1073741824 | bytes 17317888 | tf_op jit(solution)/shard_map/pallas_call | solution.py:30
  67.7 11.6 %all_to_all.92 = f32[16,8,512]{2,1,0:T(8,128)S(1)} all-to-all(f32[16,8,512]{2,1,0:T(8,128)S(1)} %bitcast.42), channel_id=1, replica_groups=mesh['x'=4,'core'=2,'z'=4,'y'=4] {'z','y'}, dimensions={0} | all-to-all | bytes 524288 | tf_op jit(solution)/shard_map/all_to_all | solution.py:240
  79.4 11.6 %all_to_all.93 = f32[16,8,512]{2,1,0:T(8,128)S(1)} all-to-all(f32[16,8,512]{2,1,0:T(8,128)S(1)} %broadcast_in_dim.24), channel_id=1, replica_groups=mesh['x'=4,'core'=2,'z'=4,'y'=4] {'z','y'}, dimensions={0} | all-to-all | bytes 524288 | tf_op jit(solution)/shard_map/all_to_all | solution.py:233
  91.0 4.5 %shard_map.132 = (f32[128,4096]{1,0:T(8,128)S(1)}, f32[128,512]{1,0:T(8,128)S(1)}) custom-call(f32[128,512]{1,0:T(8,128)S(1)} %bitcast.33, f32[128,4096]{1,0:T(8,128)S(1)} %get-tuple-element.38.x_ref, f32[128,32]{1,0:T(8,128)S(1)} %convert_multiply_fusion.gain_ref, bf16[512,4096]{1,0:T(8,128)(2,1)} %tech_far.17, ...), custom_call_target="tpu_custom_call", output_to_operand_aliasing={{0}: (1, {})} | custom-call | flops 1073741824 | bytes 17317888 | tf_op jit(solution)/shard_map/pallas_call | solution.py:30
  95.5 11.7 %all_to_all.94 = f32[16,8,512]{2,1,0:T(8,128)S(1)} all-to-all(f32[16,8,512]{2,1,0:T(8,128)S(1)} %bitcast.43), channel_id=1, replica_groups=mesh['x'=4,'core'=2,'z'=4,'y'=4] {'z','y'}, dimensions={0} | all-to-all | bytes 524288 | tf_op jit(solution)/shard_map/all_to_all | solution.py:240
  107.2 11.5 %all_to_all.95 = f32[16,8,512]{2,1,0:T(8,128)S(1)} all-to-all(f32[16,8,512]{2,1,0:T(8,128)S(1)} %broadcast_in_dim.25), channel_id=1, replica_groups=mesh['x'=4,'core'=2,'z'=4,'y'=4] {'z','y'}, dimensions={0} | all-to-all | bytes 524288 | tf_op jit(solution)/shard_map/all_to_all | solution.py:233
  118.7 4.5 %shard_map.133 = (f32[128,4096]{1,0:T(8,128)S(1)}, f32[128,512]{1,0:T(8,128)S(1)}) custom-call(f32[128,512]{1,0:T(8,128)S(1)} %bitcast.34, f32[128,4096]{1,0:T(8,128)S(1)} %get-tuple-element.40.x_ref, f32[128,32]{1,0:T(8,128)S(1)} %convert_multiply_fusion.gain_ref, bf16[512,4096]{1,0:T(8,128)(2,1)} %tech_far.17, ...), custom_call_target="tpu_custom_call", output_to_operand_aliasing={{0}: (1, {})} | custom-call | flops 1073741824 | bytes 17317888 | tf_op jit(solution)/shard_map/pallas_call | solution.py:30
  123.2 11.8 %all_to_all.96 = f32[16,8,512]{2,1,0:T(8,128)S(1)} all-to-all(f32[16,8,512]{2,1,0:T(8,128)S(1)} %bitcast.44), channel_id=1, replica_groups=mesh['x'=4,'core'=2,'z'=4,'y'=4] {'z','y'}, dimensions={0} | all-to-all | bytes 524288 | tf_op jit(solution)/shard_map/all_to_all | solution.py:240
  135.1 11.6 %all_to_all.97 = f32[16,8,512]{2,1,0:T(8,128)S(1)} all-to-all(f32[16,8,512]{2,1,0:T(8,128)S(1)} %broadcast_in_dim.26), channel_id=1, replica_groups=mesh['x'=4,'core'=2,'z'=4,'y'=4] {'z','y'}, dimensions={0} | all-to-all | bytes 524288 | tf_op jit(solution)/shard_map/all_to_all | solution.py:233
  146.7 4.5 %shard_map.134 = (f32[128,4096]{1,0:T(8,128)S(1)}, f32[128,512]{1,0:T(8,128)S(1)}) custom-call(f32[128,512]{1,0:T(8,128)S(1)} %bitcast.35, f32[128,4096]{1,0:T(8,128)S(1)} %get-tuple-element.42.x_ref, f32[128,32]{1,0:T(8,128)S(1)} %convert_multiply_fusion.gain_ref, bf16[512,4096]{1,0:T(8,128)(2,1)} %tech_far.17, ...), custom_call_target="tpu_custom_call", output_to_operand_aliasing={{0}: (1, {})} | custom-call | flops 1073741824 | bytes 17317888 | tf_op jit(solution)/shard_map/pallas_call | solution.py:30
  151.2 11.6 %all_to_all.98 = f32[16,8,512]{2,1,0:T(8,128)S(1)} all-to-all(f32[16,8,512]{2,1,0:T(8,128)S(1)} %bitcast.45), channel_id=1, replica_groups=mesh['x'=4,'core'=2,'z'=4,'y'=4] {'z','y'}, dimensions={0} | all-to-all | bytes 524288 | tf_op jit(solution)/shard_map/all_to_all | solution.py:240
  162.8 12.2 %all_to_all.99 = f32[16,8,512]{2,1,0:T(8,128)S(1)} all-to-all(f32[16,8,512]{2,1,0:T(8,128)S(1)} %broadcast_in_dim.27), channel_id=1, replica_groups=mesh['x'=4,'core'=2,'z'=4,'y'=4] {'z','y'}, dimensions={0} | all-to-all | bytes 524288 | tf_op jit(solution)/shard_map/all_to_all | solution.py:233
  175.0 4.5 %shard_map.135 = (f32[128,4096]{1,0:T(8,128)S(1)}, f32[128,512]{1,0:T(8,128)S(1)}) custom-call(f32[128,512]{1,0:T(8,128)S(1)} %bitcast.36, f32[128,4096]{1,0:T(8,128)S(1)} %get-tuple-element.44.x_ref, f32[128,32]{1,0:T(8,128)S(1)} %convert_multiply_fusion.gain_ref, bf16[512,4096]{1,0:T(8,128)(2,1)} %tech_far.17, ...), custom_call_target="tpu_custom_call", output_to_operand_aliasing={{0}: (1, {})} | custom-call | flops 1073741824 | bytes 17317888 | tf_op jit(solution)/shard_map/pallas_call | solution.py:30
  179.5 11.6 %all_to_all.100 = f32[16,8,512]{2,1,0:T(8,128)S(1)} all-to-all(f32[16,8,512]{2,1,0:T(8,128)S(1)} %bitcast.46), channel_id=1, replica_groups=mesh['x'=4,'core'=2,'z'=4,'y'=4] {'z','y'}, dimensions={0} | all-to-all | bytes 524288 | tf_op jit(solution)/shard_map/all_to_all | solution.py:240
  191.2 11.6 %all_to_all.101 = f32[16,8,512]{2,1,0:T(8,128)S(1)} all-to-all(f32[16,8,512]{2,1,0:T(8,128)S(1)} %broadcast_in_dim.28), channel_id=1, replica_groups=mesh['x'=4,'core'=2,'z'=4,'y'=4] {'z','y'}, dimensions={0} | all-to-all | bytes 524288 | tf_op jit(solution)/shard_map/all_to_all | solution.py:233
  202.8 0.0 copy-start.5
  202.8 4.5 %shard_map.136 = (f32[128,4096]{1,0:T(8,128)S(1)}, f32[128,512]{1,0:T(8,128)S(1)}) custom-call(f32[128,512]{1,0:T(8,128)S(1)} %bitcast.37, f32[128,4096]{1,0:T(8,128)S(1)} %get-tuple-element.46.x_ref, f32[128,32]{1,0:T(8,128)S(1)} %convert_multiply_fusion.gain_ref, bf16[512,4096]{1,0:T(8,128)(2,1)} %tech_far.17, ...), custom_call_target="tpu_custom_call", output_to_operand_aliasing={{0}: (1, {})} | custom-call | flops 1073741824 | bytes 17317888 | tf_op jit(solution)/shard_map/pallas_call | solution.py:30
  207.3 11.6 %all_to_all.102 = f32[16,8,512]{2,1,0:T(8,128)S(1)} all-to-all(f32[16,8,512]{2,1,0:T(8,128)S(1)} %bitcast.47), channel_id=1, replica_groups=mesh['x'=4,'core'=2,'z'=4,'y'=4] {'z','y'}, dimensions={0} | all-to-all | bytes 524288 | tf_op jit(solution)/shard_map/all_to_all | solution.py:240
  218.9 0.7 broadcast_in_dim.29
  219.6 3.8 %all-to-all-start.15 = ((f32[16,8,512]{2,1,0:T(8,128)}), f32[16,8,512]{2,1,0:T(8,128)S(1)}, u32[]{:S(2)}, u32[]{:S(2)}) async-start(f32[16,8,512]{2,1,0:T(8,128)} %broadcast_in_dim.29), calls=%async_computation.15 | async-start | bytes 524288 | tf_op jit(solution)/shard_map/all_to_all | solution.py:233
  223.4 0.0 copy-done.5
  223.4 0.1 copy.23.weight_ref
  223.5 8.3 %all-to-all-done.15 = f32[16,8,512]{2,1,0:T(8,128)S(1)} async-done(((f32[16,8,512]{2,1,0:T(8,128)}), f32[16,8,512]{2,1,0:T(8,128)S(1)}, u32[]{:S(2)}, u32[]{:S(2)}) %all-to-all-start.15) | async-done | bytes 262176 | tf_op jit(solution)/shard_map/all_to_all | solution.py:233
  231.8 4.7 %shard_map.137 = (f32[128,4096]{1,0:T(8,128)S(1)}, f32[128,4096]{1,0:T(8,128)}, f32[34,128]{1,0:T(8,128)S(1)}) custom-call(f32[128,512]{1,0:T(8,128)S(1)} %bitcast.31, f32[128,4096]{1,0:T(8,128)S(1)} %get-tuple-element.48.x_ref, f32[128,32]{1,0:T(8,128)S(1)} %convert_multiply_fusion.gain_ref, ...), custom_call_target="tpu_custom_call", output_to_operand_aliasing={{0}: (1, {})} | custom-call | flops 536870912 | bytes 19170816 | tf_op jit(solution)/shard_map/pallas_call | solution.py:30
  236.5 10.6 %all_to_all.103.all_ref = f32[8,34,128]{2,1,0:T(8,128)S(1)} all-to-all(f32[8,34,128]{2,1,0:T(8,128)S(1)} %broadcast_in_dim.32), channel_id=1, replica_groups=mesh['x'=4,'core'=2,'z'=4,'y'=4] {'x','core'}, dimensions={0} | all-to-all | bytes 278528 | tf_op jit(solution)/shard_map/all_to_all | solution.py:233
  247.1 0.8 shard_map.138
  247.9 3.5 %all-to-all-start.17 = ((f32[16,8,128]{2,1,0:T(8,128)}), f32[16,8,128]{2,1,0:T(8,128)S(1)}, u32[]{:S(2)}, u32[]{:S(2)}) async-start(f32[16,8,128]{2,1,0:T(8,128)} %get-tuple-element.53), calls=%async_computation.17 | async-start | bytes 131072 | tf_op jit(solution)/shard_map/all_to_all | solution.py:319
  251.4 0.7 copy.28
  252.1 6.9 %all-to-all-done.17.parts_ref = f32[16,8,128]{2,1,0:T(8,128)S(1)} async-done(((f32[16,8,128]{2,1,0:T(8,128)}), f32[16,8,128]{2,1,0:T(8,128)S(1)}, u32[]{:S(2)}, u32[]{:S(2)}) %all-to-all-start.17) | async-done | bytes 65568 | tf_op jit(solution)/shard_map/all_to_all | solution.py:319
  259.0 3.1 %shard_map.139 = (f32[128,4096]{1,0:T(8,128)}, f32[1,1]{1,0:T(1,128)}, f32[1,1]{1,0:T(1,128)}) custom-call(s32[1]{0:T(128)} %bitcast.18.node_ref, f32[128,4096]{1,0:T(8,128)S(1)} %get-tuple-element.50.x_ref, f32[4,32,128]{2,1,0:T(8,128)S(1)} %get-tuple-element.52.means_ref, f32[16,8,128]{2,1,0:T(8,128)S(1)} %all-to-all-done.17.parts_ref, f32[128,4096]{1,0:T(8,128)} %mult_far.3), custom_call_target="tpu_custom_call" | custom-call | flops 1572864 | bytes 6422540 | tf_op jit(solution)/shard_map/pallas_call | solution.py:30
  (27 shorter events, 0.4 us)
Async XLA Ops:
  0.6 12.3 %copy-start = (f32[128,512]{1,0:T(8,128)S(1)}, f32[128,512]{1,0:T(8,128)}, u32[]{:S(2)}) copy-start(f32[128,512]{1,0:T(8,128)} %param.13) | copy-start | bytes 786436
  0.6 12.3 %copy-start.3 = (f32[4,4096]{1,0:T(4,128)S(1)}, f32[4,4096]{1,0:T(4,128)}, u32[]{:S(2)}) copy-start(f32[4,4096]{1,0:T(4,128)} %param.16) | copy-start | bytes 196612
  0.7 25.3 %copy-start.4 = (s32[128,32]{0,1:T(8,128)S(1)}, s32[128,32]{0,1:T(8,128)}, u32[]{:S(2)}) copy-start(s32[128,32]{0,1:T(8,128)} %param.17) | copy-start | bytes 49156
  4.7 16.8 %all-to-all-start = ((f32[16,8,512]{2,1,0:T(8,128)}), f32[16,8,512]{2,1,0:T(8,128)S(1)}, u32[]{:S(2)}, u32[]{:S(2)}) async-start(f32[16,8,512]{2,1,0:T(8,128)} %bitcast), calls=%async_computation | async-start | bytes 524288 | tf_op jit(solution)/shard_map/all_to_all | solution.py:240
  22.4 12.2 %all-to-all-start.1 = ((f32[16,8,512]{2,1,0:T(8,128)}), f32[16,8,512]{2,1,0:T(8,128)S(1)}, u32[]{:S(2)}, u32[]{:S(2)}) async-start(f32[16,8,512]{2,1,0:T(8,128)} %broadcast_in_dim.22), calls=%async_computation.1 | async-start | bytes 524288 | tf_op jit(solution)/shard_map/all_to_all | solution.py:233
  26.0 1.2 copy-start.1
  27.3 1.2 copy-start.2
  202.8 20.6 %copy-start.5 = (f32[128]{0:T(128)S(1)}, f32[128]{0:T(128)}, u32[]{:S(2)}) copy-start(f32[128]{0:T(128)} %param.15) | copy-start | bytes 1540
  219.6 12.2 %all-to-all-start.15 = ((f32[16,8,512]{2,1,0:T(8,128)}), f32[16,8,512]{2,1,0:T(8,128)S(1)}, u32[]{:S(2)}, u32[]{:S(2)}) async-start(f32[16,8,512]{2,1,0:T(8,128)} %broadcast_in_dim.29), calls=%async_computation.15 | async-start | bytes 524288 | tf_op jit(solution)/shard_map/all_to_all | solution.py:233
  247.9 11.1 %all-to-all-start.17 = ((f32[16,8,128]{2,1,0:T(8,128)}), f32[16,8,128]{2,1,0:T(8,128)S(1)}, u32[]{:S(2)}, u32[]{:S(2)}) async-start(f32[16,8,128]{2,1,0:T(8,128)} %get-tuple-element.53), calls=%async_computation.17 | async-start | bytes 131072 | tf_op jit(solution)/shard_map/all_to_all | solution.py:319

commit v4 on v3

--- a/solution.py
+++ b/solution.py
@@ -11,7 +11,7 @@
 SCEN = ("x", "core")
 VAR = ("z", "y")
 LANES = 128
-SPANS = ((0, 512), (512, 1024), (1536, 1024), (2560, 1024), (3584, 512))
+SPANS = ((0, 256), (256, 512), (768, 1024), (1792, 1024), (2816, 768), (3584, 512))
 
 penalty = 1.0
 recourse_scale = 4.0
@@ -21,7 +21,7 @@
 WHOLE = pl.BlockSpec(memory_space=pltpu.VMEM)
 FAR = pl.BlockSpec(memory_space=pltpu.HBM)
 SMALL = pl.BlockSpec(memory_space=pltpu.SMEM)
-ROOM = 51 << 20
+ROOM = 50 << 20
 
 
 def local_call(body, outs, args, flops=0, scalar_in=(), far_in=(), far_out=(), scratch=(), aliases=None):
@@ -48,13 +48,14 @@
     return slice(start, start + size)
 
 
-def spans(*triples):
+def spans(*triples, first=0):
     copies = []
     for k, span in enumerate(SPANS):
         cols = pl.ds(*span)
         row = [
             pltpu.make_async_copy(far.at[pl.ds(0, near.shape[0]), cols], near.at[:, cols], sems.at[k])
             for far, near, sems in triples
+            if k >= first
         ]
         for copy in row:
             copy.start()
@@ -71,7 +72,7 @@
     )
 
 
-def first_image(start_far, tech_far, x_ref, image_ref, start_near, start_sem, tech_near, tech_sem):
+def first_image(start_far, tech_far, x_ref, image_ref, tech_head, start_near, start_sem, tech_near, tech_sem):
     total = None
     for _, cols in spans((tech_far, tech_near, tech_sem), (start_far, start_near, start_sem)):
         x = start_near[:, cols]
@@ -79,6 +80,7 @@
         part = image_of(x, tech_near[:, cols])
         total = part if total is None else total + part
     image_ref[...] = total
+    tech_head[...] = tech_near[:, cols_of(0)]
 
 
 def per_lane_block(cols):
@@ -86,7 +88,7 @@
 
 
 def linear_terms(
-    mult_far, cost_far, curv_far, old_ref, linear_far, curv_out,
+    mult_far, cost_far, curv_far, old_ref, linear_far, curv_out, linear_head, curv_head,
     mult_near, mult_sem, cost_near, cost_sem, curv_near, curv_sem, out_near, out_sem, curv_out_sem,
 ):
     rows = curv_far.shape[0]
@@ -99,6 +101,8 @@
             out = pltpu.make_async_copy(near.at[:, cols], far.at[pl.ds(0, rows), cols], sems.at[k])
             out.start()
             outs.append(out)
+    linear_head[...] = out_near[:, cols_of(0)]
+    curv_head[...] = curv_near[:, cols_of(0)]
     for out in outs:
         out.wait()
 
@@ -114,9 +118,11 @@
     return jnp.concatenate(pieces, axis=1)
 
 
-def each_span(arrivals, shortfall, tech_near, finish):
+def each_span(arrivals, shortfall, near, heads, finish):
     for k, cols in arrivals:
-        finish(k, cols, jnp.dot(shortfall, tech_near[:, cols], preferred_element_type=jnp.float32))
+        tech, linear, curv = near if k else heads
+        tech = tech[:, cols]
+        finish(k, cols, jnp.dot(shortfall, tech, preferred_element_type=jnp.float32), tech, linear, curv)
 
 
 def scaled_shortfall(excess_ref):
@@ -124,39 +130,45 @@
 
 
 def step(
-    excess_ref, x_ref, gain_ref, tech_far, linear_far, curv_far, new_ref, out_ref,
+    excess_ref, x_ref, gain_ref, tech_head, linear_head, curv_head, tech_far, linear_far, curv_far, new_ref, out_ref,
     tech_near, tech_sem, linear_near, linear_sem, curv_near, curv_sem,
 ):
     parts = []
 
-    def finish(k, cols, pullback):
-        new = moved(cols, pullback, x_ref, linear_near, curv_near, gain_ref)
+    def finish(k, cols, pullback, tech, linear, curv):
+        new = moved(cols, pullback, x_ref, linear, curv, gain_ref)
         new_ref[:, cols] = new
-        part = image_of(new, tech_near[:, cols])
+        part = image_of(new, tech)
         parts[:] = [parts[0] + part if parts else part]
 
     each_span(
-        spans((tech_far, tech_near, tech_sem), (curv_far, curv_near, curv_sem), (linear_far, linear_near, linear_sem)),
+        spans(
+            (tech_far, tech_near, tech_sem), (curv_far, curv_near, curv_sem), (linear_far, linear_near, linear_sem), first=1
+        ),
         scaled_shortfall(excess_ref),
-        tech_near,
+        (tech_near, linear_near, curv_near),
+        (tech_head, linear_head, curv_head),
         finish,
     )
     out_ref[...] = parts[0]
 
 
 def last_step(
-    excess_ref, x_ref, gain_ref, weight_ref, tech_far, linear_far, curv_far, new_ref, final_far, row_ref,
+    excess_ref, x_ref, gain_ref, tech_head, linear_head, curv_head, weight_ref, tech_far, linear_far, curv_far, new_ref, final_far, row_ref,
     tech_near, tech_sem, linear_near, linear_sem, curv_near, curv_sem, out_sem,
 ):
     rows, width = x_ref.shape
     blocks = width // LANES
-    weight = jnp.broadcast_to(weight_ref[...], (rows, LANES))
+    square = (rows, rows)
+    diagonal = lax.broadcasted_iota(jnp.int32, square, 0) == lax.broadcasted_iota(jnp.int32, square, 1)
+    column = jnp.sum(jnp.where(diagonal, jnp.broadcast_to(weight_ref[...], square), 0.0), axis=1, keepdims=True)
+    weight = jnp.broadcast_to(column, (rows, LANES))
     mass = jnp.sum(weight, axis=0, keepdims=True)
     spreads = [jnp.zeros((rows, LANES), jnp.float32)]
     outs = []
 
-    def finish(k, cols, pullback):
-        new = moved(cols, pullback, x_ref, linear_near, curv_near, gain_ref)
+    def finish(k, cols, pullback, tech, linear, curv):
+        new = moved(cols, pullback, x_ref, linear, curv, gain_ref)
         new_ref[:, cols] = new
         out = pltpu.make_async_copy(new_ref.at[:, cols], final_far.at[:, cols], out_sem.at[k])
         out.start()
@@ -169,9 +181,12 @@
             spreads[0] = spreads[0] + weight * away * away
 
     each_span(
-        spans((tech_far, tech_near, tech_sem), (curv_far, curv_near, curv_sem), (linear_far, linear_near, linear_sem)),
+        spans(
+            (tech_far, tech_near, tech_sem), (curv_far, curv_near, curv_sem), (linear_far, linear_near, linear_sem), first=1
+        ),
         scaled_shortfall(excess_ref),
-        tech_near,
+        (tech_near, linear_near, curv_near),
+        (tech_head, linear_head, curv_head),
         finish,
     )
     row_ref[blocks : blocks + 1, :] = mass
@@ -263,22 +278,28 @@
     owned = rows // lax.axis_size(VAR)
     rhs_rows = lax.dynamic_slice_in_dim(recourse_rhs, lax.axis_index(VAR) * owned, owned, 0)
     rhs_rows = lax.optimization_barrier(rhs_rows)
-    weight = scenario_weight[:, None]
+    weight = scenario_weight[None, :]
     gain = stride * active.astype(jnp.float32)
     product = 2 * rows * width * images
     spread_over = pltpu.SemaphoreType.DMA((len(SPANS),))
 
-    iterate, partial = local_call(
+    head = SPANS[0][1]
+    iterate, partial, tech_head = local_call(
         first_image,
-        [(rows, width), (rows, images)],
+        [(rows, width), (rows, images), jax.ShapeDtypeStruct((images, head), technology.dtype)],
         [start_point, technology],
         product,
         far_in=(0, 1),
         scratch=landing(start_point) + landing(technology),
     )
-    linear, curvature_far = local_call(
+    linear, curvature_far, linear_head, curv_head = local_call(
         linear_terms,
-        [(2 * rows, width), jax.ShapeDtypeStruct((4 * rows, width), curvature.dtype)],
+        [
+            (2 * rows, width),
+            jax.ShapeDtypeStruct((4 * rows, width), curvature.dtype),
+            (rows, head),
+            jax.ShapeDtypeStruct((rows, head), curvature.dtype),
+        ],
         [multipliers, cost, curvature, old_row],
         2 * rows * width,
         far_in=(0, 1, 2),
@@ -289,14 +310,14 @@
     near = landing(technology) + landing(multipliers) + landing(curvature)
     for sweep in range(STEPS):
         excess = excess_of(partial, rhs_rows, VAR)
-        operands = [excess, iterate, gain]
+        operands = [excess, iterate, gain, tech_head, linear_head, curv_head]
         if sweep < STEPS - 1:
             iterate, partial = local_call(
                 step,
                 [(rows, width), (rows, images)],
                 operands + far,
                 2 * product,
-                far_in=(3, 4, 5),
+                far_in=(6, 7, 8),
                 scratch=near,
                 aliases={1: 0},
             )
@@ -306,7 +327,7 @@
                 [(rows, width), (rows, width), (blocks + 2, LANES)],
                 operands + [weight] + far,
                 product,
-                far_in=(4, 5, 6),
+                far_in=(7, 8, 9),
                 far_out=(1,),
                 scratch=near + [spread_over],
                 aliases={1: 0},

time: 263 us -> 260 us (0.989)
  blocking collectives: 163 us -> 174 us
  waiting for transfers between devices: 27 us -> 18.6 us
  starting transfers between devices: 18.9 us -> 15.2 us
    all_to_all x7 -> x8, blocking collectives: 80.6 us -> 92.1 us  [to_all(): lax.all_to_all(jnp.broadcast_to(x[None], (devices, *x.shape)), axes, 0, 0...]
    all_to_all x2 -> x1, waiting for transfers between devices: 11.5 us -> 3.09 us  [to_all(): lax.all_to_all(jnp.broadcast_to(x[None], (devices, *x.shape)), axes, 0, 0...]
    all_to_all x2 -> x1, starting transfers between devices: 7.29 us -> 3.53 us  [to_all(): lax.all_to_all(jnp.broadcast_to(x[None], (devices, *x.shape)), axes, 0, 0...]
  transfers between devices with their start and end apart: 4 -> 3, of which waited for: 4 -> 3; matrix products, arithmetic and copies ran while one was open for 0% -> 0% of each run, Pallas kernels for 1% -> 1%
where the time goes in v4:
time: 260 us; the launch traced here: 259 us
  blocking collectives  174 us (67%)
  Pallas kernels  44.9 us (17%)
  waiting for transfers between devices  18.6 us (7%)
  starting transfers between devices  15.2 us (6%)
  local copies, waits for them, and re-layouts  4.14 us (2%)
    all_to_all x8, blocking collectives, to_all(): lax.all_to_all(jnp.broadcast_to(x[None], (devices, *x.shape)), axes, 0, 0...  92.1 us
    all_to_all x7, blocking collectives, excess_of(): arrived = lax.all_to_all(pieces, axes, 0, 0, tiled=True)  82.3 us
    pallas_call x12, Pallas kernels, local_call(): pl.pallas_call(body, out_shape=outs, in_specs=[SMALL if k in scalar_in el...  44.9 us
    all_to_all x1, waiting for transfers between devices, excess_of(): arrived = lax.all_to_all(pieces, axes, 0, 0, tiled=True)  8.61 us
    all_to_all x1, starting transfers between devices, excess_of(): arrived = lax.all_to_all(pieces, axes, 0, 0, tiled=True)  8.14 us
    all_to_all x1, waiting for transfers between devices, shards(): parts = lax.all_to_all(parts, VAR, 0, 0, tiled=True)  6.93 us
  transfers between devices with their start and end apart: 3, of which 3 were waited for; matrix products, arithmetic and copies ran while one was open for 0% of the time, Pallas kernels for 1%

profile of v4, /device:TPU:0, one launch (start us, length us, event | category | flops | bytes accessed | tf_op | source)
XLA Modules:
  0.0 258.6 jit_solution(6741645862695025994)
XLA Ops:
  0.6 0.0 copy-start
  0.6 0.0 copy-start.4
  0.7 0.0 copy-start.5
  0.7 4.1 %shard_map.128 = (f32[128,4096]{1,0:T(8,128)S(1)}, f32[128,512]{1,0:T(8,128)}, bf16[512,256]{1,0:T(8,128)(2,1)S(1)}) custom-call(f32[128,4096]{1,0:T(8,128)} %start_far.1, bf16[512,4096]{1,0:T(8,128)(2,1)} %tech_far.17), custom_call_target="tpu_custom_call" | custom-call | flops 536870912 | bytes 8912896 | tf_op jit(solution)/shard_map/pallas_call | solution.py:30
  4.7 8.1 %all-to-all-start = ((f32[16,8,512]{2,1,0:T(8,128)}), f32[16,8,512]{2,1,0:T(8,128)S(1)}, u32[]{:S(2)}, u32[]{:S(2)}) async-start(f32[16,8,512]{2,1,0:T(8,128)} %bitcast), calls=%async_computation | async-start | bytes 524288 | tf_op jit(solution)/shard_map/all_to_all | solution.py:255
  12.9 0.0 copy-done
  12.9 0.0 copy-done.4
  13.0 8.6 %all-to-all-done = f32[16,8,512]{2,1,0:T(8,128)S(1)} async-done(((f32[16,8,512]{2,1,0:T(8,128)}), f32[16,8,512]{2,1,0:T(8,128)S(1)}, u32[]{:S(2)}, u32[]{:S(2)}) %all-to-all-start) | async-done | bytes 262176 | tf_op jit(solution)/shard_map/all_to_all | solution.py:255
  21.6 0.7 broadcast_in_dim.22
  22.3 3.5 %all-to-all-start.1 = ((f32[16,8,512]{2,1,0:T(8,128)}), f32[16,8,512]{2,1,0:T(8,128)S(1)}, u32[]{:S(2)}, u32[]{:S(2)}) async-start(f32[16,8,512]{2,1,0:T(8,128)} %broadcast_in_dim.22), calls=%async_computation.1 | async-start | bytes 524288 | tf_op jit(solution)/shard_map/all_to_all | solution.py:248
  25.9 0.0 copy-done.5
  25.9 0.1 copy.22
  26.0 0.0 copy-start.1
  26.0 1.2 copy-done.1
  27.2 0.0 copy-start.2
  27.2 1.2 copy-done.2
  28.5 3.0 %shard_map.129 = (f32[256,4096]{1,0:T(8,128)}, bf16[512,4096]{1,0:T(8,128)(2,1)}, f32[128,256]{1,0:T(8,128)S(1)}, bf16[128,256]{1,0:T(8,128)(2,1)S(1)}) custom-call(f32[128,4096]{1,0:T(8,128)} %mult_far.3, bf16[128,4096]{1,0:T(8,128)(2,1)S(1)} %copy-done.1, bf16[128,4096]{1,0:T(8,128)(2,1)S(1)} %copy-done.2, f32[32,128]{1,0:T(8,128)S(1)} %dynamic-slice_bitcast_fusion.old_ref), custom_call_target="tpu_custom_call" | custom-call | flops 1048576 | bytes 12795904 | tf_op jit(solution)/shard_map/pallas_call | solution.py:30
  31.5 3.1 %all-to-all-done.1 = f32[16,8,512]{2,1,0:T(8,128)S(1)} async-done(((f32[16,8,512]{2,1,0:T(8,128)}), f32[16,8,512]{2,1,0:T(8,128)S(1)}, u32[]{:S(2)}, u32[]{:S(2)}) %all-to-all-start.1) | async-done | bytes 262176 | tf_op jit(solution)/shard_map/all_to_all | solution.py:248
  34.5 4.2 %shard_map.130 = (f32[128,4096]{1,0:T(8,128)S(1)}, f32[128,512]{1,0:T(8,128)S(1)}) custom-call(f32[128,512]{1,0:T(8,128)S(1)} %bitcast.30, f32[128,4096]{1,0:T(8,128)S(1)} %get-tuple-element.35.x_ref, f32[128,32]{1,0:T(8,128)S(1)} %convert_multiply_fusion.gain_ref, ...), custom_call_target="tpu_custom_call", output_to_operand_aliasing={{0}: (1, {})} | custom-call | flops 1073741824 | bytes 17776640 | tf_op jit(solution)/shard_map/pallas_call | solution.py:30
  38.7 12.6 %all_to_all.90 = f32[16,8,512]{2,1,0:T(8,128)S(1)} all-to-all(f32[16,8,512]{2,1,0:T(8,128)S(1)} %bitcast.41), channel_id=1, replica_groups=mesh['x'=4,'core'=2,'z'=4,'y'=4] {'z','y'}, dimensions={0} | all-to-all | bytes 524288 | tf_op jit(solution)/shard_map/all_to_all | solution.py:255
  51.3 11.6 %all_to_all.91 = f32[16,8,512]{2,1,0:T(8,128)S(1)} all-to-all(f32[16,8,512]{2,1,0:T(8,128)S(1)} %broadcast_in_dim.23), channel_id=1, replica_groups=mesh['x'=4,'core'=2,'z'=4,'y'=4] {'z','y'}, dimensions={0} | all-to-all | bytes 524288 | tf_op jit(solution)/shard_map/all_to_all | solution.py:248
  62.9 4.2 %shard_map.131 = (f32[128,4096]{1,0:T(8,128)S(1)}, f32[128,512]{1,0:T(8,128)S(1)}) custom-call(f32[128,512]{1,0:T(8,128)S(1)} %bitcast.32, f32[128,4096]{1,0:T(8,128)S(1)} %get-tuple-element.42.x_ref, f32[128,32]{1,0:T(8,128)S(1)} %convert_multiply_fusion.gain_ref, ...), custom_call_target="tpu_custom_call", output_to_operand_aliasing={{0}: (1, {})} | custom-call | flops 1073741824 | bytes 17776640 | tf_op jit(solution)/shard_map/pallas_call | solution.py:30
  67.1 11.6 %all_to_all.92 = f32[16,8,512]{2,1,0:T(8,128)S(1)} all-to-all(f32[16,8,512]{2,1,0:T(8,128)S(1)} %bitcast.42), channel_id=1, replica_groups=mesh['x'=4,'core'=2,'z'=4,'y'=4] {'z','y'}, dimensions={0} | all-to-all | bytes 524288 | tf_op jit(solution)/shard_map/all_to_all | solution.py:255
  78.8 11.6 %all_to_all.93 = f32[16,8,512]{2,1,0:T(8,128)S(1)} all-to-all(f32[16,8,512]{2,1,0:T(8,128)S(1)} %broadcast_in_dim.24), channel_id=1, replica_groups=mesh['x'=4,'core'=2,'z'=4,'y'=4] {'z','y'}, dimensions={0} | all-to-all | bytes 524288 | tf_op jit(solution)/shard_map/all_to_all | solution.py:248
  90.3 4.2 %shard_map.132 = (f32[128,4096]{1,0:T(8,128)S(1)}, f32[128,512]{1,0:T(8,128)S(1)}) custom-call(f32[128,512]{1,0:T(8,128)S(1)} %bitcast.33, f32[128,4096]{1,0:T(8,128)S(1)} %get-tuple-element.44.x_ref, f32[128,32]{1,0:T(8,128)S(1)} %convert_multiply_fusion.gain_ref, ...), custom_call_target="tpu_custom_call", output_to_operand_aliasing={{0}: (1, {})} | custom-call | flops 1073741824 | bytes 17776640 | tf_op jit(solution)/shard_map/pallas_call | solution.py:30
  94.5 11.7 %all_to_all.94 = f32[16,8,512]{2,1,0:T(8,128)S(1)} all-to-all(f32[16,8,512]{2,1,0:T(8,128)S(1)} %bitcast.43), channel_id=1, replica_groups=mesh['x'=4,'core'=2,'z'=4,'y'=4] {'z','y'}, dimensions={0} | all-to-all | bytes 524288 | tf_op jit(solution)/shard_map/all_to_all | solution.py:255
  106.3 11.5 %all_to_all.95 = f32[16,8,512]{2,1,0:T(8,128)S(1)} all-to-all(f32[16,8,512]{2,1,0:T(8,128)S(1)} %broadcast_in_dim.25), channel_id=1, replica_groups=mesh['x'=4,'core'=2,'z'=4,'y'=4] {'z','y'}, dimensions={0} | all-to-all | bytes 524288 | tf_op jit(solution)/shard_map/all_to_all | solution.py:248
  117.8 4.2 %shard_map.133 = (f32[128,4096]{1,0:T(8,128)S(1)}, f32[128,512]{1,0:T(8,128)S(1)}) custom-call(f32[128,512]{1,0:T(8,128)S(1)} %bitcast.34, f32[128,4096]{1,0:T(8,128)S(1)} %get-tuple-element.46.x_ref, f32[128,32]{1,0:T(8,128)S(1)} %convert_multiply_fusion.gain_ref, ...), custom_call_target="tpu_custom_call", output_to_operand_aliasing={{0}: (1, {})} | custom-call | flops 1073741824 | bytes 17776640 | tf_op jit(solution)/shard_map/pallas_call | solution.py:30
  121.9 11.8 %all_to_all.96 = f32[16,8,512]{2,1,0:T(8,128)S(1)} all-to-all(f32[16,8,512]{2,1,0:T(8,128)S(1)} %bitcast.44), channel_id=1, replica_groups=mesh['x'=4,'core'=2,'z'=4,'y'=4] {'z','y'}, dimensions={0} | all-to-all | bytes 524288 | tf_op jit(solution)/shard_map/all_to_all | solution.py:255
  133.8 11.7 %all_to_all.97 = f32[16,8,512]{2,1,0:T(8,128)S(1)} all-to-all(f32[16,8,512]{2,1,0:T(8,128)S(1)} %broadcast_in_dim.26), channel_id=1, replica_groups=mesh['x'=4,'core'=2,'z'=4,'y'=4] {'z','y'}, dimensions={0} | all-to-all | bytes 524288 | tf_op jit(solution)/shard_map/all_to_all | solution.py:248
  145.6 4.2 %shard_map.134 = (f32[128,4096]{1,0:T(8,128)S(1)}, f32[128,512]{1,0:T(8,128)S(1)}) custom-call(f32[128,512]{1,0:T(8,128)S(1)} %bitcast.35, f32[128,4096]{1,0:T(8,128)S(1)} %get-tuple-element.48.x_ref, f32[128,32]{1,0:T(8,128)S(1)} %convert_multiply_fusion.gain_ref, ...), custom_call_target="tpu_custom_call", output_to_operand_aliasing={{0}: (1, {})} | custom-call | flops 1073741824 | bytes 17776640 | tf_op jit(solution)/shard_map/pallas_call | solution.py:30
  149.7 11.4 %all_to_all.98 = f32[16,8,512]{2,1,0:T(8,128)S(1)} all-to-all(f32[16,8,512]{2,1,0:T(8,128)S(1)} %bitcast.45), channel_id=1, replica_groups=mesh['x'=4,'core'=2,'z'=4,'y'=4] {'z','y'}, dimensions={0} | all-to-all | bytes 524288 | tf_op jit(solution)/shard_map/all_to_all | solution.py:255
  161.2 11.9 %all_to_all.99 = f32[16,8,512]{2,1,0:T(8,128)S(1)} all-to-all(f32[16,8,512]{2,1,0:T(8,128)S(1)} %broadcast_in_dim.27), channel_id=1, replica_groups=mesh['x'=4,'core'=2,'z'=4,'y'=4] {'z','y'}, dimensions={0} | all-to-all | bytes 524288 | tf_op jit(solution)/shard_map/all_to_all | solution.py:248
  173.1 4.2 %shard_map.135 = (f32[128,4096]{1,0:T(8,128)S(1)}, f32[128,512]{1,0:T(8,128)S(1)}) custom-call(f32[128,512]{1,0:T(8,128)S(1)} %bitcast.36, f32[128,4096]{1,0:T(8,128)S(1)} %get-tuple-element.50.x_ref, f32[128,32]{1,0:T(8,128)S(1)} %convert_multiply_fusion.gain_ref, ...), custom_call_target="tpu_custom_call", output_to_operand_aliasing={{0}: (1, {})} | custom-call | flops 1073741824 | bytes 17776640 | tf_op jit(solution)/shard_map/pallas_call | solution.py:30
  177.3 11.6 %all_to_all.100 = f32[16,8,512]{2,1,0:T(8,128)S(1)} all-to-all(f32[16,8,512]{2,1,0:T(8,128)S(1)} %bitcast.46), channel_id=1, replica_groups=mesh['x'=4,'core'=2,'z'=4,'y'=4] {'z','y'}, dimensions={0} | all-to-all | bytes 524288 | tf_op jit(solution)/shard_map/all_to_all | solution.py:255
  188.9 11.6 %all_to_all.101 = f32[16,8,512]{2,1,0:T(8,128)S(1)} all-to-all(f32[16,8,512]{2,1,0:T(8,128)S(1)} %broadcast_in_dim.28), channel_id=1, replica_groups=mesh['x'=4,'core'=2,'z'=4,'y'=4] {'z','y'}, dimensions={0} | all-to-all | bytes 524288 | tf_op jit(solution)/shard_map/all_to_all | solution.py:248
  200.5 0.0 copy-start.3
  200.5 4.2 %shard_map.136 = (f32[128,4096]{1,0:T(8,128)S(1)}, f32[128,512]{1,0:T(8,128)S(1)}) custom-call(f32[128,512]{1,0:T(8,128)S(1)} %bitcast.37, f32[128,4096]{1,0:T(8,128)S(1)} %get-tuple-element.52.x_ref, f32[128,32]{1,0:T(8,128)S(1)} %convert_multiply_fusion.gain_ref, ...), custom_call_target="tpu_custom_call", output_to_operand_aliasing={{0}: (1, {})} | custom-call | flops 1073741824 | bytes 17776640 | tf_op jit(solution)/shard_map/pallas_call | solution.py:30
  204.7 11.6 %all_to_all.102 = f32[16,8,512]{2,1,0:T(8,128)S(1)} all-to-all(f32[16,8,512]{2,1,0:T(8,128)S(1)} %bitcast.47), channel_id=1, replica_groups=mesh['x'=4,'core'=2,'z'=4,'y'=4] {'z','y'}, dimensions={0} | all-to-all | bytes 524288 | tf_op jit(solution)/shard_map/all_to_all | solution.py:255
  216.4 11.6 %all_to_all.103 = f32[16,8,512]{2,1,0:T(8,128)S(1)} all-to-all(f32[16,8,512]{2,1,0:T(8,128)S(1)} %broadcast_in_dim.29), channel_id=1, replica_groups=mesh['x'=4,'core'=2,'z'=4,'y'=4] {'z','y'}, dimensions={0} | all-to-all | bytes 524288 | tf_op jit(solution)/shard_map/all_to_all | solution.py:248
  228.0 0.0 copy-done.3
  228.0 4.9 %shard_map.137 = (f32[128,4096]{1,0:T(8,128)S(1)}, f32[128,4096]{1,0:T(8,128)}, f32[34,128]{1,0:T(8,128)S(1)}) custom-call(f32[128,512]{1,0:T(8,128)S(1)} %bitcast.31, f32[128,4096]{1,0:T(8,128)S(1)} %get-tuple-element.54.x_ref, f32[128,32]{1,0:T(8,128)S(1)} %convert_multiply_fusion.gain_ref, ...), custom_call_target="tpu_custom_call", output_to_operand_aliasing={{0}: (1, {})} | custom-call | flops 536870912 | bytes 19629568 | tf_op jit(solution)/shard_map/pallas_call | solution.py:30
  232.9 10.6 %all_to_all.104.all_ref = f32[8,34,128]{2,1,0:T(8,128)S(1)} all-to-all(f32[8,34,128]{2,1,0:T(8,128)S(1)} %broadcast_in_dim.32), channel_id=1, replica_groups=mesh['x'=4,'core'=2,'z'=4,'y'=4] {'x','core'}, dimensions={0} | all-to-all | bytes 278528 | tf_op jit(solution)/shard_map/all_to_all | solution.py:248
  243.5 0.8 shard_map.138
  244.3 3.5 %all-to-all-start.17 = ((f32[16,8,128]{2,1,0:T(8,128)}), f32[16,8,128]{2,1,0:T(8,128)S(1)}, u32[]{:S(2)}, u32[]{:S(2)}) async-start(f32[16,8,128]{2,1,0:T(8,128)} %get-tuple-element.59), calls=%async_computation.17 | async-start | bytes 131072 | tf_op jit(solution)/shard_map/all_to_all | solution.py:340
  247.8 0.7 copy.27
  248.5 6.9 %all-to-all-done.17.parts_ref = f32[16,8,128]{2,1,0:T(8,128)S(1)} async-done(((f32[16,8,128]{2,1,0:T(8,128)}), f32[16,8,128]{2,1,0:T(8,128)S(1)}, u32[]{:S(2)}, u32[]{:S(2)}) %all-to-all-start.17) | async-done | bytes 65568 | tf_op jit(solution)/shard_map/all_to_all | solution.py:340
  255.4 3.1 %shard_map.139 = (f32[128,4096]{1,0:T(8,128)}, f32[1,1]{1,0:T(1,128)}, f32[1,1]{1,0:T(1,128)}) custom-call(s32[1]{0:T(128)} %bitcast.18.node_ref, f32[128,4096]{1,0:T(8,128)S(1)} %get-tuple-element.56.x_ref, f32[4,32,128]{2,1,0:T(8,128)S(1)} %get-tuple-element.58.means_ref, f32[16,8,128]{2,1,0:T(8,128)S(1)} %all-to-all-done.17.parts_ref, f32[128,4096]{1,0:T(8,128)} %mult_far.3), custom_call_target="tpu_custom_call" | custom-call | flops 1572864 | bytes 6422540 | tf_op jit(solution)/shard_map/pallas_call | solution.py:30
  (28 shorter events, 0.4 us)
Async XLA Ops:
  0.6 12.3 %copy-start = (f32[128,512]{1,0:T(8,128)S(1)}, f32[128,512]{1,0:T(8,128)}, u32[]{:S(2)}) copy-start(f32[128,512]{1,0:T(8,128)} %param.13) | copy-start | bytes 786436
  0.6 12.3 %copy-start.4 = (f32[4,4096]{1,0:T(4,128)S(1)}, f32[4,4096]{1,0:T(4,128)}, u32[]{:S(2)}) copy-start(f32[4,4096]{1,0:T(4,128)} %param.16) | copy-start | bytes 196612
  0.7 25.2 %copy-start.5 = (s32[128,32]{0,1:T(8,128)S(1)}, s32[128,32]{0,1:T(8,128)}, u32[]{:S(2)}) copy-start(s32[128,32]{0,1:T(8,128)} %param.17) | copy-start | bytes 49156
  4.7 16.8 %all-to-all-start = ((f32[16,8,512]{2,1,0:T(8,128)}), f32[16,8,512]{2,1,0:T(8,128)S(1)}, u32[]{:S(2)}, u32[]{:S(2)}) async-start(f32[16,8,512]{2,1,0:T(8,128)} %bitcast), calls=%async_computation | async-start | bytes 524288 | tf_op jit(solution)/shard_map/all_to_all | solution.py:255
  22.3 12.2 %all-to-all-start.1 = ((f32[16,8,512]{2,1,0:T(8,128)}), f32[16,8,512]{2,1,0:T(8,128)S(1)}, u32[]{:S(2)}, u32[]{:S(2)}) async-start(f32[16,8,512]{2,1,0:T(8,128)} %broadcast_in_dim.22), calls=%async_computation.1 | async-start | bytes 524288 | tf_op jit(solution)/shard_map/all_to_all | solution.py:248
  26.0 1.2 copy-start.1
  27.2 1.2 copy-start.2
  200.5 27.4 %copy-start.3 = (f32[128]{0:T(128)S(1)}, f32[128]{0:T(128)}, u32[]{:S(2)}) copy-start(f32[128]{0:T(128)} %param.15) | copy-start | bytes 1540
  244.3 11.1 %all-to-all-start.17 = ((f32[16,8,128]{2,1,0:T(8,128)}), f32[16,8,128]{2,1,0:T(8,128)S(1)}, u32[]{:S(2)}, u32[]{:S(2)}) async-start(f32[16,8,128]{2,1,0:T(8,128)} %get-tuple-element.59), calls=%async_computation.17 | async-start | bytes 131072 | tf_op jit(solution)/shard_map/all_to_all | solution.py:340

commit v5 on v4

--- a/solution.py
+++ b/solution.py
@@ -24,7 +24,7 @@
 ROOM = 50 << 20
 
 
-def local_call(body, outs, args, flops=0, scalar_in=(), far_in=(), far_out=(), scratch=(), aliases=None):
+def local_call(body, outs, args, flops=0, scalar_in=(), far_in=(), far_out=(), scratch=(), aliases=None, room=ROOM):
     outs = [s if isinstance(s, jax.ShapeDtypeStruct) else jax.ShapeDtypeStruct(s, jnp.float32) for s in outs]
     moved = sum(a.size * a.dtype.itemsize for a in args) + sum(o.size * o.dtype.itemsize for o in outs)
     return pl.pallas_call(
@@ -34,7 +34,7 @@
         out_specs=[FAR if k in far_out else WHOLE for k in range(len(outs))],
         scratch_shapes=list(scratch),
         input_output_aliases=aliases or {},
-        compiler_params=pltpu.CompilerParams(vmem_limit_bytes=ROOM),
+        compiler_params=pltpu.CompilerParams(vmem_limit_bytes=room),
         cost_estimate=pl.CostEstimate(flops=flops, bytes_accessed=moved, transcendentals=0),
     )(*args)
 
@@ -304,6 +304,7 @@
         2 * rows * width,
         far_in=(0, 1, 2),
         far_out=(0, 1),
+        room=52 << 20,
         scratch=landing(multipliers) + 2 * landing(cost) + landing(multipliers) + [spread_over],
     )
     far = [technology, linear, curvature_far]

time: 260 us -> 258 us (level)
  no operation moved by 1% of the time
where the time goes in v5:
time: 258 us; the launch traced here: 257 us
  blocking collectives  173 us (67%)
  Pallas kernels  45.1 us (17%)
  waiting for transfers between devices  19.7 us (8%)
  starting transfers between devices  15.2 us (6%)
  local copies, waits for them, and re-layouts  2.91 us (1%)
    all_to_all x8, blocking collectives, to_all(): lax.all_to_all(jnp.broadcast_to(x[None], (devices, *x.shape)), axes, 0, 0...  91.9 us
    all_to_all x7, blocking collectives, excess_of(): arrived = lax.all_to_all(pieces, axes, 0, 0, tiled=True)  81.2 us
    pallas_call x12, Pallas kernels, local_call(): pl.pallas_call(body, out_shape=outs, in_specs=[SMALL if k in scalar_in el...  45.1 us
    all_to_all x1, waiting for transfers between devices, excess_of(): arrived = lax.all_to_all(pieces, axes, 0, 0, tiled=True)  8.61 us
    all_to_all x1, starting transfers between devices, excess_of(): arrived = lax.all_to_all(pieces, axes, 0, 0, tiled=True)  8.14 us
    all_to_all x1, waiting for transfers between devices, shards(): parts = lax.all_to_all(parts, VAR, 0, 0, tiled=True)  6.93 us
  transfers between devices with their start and end apart: 3, of which 3 were waited for; matrix products, arithmetic and copies ran while one was open for 0% of the time, Pallas kernels for 1%

profile of v5, /device:TPU:0, one launch (start us, length us, event | category | flops | bytes accessed | tf_op | source)
XLA Modules:
  0.0 257.4 jit_solution(13017949509663699343)
XLA Ops:
  0.6 0.0 copy-start
  0.6 0.0 copy-start.3
  0.7 0.0 copy-start.4
  0.7 4.1 %shard_map.128 = (f32[128,4096]{1,0:T(8,128)S(1)}, f32[128,512]{1,0:T(8,128)}, bf16[512,256]{1,0:T(8,128)(2,1)S(1)}) custom-call(f32[128,4096]{1,0:T(8,128)} %start_far.1, bf16[512,4096]{1,0:T(8,128)(2,1)} %tech_far.17), custom_call_target="tpu_custom_call" | custom-call | flops 536870912 | bytes 8912896 | tf_op jit(solution)/shard_map/pallas_call | solution.py:30
  4.7 8.1 %all-to-all-start = ((f32[16,8,512]{2,1,0:T(8,128)}), f32[16,8,512]{2,1,0:T(8,128)S(1)}, u32[]{:S(2)}, u32[]{:S(2)}) async-start(f32[16,8,512]{2,1,0:T(8,128)} %bitcast), calls=%async_computation | async-start | bytes 524288 | tf_op jit(solution)/shard_map/all_to_all | solution.py:255
  12.9 0.0 copy-done
  12.9 0.0 copy-done.3
  13.0 8.6 %all-to-all-done = f32[16,8,512]{2,1,0:T(8,128)S(1)} async-done(((f32[16,8,512]{2,1,0:T(8,128)}), f32[16,8,512]{2,1,0:T(8,128)S(1)}, u32[]{:S(2)}, u32[]{:S(2)}) %all-to-all-start) | async-done | bytes 262176 | tf_op jit(solution)/shard_map/all_to_all | solution.py:255
  21.6 0.7 broadcast_in_dim.22
  22.3 3.5 %all-to-all-start.1 = ((f32[16,8,512]{2,1,0:T(8,128)}), f32[16,8,512]{2,1,0:T(8,128)S(1)}, u32[]{:S(2)}, u32[]{:S(2)}) async-start(f32[16,8,512]{2,1,0:T(8,128)} %broadcast_in_dim.22), calls=%async_computation.1 | async-start | bytes 524288 | tf_op jit(solution)/shard_map/all_to_all | solution.py:248
  25.9 0.0 copy-done.4
  25.9 0.1 copy.22
  26.0 0.0 copy-start.1
  26.0 1.2 copy-done.1
  27.2 3.1 %shard_map.129 = (f32[256,4096]{1,0:T(8,128)}, bf16[512,4096]{1,0:T(8,128)(2,1)}, f32[128,256]{1,0:T(8,128)S(1)}, bf16[128,256]{1,0:T(8,128)(2,1)S(1)}) custom-call(f32[128,4096]{1,0:T(8,128)} %mult_far.3, bf16[128,4096]{1,0:T(8,128)(2,1)S(1)} %copy-done.1, bf16[128,4096]{1,0:T(8,128)(2,1)} %curv_far.1, f32[32,128]{1,0:T(8,128)S(1)} %dynamic-slice_bitcast_fusion.old_ref), custom_call_target="tpu_custom_call" | custom-call | flops 1048576 | bytes 12795904 | tf_op jit(solution)/shard_map/pallas_call | solution.py:30
  30.4 4.2 %all-to-all-done.1 = f32[16,8,512]{2,1,0:T(8,128)S(1)} async-done(((f32[16,8,512]{2,1,0:T(8,128)}), f32[16,8,512]{2,1,0:T(8,128)S(1)}, u32[]{:S(2)}, u32[]{:S(2)}) %all-to-all-start.1) | async-done | bytes 262176 | tf_op jit(solution)/shard_map/all_to_all | solution.py:248
  34.5 4.2 %shard_map.130 = (f32[128,4096]{1,0:T(8,128)S(1)}, f32[128,512]{1,0:T(8,128)S(1)}) custom-call(f32[128,512]{1,0:T(8,128)S(1)} %bitcast.30, f32[128,4096]{1,0:T(8,128)S(1)} %get-tuple-element.35.x_ref, f32[128,32]{1,0:T(8,128)S(1)} %convert_multiply_fusion.gain_ref, ...), custom_call_target="tpu_custom_call", output_to_operand_aliasing={{0}: (1, {})} | custom-call | flops 1073741824 | bytes 17776640 | tf_op jit(solution)/shard_map/pallas_call | solution.py:30
  38.7 11.6 %all_to_all.90 = f32[16,8,512]{2,1,0:T(8,128)S(1)} all-to-all(f32[16,8,512]{2,1,0:T(8,128)S(1)} %bitcast.41), channel_id=1, replica_groups=mesh['x'=4,'core'=2,'z'=4,'y'=4] {'z','y'}, dimensions={0} | all-to-all | bytes 524288 | tf_op jit(solution)/shard_map/all_to_all | solution.py:255
  50.4 11.6 %all_to_all.91 = f32[16,8,512]{2,1,0:T(8,128)S(1)} all-to-all(f32[16,8,512]{2,1,0:T(8,128)S(1)} %broadcast_in_dim.23), channel_id=1, replica_groups=mesh['x'=4,'core'=2,'z'=4,'y'=4] {'z','y'}, dimensions={0} | all-to-all | bytes 524288 | tf_op jit(solution)/shard_map/all_to_all | solution.py:248
  62.0 4.2 %shard_map.131 = (f32[128,4096]{1,0:T(8,128)S(1)}, f32[128,512]{1,0:T(8,128)S(1)}) custom-call(f32[128,512]{1,0:T(8,128)S(1)} %bitcast.32, f32[128,4096]{1,0:T(8,128)S(1)} %get-tuple-element.42.x_ref, f32[128,32]{1,0:T(8,128)S(1)} %convert_multiply_fusion.gain_ref, ...), custom_call_target="tpu_custom_call", output_to_operand_aliasing={{0}: (1, {})} | custom-call | flops 1073741824 | bytes 17776640 | tf_op jit(solution)/shard_map/pallas_call | solution.py:30
  66.1 11.6 %all_to_all.92 = f32[16,8,512]{2,1,0:T(8,128)S(1)} all-to-all(f32[16,8,512]{2,1,0:T(8,128)S(1)} %bitcast.42), channel_id=1, replica_groups=mesh['x'=4,'core'=2,'z'=4,'y'=4] {'z','y'}, dimensions={0} | all-to-all | bytes 524288 | tf_op jit(solution)/shard_map/all_to_all | solution.py:255
  77.8 11.6 %all_to_all.93 = f32[16,8,512]{2,1,0:T(8,128)S(1)} all-to-all(f32[16,8,512]{2,1,0:T(8,128)S(1)} %broadcast_in_dim.24), channel_id=1, replica_groups=mesh['x'=4,'core'=2,'z'=4,'y'=4] {'z','y'}, dimensions={0} | all-to-all | bytes 524288 | tf_op jit(solution)/shard_map/all_to_all | solution.py:248
  89.4 4.2 %shard_map.132 = (f32[128,4096]{1,0:T(8,128)S(1)}, f32[128,512]{1,0:T(8,128)S(1)}) custom-call(f32[128,512]{1,0:T(8,128)S(1)} %bitcast.33, f32[128,4096]{1,0:T(8,128)S(1)} %get-tuple-element.44.x_ref, f32[128,32]{1,0:T(8,128)S(1)} %convert_multiply_fusion.gain_ref, ...), custom_call_target="tpu_custom_call", output_to_operand_aliasing={{0}: (1, {})} | custom-call | flops 1073741824 | bytes 17776640 | tf_op jit(solution)/shard_map/pallas_call | solution.py:30
  93.6 11.6 %all_to_all.94 = f32[16,8,512]{2,1,0:T(8,128)S(1)} all-to-all(f32[16,8,512]{2,1,0:T(8,128)S(1)} %bitcast.43), channel_id=1, replica_groups=mesh['x'=4,'core'=2,'z'=4,'y'=4] {'z','y'}, dimensions={0} | all-to-all | bytes 524288 | tf_op jit(solution)/shard_map/all_to_all | solution.py:255
  105.2 11.6 %all_to_all.95 = f32[16,8,512]{2,1,0:T(8,128)S(1)} all-to-all(f32[16,8,512]{2,1,0:T(8,128)S(1)} %broadcast_in_dim.25), channel_id=1, replica_groups=mesh['x'=4,'core'=2,'z'=4,'y'=4] {'z','y'}, dimensions={0} | all-to-all | bytes 524288 | tf_op jit(solution)/shard_map/all_to_all | solution.py:248
  116.8 4.2 %shard_map.133 = (f32[128,4096]{1,0:T(8,128)S(1)}, f32[128,512]{1,0:T(8,128)S(1)}) custom-call(f32[128,512]{1,0:T(8,128)S(1)} %bitcast.34, f32[128,4096]{1,0:T(8,128)S(1)} %get-tuple-element.46.x_ref, f32[128,32]{1,0:T(8,128)S(1)} %convert_multiply_fusion.gain_ref, ...), custom_call_target="tpu_custom_call", output_to_operand_aliasing={{0}: (1, {})} | custom-call | flops 1073741824 | bytes 17776640 | tf_op jit(solution)/shard_map/pallas_call | solution.py:30
  121.0 11.7 %all_to_all.96 = f32[16,8,512]{2,1,0:T(8,128)S(1)} all-to-all(f32[16,8,512]{2,1,0:T(8,128)S(1)} %bitcast.44), channel_id=1, replica_groups=mesh['x'=4,'core'=2,'z'=4,'y'=4] {'z','y'}, dimensions={0} | all-to-all | bytes 524288 | tf_op jit(solution)/shard_map/all_to_all | solution.py:255
  132.7 11.6 %all_to_all.97 = f32[16,8,512]{2,1,0:T(8,128)S(1)} all-to-all(f32[16,8,512]{2,1,0:T(8,128)S(1)} %broadcast_in_dim.26), channel_id=1, replica_groups=mesh['x'=4,'core'=2,'z'=4,'y'=4] {'z','y'}, dimensions={0} | all-to-all | bytes 524288 | tf_op jit(solution)/shard_map/all_to_all | solution.py:248
  144.4 4.2 %shard_map.134 = (f32[128,4096]{1,0:T(8,128)S(1)}, f32[128,512]{1,0:T(8,128)S(1)}) custom-call(f32[128,512]{1,0:T(8,128)S(1)} %bitcast.35, f32[128,4096]{1,0:T(8,128)S(1)} %get-tuple-element.48.x_ref, f32[128,32]{1,0:T(8,128)S(1)} %convert_multiply_fusion.gain_ref, ...), custom_call_target="tpu_custom_call", output_to_operand_aliasing={{0}: (1, {})} | custom-call | flops 1073741824 | bytes 17776640 | tf_op jit(solution)/shard_map/pallas_call | solution.py:30
  148.5 11.6 %all_to_all.98 = f32[16,8,512]{2,1,0:T(8,128)S(1)} all-to-all(f32[16,8,512]{2,1,0:T(8,128)S(1)} %bitcast.45), channel_id=1, replica_groups=mesh['x'=4,'core'=2,'z'=4,'y'=4] {'z','y'}, dimensions={0} | all-to-all | bytes 524288 | tf_op jit(solution)/shard_map/all_to_all | solution.py:255
  160.2 11.8 %all_to_all.99 = f32[16,8,512]{2,1,0:T(8,128)S(1)} all-to-all(f32[16,8,512]{2,1,0:T(8,128)S(1)} %broadcast_in_dim.27), channel_id=1, replica_groups=mesh['x'=4,'core'=2,'z'=4,'y'=4] {'z','y'}, dimensions={0} | all-to-all | bytes 524288 | tf_op jit(solution)/shard_map/all_to_all | solution.py:248
  171.9 4.2 %shard_map.135 = (f32[128,4096]{1,0:T(8,128)S(1)}, f32[128,512]{1,0:T(8,128)S(1)}) custom-call(f32[128,512]{1,0:T(8,128)S(1)} %bitcast.36, f32[128,4096]{1,0:T(8,128)S(1)} %get-tuple-element.50.x_ref, f32[128,32]{1,0:T(8,128)S(1)} %convert_multiply_fusion.gain_ref, ...), custom_call_target="tpu_custom_call", output_to_operand_aliasing={{0}: (1, {})} | custom-call | flops 1073741824 | bytes 17776640 | tf_op jit(solution)/shard_map/pallas_call | solution.py:30
  176.1 11.6 %all_to_all.100 = f32[16,8,512]{2,1,0:T(8,128)S(1)} all-to-all(f32[16,8,512]{2,1,0:T(8,128)S(1)} %bitcast.46), channel_id=1, replica_groups=mesh['x'=4,'core'=2,'z'=4,'y'=4] {'z','y'}, dimensions={0} | all-to-all | bytes 524288 | tf_op jit(solution)/shard_map/all_to_all | solution.py:255
  187.7 11.6 %all_to_all.101 = f32[16,8,512]{2,1,0:T(8,128)S(1)} all-to-all(f32[16,8,512]{2,1,0:T(8,128)S(1)} %broadcast_in_dim.28), channel_id=1, replica_groups=mesh['x'=4,'core'=2,'z'=4,'y'=4] {'z','y'}, dimensions={0} | all-to-all | bytes 524288 | tf_op jit(solution)/shard_map/all_to_all | solution.py:248
  199.3 0.0 copy-start.2
  199.3 4.2 %shard_map.136 = (f32[128,4096]{1,0:T(8,128)S(1)}, f32[128,512]{1,0:T(8,128)S(1)}) custom-call(f32[128,512]{1,0:T(8,128)S(1)} %bitcast.37, f32[128,4096]{1,0:T(8,128)S(1)} %get-tuple-element.52.x_ref, f32[128,32]{1,0:T(8,128)S(1)} %convert_multiply_fusion.gain_ref, ...), custom_call_target="tpu_custom_call", output_to_operand_aliasing={{0}: (1, {})} | custom-call | flops 1073741824 | bytes 17776640 | tf_op jit(solution)/shard_map/pallas_call | solution.py:30
  203.5 11.6 %all_to_all.102 = f32[16,8,512]{2,1,0:T(8,128)S(1)} all-to-all(f32[16,8,512]{2,1,0:T(8,128)S(1)} %bitcast.47), channel_id=1, replica_groups=mesh['x'=4,'core'=2,'z'=4,'y'=4] {'z','y'}, dimensions={0} | all-to-all | bytes 524288 | tf_op jit(solution)/shard_map/all_to_all | solution.py:255
  215.2 11.6 %all_to_all.103 = f32[16,8,512]{2,1,0:T(8,128)S(1)} all-to-all(f32[16,8,512]{2,1,0:T(8,128)S(1)} %broadcast_in_dim.29), channel_id=1, replica_groups=mesh['x'=4,'core'=2,'z'=4,'y'=4] {'z','y'}, dimensions={0} | all-to-all | bytes 524288 | tf_op jit(solution)/shard_map/all_to_all | solution.py:248
  226.8 0.0 copy-done.2
  226.8 4.9 %shard_map.137 = (f32[128,4096]{1,0:T(8,128)S(1)}, f32[128,4096]{1,0:T(8,128)}, f32[34,128]{1,0:T(8,128)S(1)}) custom-call(f32[128,512]{1,0:T(8,128)S(1)} %bitcast.31, f32[128,4096]{1,0:T(8,128)S(1)} %get-tuple-element.54.x_ref, f32[128,32]{1,0:T(8,128)S(1)} %convert_multiply_fusion.gain_ref, ...), custom_call_target="tpu_custom_call", output_to_operand_aliasing={{0}: (1, {})} | custom-call | flops 536870912 | bytes 19629568 | tf_op jit(solution)/shard_map/pallas_call | solution.py:30
  231.7 10.6 %all_to_all.104.all_ref = f32[8,34,128]{2,1,0:T(8,128)S(1)} all-to-all(f32[8,34,128]{2,1,0:T(8,128)S(1)} %broadcast_in_dim.32), channel_id=1, replica_groups=mesh['x'=4,'core'=2,'z'=4,'y'=4] {'x','core'}, dimensions={0} | all-to-all | bytes 278528 | tf_op jit(solution)/shard_map/all_to_all | solution.py:248
  242.3 0.8 shard_map.138
  243.1 3.5 %all-to-all-start.17 = ((f32[16,8,128]{2,1,0:T(8,128)}), f32[16,8,128]{2,1,0:T(8,128)S(1)}, u32[]{:S(2)}, u32[]{:S(2)}) async-start(f32[16,8,128]{2,1,0:T(8,128)} %get-tuple-element.59), calls=%async_computation.17 | async-start | bytes 131072 | tf_op jit(solution)/shard_map/all_to_all | solution.py:341
  246.6 0.7 copy.27
  247.2 6.9 %all-to-all-done.17.parts_ref = f32[16,8,128]{2,1,0:T(8,128)S(1)} async-done(((f32[16,8,128]{2,1,0:T(8,128)}), f32[16,8,128]{2,1,0:T(8,128)S(1)}, u32[]{:S(2)}, u32[]{:S(2)}) %all-to-all-start.17) | async-done | bytes 65568 | tf_op jit(solution)/shard_map/all_to_all | solution.py:341
  254.2 3.1 %shard_map.139 = (f32[128,4096]{1,0:T(8,128)}, f32[1,1]{1,0:T(1,128)}, f32[1,1]{1,0:T(1,128)}) custom-call(s32[1]{0:T(128)} %bitcast.18.node_ref, f32[128,4096]{1,0:T(8,128)S(1)} %get-tuple-element.56.x_ref, f32[4,32,128]{2,1,0:T(8,128)S(1)} %get-tuple-element.58.means_ref, f32[16,8,128]{2,1,0:T(8,128)S(1)} %all-to-all-done.17.parts_ref, f32[128,4096]{1,0:T(8,128)} %mult_far.3), custom_call_target="tpu_custom_call" | custom-call | flops 1572864 | bytes 6422540 | tf_op jit(solution)/shard_map/pallas_call | solution.py:30
  (28 shorter events, 0.4 us)
Async XLA Ops:
  0.6 12.3 %copy-start = (f32[128,512]{1,0:T(8,128)S(1)}, f32[128,512]{1,0:T(8,128)}, u32[]{:S(2)}) copy-start(f32[128,512]{1,0:T(8,128)} %param.13) | copy-start | bytes 786436
  0.6 12.3 %copy-start.3 = (f32[4,4096]{1,0:T(4,128)S(1)}, f32[4,4096]{1,0:T(4,128)}, u32[]{:S(2)}) copy-start(f32[4,4096]{1,0:T(4,128)} %param.16) | copy-start | bytes 196612
  0.7 25.2 %copy-start.4 = (s32[128,32]{0,1:T(8,128)S(1)}, s32[128,32]{0,1:T(8,128)}, u32[]{:S(2)}) copy-start(s32[128,32]{0,1:T(8,128)} %param.17) | copy-start | bytes 49156
  4.7 16.8 %all-to-all-start = ((f32[16,8,512]{2,1,0:T(8,128)}), f32[16,8,512]{2,1,0:T(8,128)S(1)}, u32[]{:S(2)}, u32[]{:S(2)}) async-start(f32[16,8,512]{2,1,0:T(8,128)} %bitcast), calls=%async_computation | async-start | bytes 524288 | tf_op jit(solution)/shard_map/all_to_all | solution.py:255
  22.3 12.2 %all-to-all-start.1 = ((f32[16,8,512]{2,1,0:T(8,128)}), f32[16,8,512]{2,1,0:T(8,128)S(1)}, u32[]{:S(2)}, u32[]{:S(2)}) async-start(f32[16,8,512]{2,1,0:T(8,128)} %broadcast_in_dim.22), calls=%async_computation.1 | async-start | bytes 524288 | tf_op jit(solution)/shard_map/all_to_all | solution.py:248
  26.0 1.2 copy-start.1
  199.3 27.4 %copy-start.2 = (f32[128]{0:T(128)S(1)}, f32[128]{0:T(128)}, u32[]{:S(2)}) copy-start(f32[128]{0:T(128)} %param.15) | copy-start | bytes 1540
  243.1 11.1 %all-to-all-start.17 = ((f32[16,8,128]{2,1,0:T(8,128)}), f32[16,8,128]{2,1,0:T(8,128)S(1)}, u32[]{:S(2)}, u32[]{:S(2)}) async-start(f32[16,8,128]{2,1,0:T(8,128)} %get-tuple-element.59), calls=%async_computation.17 | async-start | bytes 131072 | tf_op jit(solution)/shard_map/all_to_all | solution.py:341

commit v6 on v5

--- a/solution.py
+++ b/solution.py
@@ -60,10 +60,14 @@
         for copy in row:
             copy.start()
         copies.append(row)
-    for k, row in enumerate(copies):
-        for copy in row:
-            copy.wait()
-        yield k, cols_of(k)
+
+    def arrivals():
+        for k, row in enumerate(copies):
+            for copy in row:
+                copy.wait()
+            yield k, cols_of(k)
+
+    return arrivals()
 
 
 def image_of(x, tech):
@@ -222,18 +226,17 @@
     node_ref, x_ref, means_ref, parts_ref, mult_far, out_far, primal_ref, dual_ref,
     mult_near, mult_sem, out_near, out_sem,
 ):
-    factor = None
+    arrivals = spans((mult_far, mult_near, mult_sem))
+    sums = jnp.sum(parts_ref[...], axis=0)[0:1, :]
+    normaliser = parts_ref[0, 0:1, 2:3] * V
+    primal = jnp.sqrt(sums[:, 0:1] / normaliser + epsilon)
+    dual = penalty * jnp.sqrt(sums[:, 1:2] / normaliser + epsilon)
+    factor = penalty * jnp.sqrt(primal / dual)
+    primal_ref[...] = primal
+    dual_ref[...] = dual
+    mean = means_ref[node_ref[0]]
     outs = []
-    for k, cols in spans((mult_far, mult_near, mult_sem)):
-        if factor is None:
-            sums = jnp.sum(parts_ref[...], axis=0)[0:1, :]
-            normaliser = parts_ref[0, 0:1, 2:3] * V
-            primal = jnp.sqrt(sums[:, 0:1] / normaliser + epsilon)
-            dual = penalty * jnp.sqrt(sums[:, 1:2] / normaliser + epsilon)
-            factor = penalty * jnp.sqrt(primal / dual)
-            primal_ref[...] = primal
-            dual_ref[...] = dual
-            mean = means_ref[node_ref[0]]
+    for k, cols in arrivals:
         for b, block in per_lane_block(cols):
             out_near[:, block] = mult_near[:, block] + factor * (x_ref[:, block] - mean[b : b + 1, :])
         out = pltpu.make_async_copy(out_near.at[:, cols], out_far.at[:, cols], out_sem.at[k])

time: 258 us -> 258 us (level)
  no operation moved by 1% of the time
where the time goes in v6:
time: 258 us; the launch traced here: 257 us
  blocking collectives  173 us (67%)
  Pallas kernels  45.1 us (17%)
  waiting for transfers between devices  19.7 us (8%)
  starting transfers between devices  15.2 us (6%)
  local copies, waits for them, and re-layouts  2.91 us (1%)
    all_to_all x8, blocking collectives, to_all(): lax.all_to_all(jnp.broadcast_to(x[None], (devices, *x.shape)), axes, 0, 0...  91.9 us
    all_to_all x7, blocking collectives, excess_of(): arrived = lax.all_to_all(pieces, axes, 0, 0, tiled=True)  81.2 us
    pallas_call x12, Pallas kernels, local_call(): pl.pallas_call(body, out_shape=outs, in_specs=[SMALL if k in scalar_in el...  45.1 us
    all_to_all x1, waiting for transfers between devices, excess_of(): arrived = lax.all_to_all(pieces, axes, 0, 0, tiled=True)  8.61 us
    all_to_all x1, starting transfers between devices, excess_of(): arrived = lax.all_to_all(pieces, axes, 0, 0, tiled=True)  8.14 us
    all_to_all x1, waiting for transfers between devices, shards(): parts = lax.all_to_all(parts, VAR, 0, 0, tiled=True)  6.93 us
  transfers between devices with their start and end apart: 3, of which 3 were waited for; matrix products, arithmetic and copies ran while one was open for 0% of the time, Pallas kernels for 1%

profile of v6, /device:TPU:0, one launch (start us, length us, event | category | flops | bytes accessed | tf_op | source)
XLA Modules:
  0.0 257.4 jit_solution(15990353613618440526)
XLA Ops:
  0.6 0.0 copy-start
  0.6 0.0 copy-start.3
  0.7 0.0 copy-start.4
  0.7 4.1 %shard_map.128 = (f32[128,4096]{1,0:T(8,128)S(1)}, f32[128,512]{1,0:T(8,128)}, bf16[512,256]{1,0:T(8,128)(2,1)S(1)}) custom-call(f32[128,4096]{1,0:T(8,128)} %start_far.1, bf16[512,4096]{1,0:T(8,128)(2,1)} %tech_far.17), custom_call_target="tpu_custom_call" | custom-call | flops 536870912 | bytes 8912896 | tf_op jit(solution)/shard_map/pallas_call | solution.py:30
  4.7 8.1 %all-to-all-start = ((f32[16,8,512]{2,1,0:T(8,128)}), f32[16,8,512]{2,1,0:T(8,128)S(1)}, u32[]{:S(2)}, u32[]{:S(2)}) async-start(f32[16,8,512]{2,1,0:T(8,128)} %bitcast), calls=%async_computation | async-start | bytes 524288 | tf_op jit(solution)/shard_map/all_to_all | solution.py:258
  12.9 0.0 copy-done
  12.9 0.0 copy-done.3
  13.0 8.6 %all-to-all-done = f32[16,8,512]{2,1,0:T(8,128)S(1)} async-done(((f32[16,8,512]{2,1,0:T(8,128)}), f32[16,8,512]{2,1,0:T(8,128)S(1)}, u32[]{:S(2)}, u32[]{:S(2)}) %all-to-all-start) | async-done | bytes 262176 | tf_op jit(solution)/shard_map/all_to_all | solution.py:258
  21.6 0.7 broadcast_in_dim.22
  22.3 3.5 %all-to-all-start.1 = ((f32[16,8,512]{2,1,0:T(8,128)}), f32[16,8,512]{2,1,0:T(8,128)S(1)}, u32[]{:S(2)}, u32[]{:S(2)}) async-start(f32[16,8,512]{2,1,0:T(8,128)} %broadcast_in_dim.22), calls=%async_computation.1 | async-start | bytes 524288 | tf_op jit(solution)/shard_map/all_to_all | solution.py:251
  25.9 0.0 copy-done.4
  25.9 0.1 copy.22
  26.0 0.0 copy-start.1
  26.0 1.2 copy-done.1
  27.2 3.1 %shard_map.129 = (f32[256,4096]{1,0:T(8,128)}, bf16[512,4096]{1,0:T(8,128)(2,1)}, f32[128,256]{1,0:T(8,128)S(1)}, bf16[128,256]{1,0:T(8,128)(2,1)S(1)}) custom-call(f32[128,4096]{1,0:T(8,128)} %mult_far.3, bf16[128,4096]{1,0:T(8,128)(2,1)S(1)} %copy-done.1, bf16[128,4096]{1,0:T(8,128)(2,1)} %curv_far.1, f32[32,128]{1,0:T(8,128)S(1)} %dynamic-slice_bitcast_fusion.old_ref), custom_call_target="tpu_custom_call" | custom-call | flops 1048576 | bytes 12795904 | tf_op jit(solution)/shard_map/pallas_call | solution.py:30
  30.4 4.2 %all-to-all-done.1 = f32[16,8,512]{2,1,0:T(8,128)S(1)} async-done(((f32[16,8,512]{2,1,0:T(8,128)}), f32[16,8,512]{2,1,0:T(8,128)S(1)}, u32[]{:S(2)}, u32[]{:S(2)}) %all-to-all-start.1) | async-done | bytes 262176 | tf_op jit(solution)/shard_map/all_to_all | solution.py:251
  34.5 4.2 %shard_map.130 = (f32[128,4096]{1,0:T(8,128)S(1)}, f32[128,512]{1,0:T(8,128)S(1)}) custom-call(f32[128,512]{1,0:T(8,128)S(1)} %bitcast.30, f32[128,4096]{1,0:T(8,128)S(1)} %get-tuple-element.35.x_ref, f32[128,32]{1,0:T(8,128)S(1)} %convert_multiply_fusion.gain_ref, ...), custom_call_target="tpu_custom_call", output_to_operand_aliasing={{0}: (1, {})} | custom-call | flops 1073741824 | bytes 17776640 | tf_op jit(solution)/shard_map/pallas_call | solution.py:30
  38.7 11.6 %all_to_all.90 = f32[16,8,512]{2,1,0:T(8,128)S(1)} all-to-all(f32[16,8,512]{2,1,0:T(8,128)S(1)} %bitcast.41), channel_id=1, replica_groups=mesh['x'=4,'core'=2,'z'=4,'y'=4] {'z','y'}, dimensions={0} | all-to-all | bytes 524288 | tf_op jit(solution)/shard_map/all_to_all | solution.py:258
  50.4 11.6 %all_to_all.91 = f32[16,8,512]{2,1,0:T(8,128)S(1)} all-to-all(f32[16,8,512]{2,1,0:T(8,128)S(1)} %broadcast_in_dim.23), channel_id=1, replica_groups=mesh['x'=4,'core'=2,'z'=4,'y'=4] {'z','y'}, dimensions={0} | all-to-all | bytes 524288 | tf_op jit(solution)/shard_map/all_to_all | solution.py:251
  62.0 4.2 %shard_map.131 = (f32[128,4096]{1,0:T(8,128)S(1)}, f32[128,512]{1,0:T(8,128)S(1)}) custom-call(f32[128,512]{1,0:T(8,128)S(1)} %bitcast.32, f32[128,4096]{1,0:T(8,128)S(1)} %get-tuple-element.42.x_ref, f32[128,32]{1,0:T(8,128)S(1)} %convert_multiply_fusion.gain_ref, ...), custom_call_target="tpu_custom_call", output_to_operand_aliasing={{0}: (1, {})} | custom-call | flops 1073741824 | bytes 17776640 | tf_op jit(solution)/shard_map/pallas_call | solution.py:30
  66.1 11.6 %all_to_all.92 = f32[16,8,512]{2,1,0:T(8,128)S(1)} all-to-all(f32[16,8,512]{2,1,0:T(8,128)S(1)} %bitcast.42), channel_id=1, replica_groups=mesh['x'=4,'core'=2,'z'=4,'y'=4] {'z','y'}, dimensions={0} | all-to-all | bytes 524288 | tf_op jit(solution)/shard_map/all_to_all | solution.py:258
  77.8 11.6 %all_to_all.93 = f32[16,8,512]{2,1,0:T(8,128)S(1)} all-to-all(f32[16,8,512]{2,1,0:T(8,128)S(1)} %broadcast_in_dim.24), channel_id=1, replica_groups=mesh['x'=4,'core'=2,'z'=4,'y'=4] {'z','y'}, dimensions={0} | all-to-all | bytes 524288 | tf_op jit(solution)/shard_map/all_to_all | solution.py:251
  89.4 4.2 %shard_map.132 = (f32[128,4096]{1,0:T(8,128)S(1)}, f32[128,512]{1,0:T(8,128)S(1)}) custom-call(f32[128,512]{1,0:T(8,128)S(1)} %bitcast.33, f32[128,4096]{1,0:T(8,128)S(1)} %get-tuple-element.44.x_ref, f32[128,32]{1,0:T(8,128)S(1)} %convert_multiply_fusion.gain_ref, ...), custom_call_target="tpu_custom_call", output_to_operand_aliasing={{0}: (1, {})} | custom-call | flops 1073741824 | bytes 17776640 | tf_op jit(solution)/shard_map/pallas_call | solution.py:30
  93.6 11.6 %all_to_all.94 = f32[16,8,512]{2,1,0:T(8,128)S(1)} all-to-all(f32[16,8,512]{2,1,0:T(8,128)S(1)} %bitcast.43), channel_id=1, replica_groups=mesh['x'=4,'core'=2,'z'=4,'y'=4] {'z','y'}, dimensions={0} | all-to-all | bytes 524288 | tf_op jit(solution)/shard_map/all_to_all | solution.py:258
  105.2 11.6 %all_to_all.95 = f32[16,8,512]{2,1,0:T(8,128)S(1)} all-to-all(f32[16,8,512]{2,1,0:T(8,128)S(1)} %broadcast_in_dim.25), channel_id=1, replica_groups=mesh['x'=4,'core'=2,'z'=4,'y'=4] {'z','y'}, dimensions={0} | all-to-all | bytes 524288 | tf_op jit(solution)/shard_map/all_to_all | solution.py:251
  116.8 4.2 %shard_map.133 = (f32[128,4096]{1,0:T(8,128)S(1)}, f32[128,512]{1,0:T(8,128)S(1)}) custom-call(f32[128,512]{1,0:T(8,128)S(1)} %bitcast.34, f32[128,4096]{1,0:T(8,128)S(1)} %get-tuple-element.46.x_ref, f32[128,32]{1,0:T(8,128)S(1)} %convert_multiply_fusion.gain_ref, ...), custom_call_target="tpu_custom_call", output_to_operand_aliasing={{0}: (1, {})} | custom-call | flops 1073741824 | bytes 17776640 | tf_op jit(solution)/shard_map/pallas_call | solution.py:30
  121.0 11.7 %all_to_all.96 = f32[16,8,512]{2,1,0:T(8,128)S(1)} all-to-all(f32[16,8,512]{2,1,0:T(8,128)S(1)} %bitcast.44), channel_id=1, replica_groups=mesh['x'=4,'core'=2,'z'=4,'y'=4] {'z','y'}, dimensions={0} | all-to-all | bytes 524288 | tf_op jit(solution)/shard_map/all_to_all | solution.py:258
  132.7 11.6 %all_to_all.97 = f32[16,8,512]{2,1,0:T(8,128)S(1)} all-to-all(f32[16,8,512]{2,1,0:T(8,128)S(1)} %broadcast_in_dim.26), channel_id=1, replica_groups=mesh['x'=4,'core'=2,'z'=4,'y'=4] {'z','y'}, dimensions={0} | all-to-all | bytes 524288 | tf_op jit(solution)/shard_map/all_to_all | solution.py:251
  144.4 4.2 %shard_map.134 = (f32[128,4096]{1,0:T(8,128)S(1)}, f32[128,512]{1,0:T(8,128)S(1)}) custom-call(f32[128,512]{1,0:T(8,128)S(1)} %bitcast.35, f32[128,4096]{1,0:T(8,128)S(1)} %get-tuple-element.48.x_ref, f32[128,32]{1,0:T(8,128)S(1)} %convert_multiply_fusion.gain_ref, ...), custom_call_target="tpu_custom_call", output_to_operand_aliasing={{0}: (1, {})} | custom-call | flops 1073741824 | bytes 17776640 | tf_op jit(solution)/shard_map/pallas_call | solution.py:30
  148.5 11.6 %all_to_all.98 = f32[16,8,512]{2,1,0:T(8,128)S(1)} all-to-all(f32[16,8,512]{2,1,0:T(8,128)S(1)} %bitcast.45), channel_id=1, replica_groups=mesh['x'=4,'core'=2,'z'=4,'y'=4] {'z','y'}, dimensions={0} | all-to-all | bytes 524288 | tf_op jit(solution)/shard_map/all_to_all | solution.py:258
  160.2 11.8 %all_to_all.99 = f32[16,8,512]{2,1,0:T(8,128)S(1)} all-to-all(f32[16,8,512]{2,1,0:T(8,128)S(1)} %broadcast_in_dim.27), channel_id=1, replica_groups=mesh['x'=4,'core'=2,'z'=4,'y'=4] {'z','y'}, dimensions={0} | all-to-all | bytes 524288 | tf_op jit(solution)/shard_map/all_to_all | solution.py:251
  171.9 4.2 %shard_map.135 = (f32[128,4096]{1,0:T(8,128)S(1)}, f32[128,512]{1,0:T(8,128)S(1)}) custom-call(f32[128,512]{1,0:T(8,128)S(1)} %bitcast.36, f32[128,4096]{1,0:T(8,128)S(1)} %get-tuple-element.50.x_ref, f32[128,32]{1,0:T(8,128)S(1)} %convert_multiply_fusion.gain_ref, ...), custom_call_target="tpu_custom_call", output_to_operand_aliasing={{0}: (1, {})} | custom-call | flops 1073741824 | bytes 17776640 | tf_op jit(solution)/shard_map/pallas_call | solution.py:30
  176.1 11.6 %all_to_all.100 = f32[16,8,512]{2,1,0:T(8,128)S(1)} all-to-all(f32[16,8,512]{2,1,0:T(8,128)S(1)} %bitcast.46), channel_id=1, replica_groups=mesh['x'=4,'core'=2,'z'=4,'y'=4] {'z','y'}, dimensions={0} | all-to-all | bytes 524288 | tf_op jit(solution)/shard_map/all_to_all | solution.py:258
  187.7 11.6 %all_to_all.101 = f32[16,8,512]{2,1,0:T(8,128)S(1)} all-to-all(f32[16,8,512]{2,1,0:T(8,128)S(1)} %broadcast_in_dim.28), channel_id=1, replica_groups=mesh['x'=4,'core'=2,'z'=4,'y'=4] {'z','y'}, dimensions={0} | all-to-all | bytes 524288 | tf_op jit(solution)/shard_map/all_to_all | solution.py:251
  199.3 0.0 copy-start.2
  199.3 4.2 %shard_map.136 = (f32[128,4096]{1,0:T(8,128)S(1)}, f32[128,512]{1,0:T(8,128)S(1)}) custom-call(f32[128,512]{1,0:T(8,128)S(1)} %bitcast.37, f32[128,4096]{1,0:T(8,128)S(1)} %get-tuple-element.52.x_ref, f32[128,32]{1,0:T(8,128)S(1)} %convert_multiply_fusion.gain_ref, ...), custom_call_target="tpu_custom_call", output_to_operand_aliasing={{0}: (1, {})} | custom-call | flops 1073741824 | bytes 17776640 | tf_op jit(solution)/shard_map/pallas_call | solution.py:30
  203.5 11.6 %all_to_all.102 = f32[16,8,512]{2,1,0:T(8,128)S(1)} all-to-all(f32[16,8,512]{2,1,0:T(8,128)S(1)} %bitcast.47), channel_id=1, replica_groups=mesh['x'=4,'core'=2,'z'=4,'y'=4] {'z','y'}, dimensions={0} | all-to-all | bytes 524288 | tf_op jit(solution)/shard_map/all_to_all | solution.py:258
  215.2 11.6 %all_to_all.103 = f32[16,8,512]{2,1,0:T(8,128)S(1)} all-to-all(f32[16,8,512]{2,1,0:T(8,128)S(1)} %broadcast_in_dim.29), channel_id=1, replica_groups=mesh['x'=4,'core'=2,'z'=4,'y'=4] {'z','y'}, dimensions={0} | all-to-all | bytes 524288 | tf_op jit(solution)/shard_map/all_to_all | solution.py:251
  226.8 0.0 copy-done.2
  226.8 4.9 %shard_map.137 = (f32[128,4096]{1,0:T(8,128)S(1)}, f32[128,4096]{1,0:T(8,128)}, f32[34,128]{1,0:T(8,128)S(1)}) custom-call(f32[128,512]{1,0:T(8,128)S(1)} %bitcast.31, f32[128,4096]{1,0:T(8,128)S(1)} %get-tuple-element.54.x_ref, f32[128,32]{1,0:T(8,128)S(1)} %convert_multiply_fusion.gain_ref, ...), custom_call_target="tpu_custom_call", output_to_operand_aliasing={{0}: (1, {})} | custom-call | flops 536870912 | bytes 19629568 | tf_op jit(solution)/shard_map/pallas_call | solution.py:30
  231.7 10.6 %all_to_all.104.all_ref = f32[8,34,128]{2,1,0:T(8,128)S(1)} all-to-all(f32[8,34,128]{2,1,0:T(8,128)S(1)} %broadcast_in_dim.32), channel_id=1, replica_groups=mesh['x'=4,'core'=2,'z'=4,'y'=4] {'x','core'}, dimensions={0} | all-to-all | bytes 278528 | tf_op jit(solution)/shard_map/all_to_all | solution.py:251
  242.3 0.8 shard_map.138
  243.1 3.5 %all-to-all-start.17 = ((f32[16,8,128]{2,1,0:T(8,128)}), f32[16,8,128]{2,1,0:T(8,128)S(1)}, u32[]{:S(2)}, u32[]{:S(2)}) async-start(f32[16,8,128]{2,1,0:T(8,128)} %get-tuple-element.59), calls=%async_computation.17 | async-start | bytes 131072 | tf_op jit(solution)/shard_map/all_to_all | solution.py:344
  246.6 0.7 copy.27
  247.2 6.9 %all-to-all-done.17.parts_ref = f32[16,8,128]{2,1,0:T(8,128)S(1)} async-done(((f32[16,8,128]{2,1,0:T(8,128)}), f32[16,8,128]{2,1,0:T(8,128)S(1)}, u32[]{:S(2)}, u32[]{:S(2)}) %all-to-all-start.17) | async-done | bytes 65568 | tf_op jit(solution)/shard_map/all_to_all | solution.py:344
  254.2 3.1 %shard_map.139 = (f32[128,4096]{1,0:T(8,128)}, f32[1,1]{1,0:T(1,128)}, f32[1,1]{1,0:T(1,128)}) custom-call(s32[1]{0:T(128)} %bitcast.18.node_ref, f32[128,4096]{1,0:T(8,128)S(1)} %get-tuple-element.56.x_ref, f32[4,32,128]{2,1,0:T(8,128)S(1)} %get-tuple-element.58.means_ref, f32[16,8,128]{2,1,0:T(8,128)S(1)} %all-to-all-done.17.parts_ref, f32[128,4096]{1,0:T(8,128)} %mult_far.3), custom_call_target="tpu_custom_call" | custom-call | flops 1572864 | bytes 6422540 | tf_op jit(solution)/shard_map/pallas_call | solution.py:30
  (28 shorter events, 0.4 us)
Async XLA Ops:
  0.6 12.3 %copy-start = (f32[128,512]{1,0:T(8,128)S(1)}, f32[128,512]{1,0:T(8,128)}, u32[]{:S(2)}) copy-start(f32[128,512]{1,0:T(8,128)} %param.13) | copy-start | bytes 786436
  0.6 12.3 %copy-start.3 = (f32[4,4096]{1,0:T(4,128)S(1)}, f32[4,4096]{1,0:T(4,128)}, u32[]{:S(2)}) copy-start(f32[4,4096]{1,0:T(4,128)} %param.16) | copy-start | bytes 196612
  0.7 25.2 %copy-start.4 = (s32[128,32]{0,1:T(8,128)S(1)}, s32[128,32]{0,1:T(8,128)}, u32[]{:S(2)}) copy-start(s32[128,32]{0,1:T(8,128)} %param.17) | copy-start | bytes 49156
  4.7 16.8 %all-to-all-start = ((f32[16,8,512]{2,1,0:T(8,128)}), f32[16,8,512]{2,1,0:T(8,128)S(1)}, u32[]{:S(2)}, u32[]{:S(2)}) async-start(f32[16,8,512]{2,1,0:T(8,128)} %bitcast), calls=%async_computation | async-start | bytes 524288 | tf_op jit(solution)/shard_map/all_to_all | solution.py:258
  22.3 12.2 %all-to-all-start.1 = ((f32[16,8,512]{2,1,0:T(8,128)}), f32[16,8,512]{2,1,0:T(8,128)S(1)}, u32[]{:S(2)}, u32[]{:S(2)}) async-start(f32[16,8,512]{2,1,0:T(8,128)} %broadcast_in_dim.22), calls=%async_computation.1 | async-start | bytes 524288 | tf_op jit(solution)/shard_map/all_to_all | solution.py:251
  26.0 1.2 copy-start.1
  199.3 27.4 %copy-start.2 = (f32[128]{0:T(128)S(1)}, f32[128]{0:T(128)}, u32[]{:S(2)}) copy-start(f32[128]{0:T(128)} %param.15) | copy-start | bytes 1540
  243.1 11.1 %all-to-all-start.17 = ((f32[16,8,128]{2,1,0:T(8,128)}), f32[16,8,128]{2,1,0:T(8,128)S(1)}, u32[]{:S(2)}, u32[]{:S(2)}) async-start(f32[16,8,128]{2,1,0:T(8,128)} %get-tuple-element.59), calls=%async_computation.17 | async-start | bytes 131072 | tf_op jit(solution)/shard_map/all_to_all | solution.py:344
